TPU v7x, 128 devices: a whole 4x4x4 slice. The times are simulated.
128 devices in a mesh: row: 8 (over y_lo, x), col: 8 (over z, core), seq: 2 (over y_hi).
Axes of the slice: x: 4, y: 4 (y_hi: 2, y_lo: 2; y = y_hi * 2 + y_lo), z: 4, core: 2. Of those that a mesh axis runs over, the one named last changes fastest.
Arguments:
- alignment_tensor: bfloat16 [256, 512, 256], P('seq', ('row', 'col')), may hold values from -6 to 6
- occupancy_matrix: int32 [256, 512], P(None, ('row', 'col')), may hold values from 0 to 1, as said below
- first_factor_matrix: bfloat16 [256, 32], replicated, may hold values from -0.375 to 0.375
- second_factor_matrix: bfloat16 [256, 32], replicated, may hold values from -0.375 to 0.375
- couple_factor_matrix: bfloat16 [1024, 128], replicated, may hold values from -3 to 3
- couple_increment_adjoint: bfloat16 [512, 512, 128], P(('row', 'seq'), 'col'), may hold values from -6 to 6
Outputs:
- couple_increment: bfloat16 [512, 512, 128], P(('row', 'seq'), 'col')
- alignment_adjoint: bfloat16 [256, 512, 256], P('seq', ('row', 'col'))
- first_factor_adjoint: float32 [256, 32], replicated
- second_factor_adjoint: float32 [256, 32], replicated
- couple_factor_adjoint: float32 [1024, 128], replicated
Inputs may be any that keep to these rules, and one draw needn't show every extreme that they name: Row 0 of occupancy_matrix (the query) is all ones; every other sequence covers residues of one contiguous range with some gaps.
All inputs are finite; a program needn't handle non-finite values.
Results may differ from a plain program's by a relative error of at most 0.0076.
Values may be sent and summed in bfloat16 or wider, within the bound.
A program may use at most 192 MiB of HBM per device.

v0:
```python
import jax
import jax.numpy as jnp
from jax import lax
from jax.sharding import PartitionSpec as P

ALIGN_DIM = 256
PROJ_DIM = 32
CZ = 128
OUTER = 1024


def broadcast(value, axis, root):
    mine = lax.axis_index(axis) == root
    return lax.psum(jnp.where(mine, value, jnp.zeros_like(value)), axis)


def local(
    alignment_tensor,
    occupancy_matrix,
    first_factor_matrix,
    second_factor_matrix,
    couple_factor_matrix,
    couple_increment_adjoint,
):
    homolog_shards = alignment_tensor.shape[0]
    embed_dimension = alignment_tensor.shape[1]
    seq_index = lax.axis_index("seq")
    col_index = lax.axis_index("col")
    argument_tensor = alignment_tensor.astype(jnp.float32)
    centered_input = argument_tensor - jnp.mean(argument_tensor, axis=-1, keepdims=True)
    reciprocal_spread = lax.rsqrt(
        jnp.mean(centered_input * centered_input, axis=-1, keepdims=True) + 1e-05
    )
    zscored_tensor = centered_input * reciprocal_spread
    rescaled_tensor = zscored_tensor.astype(jnp.bfloat16)
    raveled_matrix = rescaled_tensor.reshape(-1, ALIGN_DIM)
    maskf = occupancy_matrix.astype(jnp.float32)
    own_mask = lax.dynamic_slice_in_dim(maskf, seq_index * homolog_shards, homolog_shards, 0)
    left = (
        own_mask[:, :, None]
        * jnp.dot(raveled_matrix, first_factor_matrix, preferred_element_type=jnp.float32).reshape(
            homolog_shards, embed_dimension, PROJ_DIM
        )
    ).astype(jnp.bfloat16)
    right = (
        own_mask[:, :, None]
        * jnp.dot(raveled_matrix, second_factor_matrix, preferred_element_type=jnp.float32).reshape(
            homolog_shards, embed_dimension, PROJ_DIM
        )
    ).astype(jnp.bfloat16)
    stacked = jnp.concatenate([left, right], axis=2)
    both_rows, mask_rows = (
        lax.all_gather(stacked, "col", axis=1, tiled=True),
        lax.all_gather(occupancy_matrix.astype(jnp.bfloat16), "col", axis=1, tiled=True),
    )
    left_rows = both_rows[:, :, :PROJ_DIM]
    right_cols, mask_cols = (
        broadcast(both_rows[:, :, PROJ_DIM:], "row", lax.axis_index("col")),
        broadcast(mask_rows, "row", lax.axis_index("col")),
    )
    block = both_rows.shape[1]
    half = couple_increment_adjoint.shape[0]
    count = jnp.dot(mask_rows.T, mask_cols, preferred_element_type=jnp.float32)
    den = lax.dynamic_slice_in_dim(count, seq_index * half, half, 0) + 0.001
    wo32 = couple_factor_matrix.astype(jnp.float32)
    scaled = (couple_increment_adjoint.astype(jnp.float32) / den[:, :, None]).astype(jnp.bfloat16)
    lblock = left_rows
    outer = jnp.einsum("sic,sje->ijce", lblock, right_cols, preferred_element_type=jnp.float32)
    summed = lax.psum_scatter(
        outer.reshape(half * lax.axis_size("seq"), block, OUTER),
        "seq",
        scatter_dimension=0,
        tiled=True,
    )
    flat_outer = summed.reshape(-1, OUTER)
    projected = jnp.dot(flat_outer, wo32, precision=lax.Precision.HIGHEST).reshape(
        summed.shape[0], block, CZ
    )
    own_wo = jnp.dot(
        summed.reshape(-1, OUTER).T,
        scaled.astype(jnp.float32).reshape(-1, CZ),
        precision=lax.Precision.HIGHEST,
    )
    couple_increment = (projected / den[:, :, None]).astype(jnp.bfloat16)
    weight_t = couple_factor_matrix.T
    piece = lax.all_gather(scaled, "seq", axis=0, tiled=True)
    d_wo = own_wo
    number = piece.shape[0]
    d_outer = jnp.dot(piece.reshape(-1, CZ), weight_t, preferred_element_type=jnp.float32).astype(
        jnp.bfloat16
    )
    d_outer = d_outer.reshape(number, block, PROJ_DIM, PROJ_DIM)
    lblock = left_rows
    g_piece = jnp.einsum("ijce,sje->sic", d_outer, right_cols, preferred_element_type=jnp.float32)
    g_left = g_piece
    g_right = jnp.einsum("ijce,sic->sje", d_outer, lblock, preferred_element_type=jnp.float32)
    g_left_rows, g_right_cols, d_wo = (g_left, g_right, d_wo)
    left_total = lax.psum(g_left_rows, "col")
    g_left = lax.dynamic_slice_in_dim(left_total, col_index * embed_dimension, embed_dimension, 1)
    right_total = lax.psum(g_right_cols, "row")
    right_block = broadcast(right_total, "col", lax.axis_index("row"))
    g_right = lax.dynamic_slice_in_dim(right_block, col_index * embed_dimension, embed_dimension, 1)
    g_left = own_mask[:, :, None] * g_left
    g_right = own_mask[:, :, None] * g_right
    gl_flat = g_left.reshape(-1, PROJ_DIM)
    gr_flat = g_right.reshape(-1, PROJ_DIM)
    normed32 = raveled_matrix.astype(jnp.float32)
    first_factor_adjoint = jnp.dot(normed32.T, gl_flat, precision=lax.Precision.HIGHEST)
    second_factor_adjoint = jnp.dot(normed32.T, gr_flat, precision=lax.Precision.HIGHEST)
    rescaled_adjoint = jnp.dot(
        gl_flat, first_factor_matrix.astype(jnp.float32).T, precision=lax.Precision.HIGHEST
    )
    rescaled_adjoint = rescaled_adjoint + jnp.dot(
        gr_flat, second_factor_matrix.astype(jnp.float32).T, precision=lax.Precision.HIGHEST
    )
    rescaled_adjoint = rescaled_adjoint.reshape(homolog_shards, embed_dimension, ALIGN_DIM)
    addend_term = jnp.mean(rescaled_adjoint * zscored_tensor, axis=-1, keepdims=True)
    alignment_adjoint = (
        reciprocal_spread
        * (
            rescaled_adjoint
            - jnp.mean(rescaled_adjoint, axis=-1, keepdims=True)
            - zscored_tensor * addend_term
        )
    ).astype(jnp.bfloat16)
    subset_accumulations = lax.psum(
        (first_factor_adjoint, second_factor_adjoint, d_wo), ("row", "col", "seq")
    )
    return (
        couple_increment,
        alignment_adjoint,
        subset_accumulations[0],
        subset_accumulations[1],
        subset_accumulations[2],
    )


def solution(mesh):
    placed = (
        P("seq", ("row", "col"), None),
        P(None, ("row", "col")),
        P(),
        P(),
        P(),
        P(("row", "seq"), "col", None),
    )
    return jax.shard_map(
        local,
        mesh=mesh,
        in_specs=placed,
        out_specs=(P(("row", "seq"), "col", None), P("seq", ("row", "col"), None), P(), P(), P()),
        check_vma=False,
    )
```

profile of v0, /device:TPU:1, one launch (start us, length us, event | category | flops | bytes accessed | tf_op | source)
XLA Modules:
  0.0 915.1 jit_solution(6481463513758615300)
XLA Ops:
  7.2 0.7 convert_element_type.43
  8.0 15.3 %all_gather.10 = bf16[256,64]{0,1:T(8,128)(2,1)S(1)} all-gather(bf16[256,8]{0,1:T(8,128)(2,1)S(1)} %convert_element_type.43), channel_id=1, replica_groups=mesh['row'=8,'col'=8,'seq'=2] {'col'}, dimensions={1}, use_global_device_ids=true | all-gather | bytes 36864 | tf_op jit(solution)/shard_map/all_gather | solution.py:54
  23.3 27.3 %psum.57 = bf16[256,64]{0,1:T(8,128)(2,1)S(1)} all-reduce(bf16[256,64]{0,1:T(8,128)(2,1)S(1)} %broadcast_select_fusion.1), channel_id=1, replica_groups=mesh['row'=8,'col'=8,'seq'=2] {'row'}, use_global_device_ids=true, to_apply=%region_4.5 | all-reduce | flops 16384 | bytes 65536 | tf_op jit(solution)/shard_map/psum | solution.py:14
  50.6 0.1 fusion.39
  50.7 2.2 divide_convert_fusion
  53.0 1.3 convert_reduce_fusion
  54.2 0.7 dynamic-slice_convert_fusion
  54.9 0.1 copy.37
  55.0 1.4 fusion.12
  56.5 1.5 fusion.7
  58.0 1.5 fusion.6
  59.5 0.1 pad_maximum_fusion
  59.7 0.8 copy.38
  60.6 22.8 %all-gather.5.cloned.1.call-done = bf16[64,64,128]{2,1,0:T(8,128)(2,1)} async-done(((bf16[32,64,128]{2,1,0:T(8,128)(2,1)}), bf16[64,64,128]{2,1,0:T(8,128)(2,1)}) %all-gather.5.cloned.1.call-update) | async-done | bytes 1048592 | tf_op jit(solution)/shard_map/all_gather | solution.py:86
  83.4 6.8 convolution_convert_fusion
  90.2 11.3 %copy.41 = bf16[4096,1024]{0,1:T(8,128)(2,1)} copy(bf16[4096,1024]{1,0:T(8,128)(2,1)} %convolution_convert_fusion) | data formatting | bytes 16777216 | tf_op jit(solution)/shard_map/convert_element_type | solution.py:89
  101.4 23.6 %reshape.71 = bf16[64,64,32,32]{1,0,3,2:T(8,128)(2,1)} reshape(bf16[4096,1024]{0,1:T(8,128)(2,1)} %copy.41) | data formatting | bytes 16777216 | tf_op jit(solution)/shard_map/reshape | solution.py:92
  125.0 2.1 fusion.38
  127.1 0.2 all-reduce.10.cloned.1.call-start
  127.4 10.6 %convolution_bitcast_fusion = f32[128,64,32]{0,1,2:T(8,128)S(1)} fusion(bf16[64,64,32,32]{1,0,3,2:T(8,128)(2,1)} %reshape.71, bf16[128,64,32]{0,2,1:T(8,128)(2,1)S(1)} %get-tuple-element.9), kind=kOutput, calls=%fused_computation.2 | convolution fusion | flops 1073741824 | bytes 9961472 | tf_op jit(solution)/shard_map/ijce,sic->sje/dot_general | solution.py:96
  137.9 4.5 copy.46
  142.4 0.3 all-reduce.16.cloned.1.call-start
  142.7 23.5 %copy.42 = bf16[64,64,32,32]{0,3,1,2:T(8,128)(2,1)} copy(bf16[64,64,32,32]{1,0,3,2:T(8,128)(2,1)} %reshape.71) | data formatting | bytes 16777216 | tf_op jit(solution)/shard_map/reshape | solution.py:92
  166.2 30.1 %all-reduce.8.cloned.1.call-done = bf16[128,64,32]{0,2,1:T(8,128)(2,1)} async-done(((bf16[128,64,32]{0,2,1:T(8,128)(2,1)}), bf16[128,64,32]{0,2,1:T(8,128)(2,1)}) %all-reduce.8.cloned.1.call-update) | async-done | bytes 524304 | tf_op jit(solution)/shard_map/psum | solution.py:14
  196.3 10.7 %convolution_bitcast_fusion.1 = f32[128,64,32]{0,1,2:T(8,128)S(1)} fusion(bf16[64,64,32,32]{0,3,1,2:T(8,128)(2,1)} %copy.42, bf16[128,64,32]{0,2,1:T(8,128)(2,1)} %all-reduce.8.cloned.1.call-done), kind=kOutput, calls=%fused_computation.3 | convolution fusion | flops 1073741824 | bytes 9961472 | tf_op jit(solution)/shard_map/ijce,sje->sic/dot_general | solution.py:94
  207.1 4.5 copy.43
  211.6 97.1 %all-reduce.10.cloned.1.call-done = f32[128,64,32]{2,1,0:T(8,128)} async-done(((f32[128,64,32]{2,1,0:T(8,128)}), f32[128,64,32]{2,1,0:T(8,128)}) %all-reduce.10.cloned.1.call-update) | async-done | bytes 1048592 | tf_op jit(solution)/shard_map/psum | solution.py:100
  308.7 2.8 broadcast_select_fusion
  311.6 13.9 %fusion.14 = f32[64,32,64,32]{2,1,3,0:T(8,128)} fusion(bf16[128,64,32]{0,2,1:T(8,128)(2,1)S(1)} %copy-done.3, bf16[128,64,32]{0,2,1:T(8,128)(2,1)S(1)} %get-tuple-element.9), kind=kOutput, calls=%fused_computation.30 | convolution fusion | flops 1073741824 | bytes 17825792 | tf_op jit(solution)/shard_map/sic,sje->ijce/dot_general | solution.py:68
  325.4 26.5 %copy.40 = f32[64,64,1024]{2,1,0:T(8,128)} copy(f32[64,64,1024]{0,2,1:T(8,128)} %bitcast.70) | data formatting | bytes 33554432 | tf_op jit(solution)/shard_map/reshape | solution.py:70
  352.0 0.3 all-reduce.14.cloned.1.call-start
  352.3 63.9 %all-reduce.16.cloned.1.call-done = (f32[128,64,32]{2,1,0:T(8,128)}, f32[128,64,32]{2,1,0:T(8,128)}) async-done(((f32[128,64,32]{2,1,0:T(8,128)}, f32[128,64,32]{2,1,0:T(8,128)}), (f32[128,64,32]{2,1,0:T(8,128)}, f32[128,64,32]{2,1,0:T(8,128)})) %all-reduce.16.cloned.1.call-update) | async-done | bytes 2097168 | tf_op jit(solution)/shard_map/psum | solution.py:98
  416.2 1.7 fusion.17
  417.9 1.8 fusion.8
  419.7 0.2 reduce_sum.38
  420.0 0.1 div.34
  420.1 2.7 convolution_bitcast_fusion.4
  422.8 2.7 convolution_bitcast_fusion.3
  425.5 1.4 fusion.11
  426.9 0.0 all-reduce.12.cloned.1.call-start
  427.0 185.0 %reduce-scatter.2.cloned.1.call-done = f32[32,64,1024]{2,1,0:T(8,128)} async-done(((f32[64,64,1024]{2,1,0:T(8,128)}), f32[32,64,1024]{2,1,0:T(8,128)}) %reduce-scatter.2.cloned.1.call-update) | async-done | bytes 8388624 | tf_op jit(solution)/shard_map/reduce_scatter | solution.py:69
  612.0 9.9 %convolution_bitcast_fusion.2 = f32[1024,128]{1,0:T(8,128)} fusion(f32[32,64,1024]{2,1,0:T(8,128)} %reduce-scatter.2.cloned.1.call-done, bf16[32,64,128]{2,1,0:T(8,128)(2,1)S(1)} %copy-done.2), kind=kOutput, calls=%fused_computation.14 | convolution fusion | flops 3221225472 | bytes 9437184 | tf_op jit(solution)/shard_map/dot_general | solution.py:79
  621.9 8.1 fusion
  629.9 125.3 %all-reduce.14.cloned.1.call-done = (f32[256,32]{0,1:T(8,128)}, f32[256,32]{0,1:T(8,128)}) async-done(((f32[256,32]{0,1:T(8,128)}, f32[256,32]{0,1:T(8,128)}), (f32[256,32]{0,1:T(8,128)}, f32[256,32]{0,1:T(8,128)})) %all-reduce.14.cloned.1.call-update) | async-done | bytes 65552 | tf_op jit(solution)/shard_map/psum | solution.py:126
  755.3 148.4 %all-reduce.12.cloned.1.call-done = f32[1024,128]{1,0:T(8,128)} async-done(((f32[1024,128]{1,0:T(8,128)}), f32[1024,128]{1,0:T(8,128)}) %all-reduce.12.cloned.1.call-update) | async-done | bytes 524304 | tf_op jit(solution)/shard_map/psum | solution.py:126
  903.7 1.4 copy.70
  905.0 1.4 copy.71
  906.4 1.9 copy.72
  (31 shorter events, 0.4 us)
Async XLA Ops:
  7.2 76.2 %copy-start = (bf16[1024,128]{1,0:T(8,128)(2,1)S(1)}, bf16[1024,128]{1,0:T(8,128)(2,1)}, u32[]{:S(2)}) copy-start(bf16[1024,128]{1,0:T(8,128)(2,1)} %param.10) | copy-start | bytes 786436
  7.2 76.2 %all-gather.5.cloned.1.call-start = ((), (), s32[]{:S(2)}) async-start(), calls=%async_computation.4 | async-start | bytes 1572864 | tf_op jit(solution)/shard_map/all_gather | solution.py:86
  52.9 72.1 %all-gather.3.cloned.1.call-start = ((), (), s32[]{:S(2)}) async-start(), calls=%async_computation.1 | async-start | bytes 1179648 | tf_op jit(solution)/shard_map/all_gather | solution.py:53
  60.5 135.8 %all-reduce.8.cloned.1.call-start = ((), (), s32[]{:S(2)}) async-start(), calls=%async_computation.2 | async-start | bytes 1048576 | tf_op jit(solution)/shard_map/psum | solution.py:14
  127.1 181.6 %all-reduce.10.cloned.1.call-start = ((), (), s32[]{:S(2)}) async-start(), calls=%async_computation.5 | async-start | bytes 8388608 | tf_op jit(solution)/shard_map/psum | solution.py:100
  142.4 273.8 %all-reduce.16.cloned.1.call-start = ((), (), s32[]{:S(2)}) async-start(), calls=%async_computation.8 | async-start | bytes 16777216 | tf_op jit(solution)/shard_map/psum | solution.py:98
  211.6 100.0 %copy-start.3 = (bf16[128,64,32]{0,2,1:T(8,128)(2,1)S(1)}, bf16[128,64,32]{0,2,1:T(8,128)(2,1)}, u32[]{:S(2)}) copy-start(bf16[128,64,32]{0,2,1:T(8,128)(2,1)} %all-reduce.8.cloned.1.call-done) | copy-start | bytes 1572868
  311.5 300.5 %reduce-scatter.2.cloned.1.call-start = ((), (), s32[]{:S(2)}) async-start(), calls=%async_computation.3 | async-start | bytes 25165824 | tf_op jit(solution)/shard_map/reduce_scatter | solution.py:69
  352.0 64.3 %copy-start.4 = (bf16[256,32]{0,1:T(8,128)(2,1)S(1)}, bf16[256,32]{0,1:T(8,128)(2,1)}, u32[]{:S(2)}) copy-start(bf16[256,32]{0,1:T(8,128)(2,1)} %param.8) | copy-start | bytes 49156
  352.0 65.9 %copy-start.1 = (bf16[128,8,256]{2,1,0:T(8,128)(2,1)S(1)}, bf16[128,8,256]{2,1,0:T(8,128)(2,1)}, u32[]{:S(2)}) copy-start(bf16[128,8,256]{2,1,0:T(8,128)(2,1)} %param.6) | copy-start | bytes 1572868
  352.0 65.9 %copy-start.5 = (bf16[256,32]{0,1:T(8,128)(2,1)S(1)}, bf16[256,32]{0,1:T(8,128)(2,1)}, u32[]{:S(2)}) copy-start(bf16[256,32]{0,1:T(8,128)(2,1)} %param.9) | copy-start | bytes 49156
  352.0 260.0 %copy-start.2 = (bf16[32,64,128]{2,1,0:T(8,128)(2,1)S(1)}, bf16[32,64,128]{2,1,0:T(8,128)(2,1)}, u32[]{:S(2)}) copy-start(bf16[32,64,128]{2,1,0:T(8,128)(2,1)} %divide_convert_fusion) | copy-start | bytes 1572868
  352.0 403.3 %all-reduce.14.cloned.1.call-start = ((), (), s32[]{:S(2)}) async-start(), calls=%async_computation.7 | async-start | bytes 131072 | tf_op jit(solution)/shard_map/psum | solution.py:126
  426.9 476.8 %all-reduce.12.cloned.1.call-start = ((), (), s32[]{:S(2)}) async-start(), calls=%async_computation.6 | async-start | bytes 1048576 | tf_op jit(solution)/shard_map/psum | solution.py:126
Sparse Core Ops, SparseCore 0:
  53.0 30.2 all-gather.4
  85.7 23.3 all-gather.2
  127.3 69.0 all-reduce.7
  198.9 109.7 all-reduce.9
  311.6 104.5 all-reduce.15
  418.6 193.3 reduce-scatter.1
  617.6 137.6 all-reduce.13
  761.3 142.3 all-reduce.11
where the time goes:
time: 918 us; the launch traced here: 915 us
  waiting for transfers between devices  673 us (73%)
  local copies, waits for them, and re-layouts  99.6 us (11%)
  matrix products  71.9 us (8%)
  blocking collectives  42.6 us (5%)
  between operations  14.3 us (2%)
  other arithmetic  13 us (1%)
    psum x2, waiting for transfers between devices, local(): lax.psum((first_factor_adjoint, second_factor_adjoint, d_wo), ('row', 'co...  274 us
    reduce_scatter x1, waiting for transfers between devices, local(): lax.psum_scatter(outer.reshape(half * lax.axis_size('seq'), block, OUTER)...  185 us
    psum x1, waiting for transfers between devices, local(): right_total = lax.psum(g_right_cols, 'row')  97.1 us
    psum x1, waiting for transfers between devices, local(): left_total = lax.psum(g_left_rows, 'col')  63.9 us
    reshape x2, local copies, waits for them, and re-layouts, local(): d_outer = d_outer.reshape(number, block, PROJ_DIM, PROJ_DIM)  47.1 us
    psum x1, waiting for transfers between devices, broadcast(): return lax.psum(jnp.where(mine, value, jnp.zeros_like(value)), axis)  30.1 us
    psum x1, blocking collectives, broadcast(): return lax.psum(jnp.where(mine, value, jnp.zeros_like(value)), axis)  27.3 us
    reshape x1, local copies, waits for them, and re-layouts, local(): outer.reshape(half * lax.axis_size('seq'), block, OUTER)  26.5 us
  transfers between devices with their start and end apart: 8, of which 7 were waited for; matrix products, arithmetic and copies ran while one was open for 19% of the time, Pallas kernels for 0%

commit v1 on v0

v1 whole, which is shorter than its diff:
```python
import jax
import jax.numpy as jnp
from jax import lax
from jax.experimental import pallas as pl
from jax.experimental.pallas import tpu as pltpu
from jax.sharding import PartitionSpec as P

F32 = jnp.float32
BF16 = jnp.bfloat16
MESH = pl.DeviceIdType.MESH

NS = 128
NQ = 8
NCH = 256
NP = 32
NZ = 128
HALF = 512
PAIRS = 2048


def dot(a, b, ca, cb):
    return lax.dot_general(a, b, (((ca,), (cb,)), ((), ())), preferred_element_type=F32)


def both_halves(ref, rows):
    return jnp.concatenate([ref[0, rows, :], ref[1, rows, :]], axis=1)


def kernel(
    x_ref,
    occ_ref,
    w1_ref,
    w2_ref,
    wo_ref,
    cot_ref,
    inc_ref,
    aadj_ref,
    fa_ref,
    sa_ref,
    dwo_ref,
    msend,
    mrow,
    mcol,
    xh,
    rs,
    nres,
    tmp,
    lsend,
    rsend,
    lrecv,
    rrecv,
    wt,
    wsplit,
    wide,
    inv,
    s12,
    d2,
    lscr,
    rscr,
    beo,
    grsend,
    glsend,
    glrecv,
    grrecv,
    dwf,
    dwsend,
    dwrecv,
    fsend,
    frecv,
    f1,
    f1recv,
    f2,
    f2recv,
    e1,
    e1recv,
    e2,
    e2recv,
    e3,
    gown,
    oscr,
    ss_mr,
    rs_mr,
    ss_mc,
    rs_mc,
    ss_l,
    rs_l,
    ss_r,
    rs_r,
    ss_gl,
    rs_gl,
    ss_gr,
    rs_gr,
    ss_dw,
    rs_dw,
    ss_f,
    rs_f,
    ss_f1,
    rs_f1,
    ss_f2,
    rs_f2,
    ss_e1,
    rs_e1,
    ss_e2,
    rs_e2,
    ss_e3,
    rs_e3,
):
    r, c, q = lax.axis_index("row"), lax.axis_index("col"), lax.axis_index("seq")
    qd = c // 4
    other = (r, lax.rem(c + 1, 8), q)

    def far(src, dst, ssem, rsem, dev):
        return pltpu.make_async_remote_copy(
            src_ref=src, dst_ref=dst, send_sem=ssem, recv_sem=rsem, device_id=dev, device_id_type=MESH
        )

    def put(own, src, dst, ssem, rsem, dev):
        @pl.when(own)
        def _():
            pltpu.make_async_copy(src, dst, rsem).start()

        @pl.when(jnp.logical_not(own))
        def _():
            far(src, dst, ssem, rsem, dev).start()

    def arrived(slot, ssem, rsem):
        far(slot, slot, ssem, rsem, other).wait_recv()

    def sent(slot, ssem, rsem):
        far(slot, slot, ssem, rsem, other).wait_send()

    occ = occ_ref[...].astype(F32).astype(BF16)
    eye = (
        lax.broadcasted_iota(jnp.int32, (16, NQ), 0) == lax.broadcasted_iota(jnp.int32, (16, NQ), 1)
    ).astype(F32).astype(BF16)
    for h in range(2):
        msend[h] = dot(eye, occ[h * NS : (h + 1) * NS], 1, 1).astype(BF16)

    @pl.when(q == qd)
    def _():
        pltpu.make_async_copy(msend, mrow.at[lax.rem(c, 4)], rs_mr.at[lax.rem(c, 4)]).start()

        @pl.loop(1, 8)
        def _(t):
            far(
                msend, mrow.at[lax.rem(c, 4)], ss_mr.at[t], rs_mr.at[lax.rem(c, 4)], (r, lax.rem(c + t, 8), q)
            ).start()

    put(c == r, msend, mcol.at[c], ss_mc.at[0], rs_mc.at[c], (r, r, q))

    @pl.loop(1, 8)
    def _(t):
        far(msend, mcol.at[c], ss_mc.at[t], rs_mc.at[c], (lax.rem(r + t, 8), r, q)).start()

    @pl.loop(0, 8)
    def _(t):
        xb = x_ref[pl.ds(t * 16, 16)].astype(F32).reshape(128, NCH)
        xc = xb - jnp.mean(xb, axis=-1, keepdims=True)
        rstd = lax.rsqrt(jnp.mean(xc * xc, axis=-1, keepdims=True) + 1e-05)
        z = xc * rstd
        xh[0, pl.ds(t * 128, 128), :] = z[:, :128]
        xh[1, pl.ds(t * 128, 128), :] = z[:, 128:]
        rs[pl.ds(t * 128, 128), :] = jnp.broadcast_to(rstd, (128, 128))

    wt[0:NP, :] = w1_ref[...].astype(F32).T.astype(BF16)
    wt[NP:, :] = w2_ref[...].astype(F32).T.astype(BF16)
    mine = msend[q].astype(F32)
    for k in range(NQ):
        n = both_halves(xh, pl.ds(k, NS, stride=NQ)).astype(BF16)
        nres[k] = n
        p = dot(wt[...], n, 1, 1) * mine[k : k + 1, :]
        lsend[k * NP : (k + 1) * NP, :] = p[:NP].astype(BF16)
        tmp[pl.ds(k, NP, stride=NQ), :] = p[NP:]
    rsend[...] = tmp[...].astype(BF16)

    put(jnp.logical_and(c == r, True), rsend, rrecv.at[q, c], ss_r.at[0], rs_r.at[q, c], (r, r, q))

    @pl.loop(1, 16)
    def _(t):
        dev = (lax.rem(r + t // 2, 8), r, lax.rem(q + t, 2))
        far(rsend, rrecv.at[q, c], ss_r.at[t], rs_r.at[q, c], dev).start()

    put(q == qd, lsend, lrecv.at[q, lax.rem(c, 4)], ss_l.at[0], rs_l.at[q, lax.rem(c, 4)], (r, c, qd))

    @pl.loop(1, 8)
    def _(t):
        dev = (r, lax.rem(c + t, 8), qd)
        far(lsend, lrecv.at[q, lax.rem(c, 4)], ss_l.at[t], rs_l.at[q, lax.rem(c, 4)], dev).start()

    wide[...] = wo_ref[...].astype(F32)
    for e in range(NP):
        wsplit[e % 2, (e // 2) * NP : (e // 2 + 1) * NP, :] = wide[pl.ds(e, NP, stride=NP), :].astype(BF16)

    for m in range(4):
        arrived(mrow.at[m], ss_mr.at[m], rs_mr.at[m])
    for m in range(8):
        arrived(mcol.at[m], ss_mc.at[m], rs_mc.at[m])
    count = jnp.zeros((64, 32), F32)
    for h in range(2):
        rows = jnp.concatenate([mrow[m, h].astype(F32)[:NQ] for m in range(4)], axis=0).astype(BF16)
        cols = jnp.concatenate([mcol[m, h].astype(F32)[:NQ] for m in range(8)], axis=0).astype(BF16)
        count = count + dot(cols, rows, 1, 1)
    over = 1.0 / (count + 0.001)
    for k in range(16):
        parts = []
        for i in (k, k + 16):
            column = jnp.broadcast_to(over[:, i : i + 1], (64, NZ))
            inv[i] = column
            parts.append((cot_ref[i].astype(F32) * column).astype(BF16))
        s12[0, k * 128 : k * 128 + 64, :] = parts[0]
        s12[0, k * 128 + 64 : (k + 1) * 128, :] = parts[1]
        s12[1, k * 128 : k * 128 + 64, :] = parts[1]
        s12[1, k * 128 + 64 : (k + 1) * 128, :] = parts[0]

    low = lax.broadcasted_iota(jnp.int32, (NP, 128), 1) < 64

    @pl.loop(0, 8)
    def _(t):
        here = pl.ds(pl.multiple_of(t * 256, 256), 256)
        de = dot(wsplit[0], s12[0, here, :], 1, 1)
        do = dot(wsplit[1], s12[1, here, :], 1, 1)
        for u in range(2):
            at = pl.multiple_of((t * 2 + u) * NP, NP)
            for p in range(16):
                a = de[p * NP : (p + 1) * NP, u * 128 : (u + 1) * 128]
                b = do[p * NP : (p + 1) * NP, u * 128 : (u + 1) * 128]
                d2[0, pl.ds(at, NP), p * 128 : (p + 1) * 128] = jnp.where(low, a, b).astype(BF16)
                d2[1, pl.ds(at, NP), p * 128 : (p + 1) * 128] = jnp.where(low, b, a).astype(BF16)

    for h in range(2):
        for m in range(4):
            arrived(lrecv.at[h, m], ss_l.at[m], rs_l.at[h, m])
            lscr[m // 2, (m % 2) * 256 : (m % 2 + 1) * 256, h * NS : (h + 1) * NS] = lrecv[h, m]

    @pl.loop(0, 8)
    def _(t):
        here = pl.ds(pl.multiple_of(t * 256, 256), 256)
        a = dot(lscr[0], d2[0, :, here], 0, 0)
        b = dot(lscr[1], d2[1, :, here], 0, 0)
        for u in range(2):
            lanes = slice(u * 128, (u + 1) * 128)
            g = a[:, lanes] + pltpu.roll(b[:, lanes], 64, 1)
            for h in range(2):
                gt = g[h * NS : (h + 1) * NS].T
                at = pl.multiple_of((t * 2 + u) * 16, 16)
                for m in range(8):
                    both = jnp.concatenate([gt[m * 8 : m * 8 + 8], gt[64 + m * 8 : 72 + m * 8]], axis=0)
                    grsend[m, h, pl.ds(at, 16), :] = both.astype(BF16)

    put(
        r == c,
        grsend.at[c, q],
        grrecv.at[r, q],
        ss_gr.at[0],
        rs_gr.at[r, q],
        (c, c, q),
    )

    @pl.loop(1, 16)
    def _(t):
        m, h = lax.rem(c + t // 2, 8), lax.rem(q + t, 2)
        far(grsend.at[m, h], grrecv.at[r, q], ss_gr.at[t], rs_gr.at[r, q], (c, m, h)).start()

    for h in range(2):
        for m in range(8):
            arrived(rrecv.at[h, m], ss_r.at[m], rs_r.at[h, m])

    @pl.loop(0, 16)
    def _(p):
        rows = pl.ds(pl.multiple_of(p * 16, 16), 16)
        for h in range(2):
            got = [rrecv[h, m, rows, :].astype(F32) for m in range(8)]
            one = jnp.concatenate([g[:NQ] for g in got], axis=0).astype(BF16)
            two = jnp.concatenate([g[NQ:] for g in got], axis=0).astype(BF16)
            lanes = slice(h * NS, (h + 1) * NS)
            first = pl.ds(pl.multiple_of(p * 128, 128), 64)
            second = pl.ds(pl.multiple_of(p * 128 + 64, 64), 64)
            rscr[0, first, lanes] = one
            rscr[0, second, lanes] = two
            rscr[1, first, lanes] = two
            rscr[1, second, lanes] = one

    @pl.loop(0, 4)
    def _(t):
        m = lax.rem(c + t, 4)
        rows = pl.ds(pl.multiple_of(lax.rem(m, 2) * 256, 256), 256)
        g = dot(d2[m // 2, rows, :], rscr[m // 2], 1, 0)
        for h in range(2):
            glsend[m, h] = g[:, h * NS : (h + 1) * NS].astype(BF16)
            put(
                jnp.logical_and(4 * q + m == c, q == h),
                glsend.at[m, h],
                glrecv.at[c],
                ss_gl.at[m, h],
                rs_gl.at[c],
                (r, 4 * q + m, h),
            )

    @pl.loop(0, 8)
    def _(t):
        here = pl.ds(pl.multiple_of(t * 256, 256), 256)
        a = dot(lscr[0], rscr[0, here, :], 1, 1)
        b = dot(lscr[1], rscr[1, here, :], 1, 1)
        for u in range(2):
            at = pl.ds(pl.multiple_of((t * 2 + u) * NP, NP), NP)
            for k in range(16):
                va = a[k * NP : (k + 1) * NP, u * 128 : (u + 1) * 128]
                vb = b[k * NP : (k + 1) * NP, u * 128 : (u + 1) * 128]
                beo[0, at, k * 128 : (k + 1) * 128] = jnp.where(low, va, vb).astype(BF16)
                beo[1, at, k * 128 : (k + 1) * 128] = jnp.where(low, vb, va).astype(BF16)

    for h in range(2):
        part = dot(beo[h], s12[h], 1, 0)
        for p in range(16):
            dwf[pl.ds(2 * p + h, NP, stride=NP), :] = part[p * NP : (p + 1) * NP]
    for m in range(8):
        dwsend[m] = dwf[m * 128 : (m + 1) * 128, :].astype(BF16)
    pltpu.make_async_copy(dwsend.at[c], dwrecv.at[c], rs_dw.at[c]).start()

    @pl.loop(1, 8)
    def _(t):
        m = lax.rem(c + t, 8)
        far(dwsend.at[m], dwrecv.at[c], ss_dw.at[t], rs_dw.at[c], (r, m, q)).start()

    @pl.loop(0, 8)
    def _(t):
        here = pl.ds(pl.multiple_of(t * 256, 256), 256)
        a = dot(wsplit[0], beo[0, :, here], 0, 0)
        b = dot(wsplit[1], beo[1, :, here], 0, 0)
        for u in range(2):
            lanes = slice(u * 128, (u + 1) * 128)
            o = (a[:, lanes] + pltpu.roll(b[:, lanes], 64, 1)).T
            k = t * 2 + u
            inc_ref[k] = (o[:64] * inv[k]).astype(BF16)
            inc_ref[k + 16] = (o[64:] * inv[k + 16]).astype(BF16)

    for m in range(8):
        arrived(dwrecv.at[m], ss_dw.at[m], rs_dw.at[m])
    total = dwrecv[0].astype(F32)
    for m in range(1, 8):
        total = total + dwrecv[m].astype(F32)
    e1[...] = total
    me = r * 2 + q
    pltpu.make_async_copy(e1.at[pl.ds(pl.multiple_of(me * 8, 8), 8), :], e1recv.at[me], rs_e1.at[me]).start()

    @pl.loop(1, 16)
    def _(t):
        m = lax.rem(me + t, 16)
        far(
            e1.at[pl.ds(pl.multiple_of(m * 8, 8), 8), :],
            e1recv.at[me],
            ss_e1.at[t],
            rs_e1.at[me],
            (m // 2, c, lax.rem(m, 2)),
        ).start()

    for m in range(8):
        arrived(glrecv.at[m], ss_gl.at[0, 0], rs_gl.at[m])
    for m in range(8):
        for h in range(2):
            arrived(grrecv.at[m, h], ss_gr.at[0], rs_gr.at[m, h])
    gl = glrecv[0].astype(F32)
    for m in range(1, 8):
        gl = gl + glrecv[m].astype(F32)
    gr = jnp.zeros((256, NS), F32)
    for m in range(8):
        for h in range(2):
            gr = gr + grrecv[m, h].astype(F32)
    tmp[...] = gr
    fsum = jnp.zeros((128, NCH), F32)
    for k in range(NQ):
        g = jnp.concatenate([gl[k * NP : (k + 1) * NP], tmp[pl.ds(k, NP, stride=NQ), :]], axis=0)
        g = g * mine[k : k + 1, :]
        high = g.astype(BF16)
        rest = (g - high.astype(F32)).astype(BF16)
        g2 = jnp.concatenate([high, rest], axis=0)
        gown[k] = g2
        fsum = fsum + dot(g2, nres[k], 1, 0)
    fsum = fsum[:64] + fsum[64:]
    for m in range(8):
        fsend[m] = fsum[m * 8 : (m + 1) * 8]
    pltpu.make_async_copy(fsend.at[c], frecv.at[c], rs_f.at[c]).start()

    @pl.loop(1, 8)
    def _(t):
        m = lax.rem(c + t, 8)
        far(fsend.at[m], frecv.at[c], ss_f.at[t], rs_f.at[c], (r, m, q)).start()

    w2x = jnp.concatenate([wt[...], wt[...]], axis=0)

    def adjoint(k):
        d = dot(gown[k], w2x, 0, 0)
        at = pl.ds(k, NS, stride=NQ)
        z = both_halves(xh, at)
        scale = rs[at, :]
        m1 = jnp.mean(d, axis=-1, keepdims=True)
        m2 = jnp.mean(d * z, axis=-1, keepdims=True)
        o = d - m1 - z * m2
        oscr[0, at, :] = scale * o[:, :128]
        oscr[1, at, :] = scale * o[:, 128:]

    for k in range(0, 2):
        adjoint(k)

    for m in range(16):
        arrived(e1recv.at[m], ss_e1.at[m], rs_e1.at[m])
    total = e1recv[0]
    for m in range(1, 16):
        total = total + e1recv[m]
    e2[...] = total
    pltpu.make_async_copy(e2, e2recv.at[me], rs_e2.at[me]).start()

    @pl.loop(1, 16)
    def _(t):
        m = lax.rem(me + t, 16)
        far(e2, e2recv.at[me], ss_e2.at[t], rs_e2.at[me], (m // 2, c, lax.rem(m, 2))).start()

    for m in range(8):
        arrived(frecv.at[m], ss_f.at[m], rs_f.at[m])
    total = frecv[0]
    for m in range(1, 8):
        total = total + frecv[m]
    f1[...] = total
    pltpu.make_async_copy(f1, f1recv.at[me], rs_f1.at[me]).start()

    @pl.loop(1, 16)
    def _(t):
        m = lax.rem(me + t, 16)
        far(f1, f1recv.at[me], ss_f1.at[t], rs_f1.at[me], (m // 2, c, lax.rem(m, 2))).start()

    for k in range(2, 5):
        adjoint(k)

    for m in range(16):
        arrived(e2recv.at[m], ss_e2.at[m], rs_e2.at[m])
    for m in range(16):
        e3[m * 8 : (m + 1) * 8, :] = e2recv[m]
    rows = pl.ds(pl.multiple_of(c * 128, 128), 128)
    pltpu.make_async_copy(e3, dwo_ref.at[rows, :], rs_e3.at[c]).start()

    @pl.loop(1, 8)
    def _(t):
        far(e3, dwo_ref.at[rows, :], ss_e3.at[t], rs_e3.at[c], (r, lax.rem(c + t, 8), q)).start()

    for m in range(16):
        arrived(f1recv.at[m], ss_f1.at[m], rs_f1.at[m])
    total = f1recv[0]
    for m in range(1, 16):
        total = total + f1recv[m]
    f2[...] = total
    pltpu.make_async_copy(f2, f2recv.at[c], rs_f2.at[c]).start()

    @pl.loop(1, 8)
    def _(t):
        far(f2, f2recv.at[c], ss_f2.at[t], rs_f2.at[c], (r, lax.rem(c + t, 8), q)).start()

    for k in range(5, 8):
        adjoint(k)

    @pl.loop(0, 8)
    def _(t):
        aadj_ref[pl.ds(t * 16, 16)] = both_halves(oscr, pl.ds(t * 128, 128)).reshape(16, NQ, NCH).astype(BF16)

    for m in range(8):
        arrived(f2recv.at[m], ss_f2.at[m], rs_f2.at[m])
    fa_ref[...] = jnp.concatenate([f2recv[m] for m in range(4)], axis=0).T
    sa_ref[...] = jnp.concatenate([f2recv[m] for m in range(4, 8)], axis=0).T
    for m in range(8):
        arrived(dwo_ref.at[pl.ds(m * 128, 128), :], ss_e3.at[m], rs_e3.at[m])

    @pl.when(q == qd)
    def _():
        @pl.loop(1, 8)
        def _(t):
            sent(msend, ss_mr.at[t], rs_mr.at[0])

    @pl.loop(1, 8)
    def _(t):
        sent(msend, ss_mc.at[t], rs_mc.at[0])
        sent(lsend, ss_l.at[t], rs_l.at[0, 0])
        sent(dwsend.at[0], ss_dw.at[t], rs_dw.at[0])
        sent(fsend.at[0], ss_f.at[t], rs_f.at[0])
        sent(f2, ss_f2.at[t], rs_f2.at[0])
        sent(e3, ss_e3.at[t], rs_e3.at[0])

    @pl.loop(1, 16)
    def _(t):
        sent(rsend, ss_r.at[t], rs_r.at[0, 0])
        sent(grsend.at[0, 0], ss_gr.at[t], rs_gr.at[0, 0])
        sent(f1, ss_f1.at[t], rs_f1.at[0])
        sent(e2, ss_e2.at[t], rs_e2.at[0])
        sent(e2, ss_e1.at[t], rs_e1.at[0])

    @pl.when(c != r)
    def _():
        sent(msend, ss_mc.at[0], rs_mc.at[0])
        sent(rsend, ss_r.at[0], rs_r.at[0, 0])
        sent(grsend.at[0, 0], ss_gr.at[0], rs_gr.at[0, 0])

    @pl.when(q != qd)
    def _():
        sent(lsend, ss_l.at[0], rs_l.at[0, 0])

    for m in range(4):
        for h in range(2):

            @pl.when(jnp.logical_not(jnp.logical_and(4 * q + m == c, q == h)))
            def _(m=m, h=h):
                sent(glsend.at[0, 0], ss_gl.at[m, h], rs_gl.at[0])


def local(x, occ, w1, w2, wo, cot):
    vmem = pl.BlockSpec(memory_space=pltpu.VMEM)
    dma = pltpu.SemaphoreType.DMA
    scratch = [
        pltpu.VMEM((2, 16, NS), BF16),
        pltpu.VMEM((4, 2, 16, NS), BF16),
        pltpu.VMEM((8, 2, 16, NS), BF16),
        pltpu.VMEM((2, 1024, 128), F32),
        pltpu.VMEM((1024, 128), F32),
        pltpu.VMEM((NQ, NS, NCH), BF16),
        pltpu.VMEM((256, NS), F32),
        pltpu.VMEM((256, NS), BF16),
        pltpu.VMEM((256, NS), BF16),
        pltpu.VMEM((2, 4, 256, NS), BF16),
        pltpu.VMEM((2, 8, 256, NS), BF16),
        pltpu.VMEM((64, NCH), BF16),
        pltpu.VMEM((2, HALF, NZ), BF16),
        pltpu.VMEM((1024, NZ), F32),
        pltpu.VMEM((32, 64, NZ), F32),
        pltpu.VMEM((2, PAIRS, NZ), BF16),
        pltpu.VMEM((2, HALF, PAIRS), BF16),
        pltpu.VMEM((2, HALF, 256), BF16),
        pltpu.VMEM((2, PAIRS, 256), BF16),
        pltpu.VMEM((2, HALF, PAIRS), BF16),
        pltpu.VMEM((8, 2, 256, NS), BF16),
        pltpu.VMEM((4, 2, 256, NS), BF16),
        pltpu.VMEM((8, 256, NS), BF16),
        pltpu.VMEM((8, 2, 256, NS), BF16),
        pltpu.VMEM((1024, NZ), F32),
        pltpu.VMEM((8, 128, NZ), BF16),
        pltpu.VMEM((8, 128, NZ), BF16),
        pltpu.VMEM((8, 8, NCH), F32),
        pltpu.VMEM((8, 8, NCH), F32),
        pltpu.VMEM((8, NCH), F32),
        pltpu.VMEM((16, 8, NCH), F32),
        pltpu.VMEM((8, NCH), F32),
        pltpu.VMEM((8, 8, NCH), F32),
        pltpu.VMEM((128, NZ), F32),
        pltpu.VMEM((16, 8, NZ), F32),
        pltpu.VMEM((8, NZ), F32),
        pltpu.VMEM((16, 8, NZ), F32),
        pltpu.VMEM((128, NZ), F32),
        pltpu.VMEM((NQ, 128, NS), BF16),
        pltpu.VMEM((2, 1024, 128), F32),
        dma((8,)),
        dma((4,)),
        dma((8,)),
        dma((8,)),
        dma((8,)),
        dma((2, 4)),
        dma((16,)),
        dma((2, 8)),
        dma((4, 2)),
        dma((8,)),
        dma((16,)),
        dma((8, 2)),
        dma((8,)),
        dma((8,)),
        dma((8,)),
        dma((8,)),
        dma((16,)),
        dma((16,)),
        dma((8,)),
        dma((8,)),
        dma((16,)),
        dma((16,)),
        dma((16,)),
        dma((16,)),
        dma((8,)),
        dma((8,)),
    ]
    return pl.pallas_call(
        kernel,
        out_shape=(
            jax.ShapeDtypeStruct((32, 64, NZ), BF16),
            jax.ShapeDtypeStruct((NS, NQ, NCH), BF16),
            jax.ShapeDtypeStruct((NCH, NP), F32),
            jax.ShapeDtypeStruct((NCH, NP), F32),
            jax.ShapeDtypeStruct((1024, NZ), F32),
        ),
        in_specs=[vmem] * 6,
        out_specs=(vmem,) * 5,
        scratch_shapes=scratch,
        compiler_params=pltpu.CompilerParams(vmem_limit_bytes=56 * 1024 * 1024, has_side_effects=True),
    )(x, occ, w1, w2, wo, cot)


def solution(mesh):
    placed = (
        P("seq", ("row", "col"), None),
        P(None, ("row", "col")),
        P(),
        P(),
        P(),
        P(("row", "seq"), "col", None),
    )
    return jax.shard_map(
        local,
        mesh=mesh,
        in_specs=placed,
        out_specs=(P(("row", "seq"), "col", None), P("seq", ("row", "col"), None), P(), P(), P()),
        check_vma=False,
    )
```

time: 918 us -> 139 us (0.15)
  waiting for transfers between devices: 673 us -> 0 us
  Pallas kernels: 0 us -> 129 us
  local copies, waits for them, and re-layouts: 99.6 us -> 9.26 us
  matrix products: 71.9 us -> 0 us
  blocking collectives: 42.6 us -> 0 us
  between operations: 14.3 us -> 0.66 us
  other arithmetic: 13 us -> 0 us
    psum x5 -> x0, waiting for transfers between devices: 465 us -> none  [the longest x2 274 us: local(): lax.psum((first_factor_adjoint, second_factor_adjoint, d_wo), ('row', 'co...]
    reduce_scatter x1 -> x0, waiting for transfers between devices: 185 us -> none  [local(): lax.psum_scatter(outer.reshape(half * lax.axis_size('seq'), block, OUTER)...]
    pallas_call x0 -> x1, Pallas kernels: none -> 129 us  [local(): pl.pallas_call(kernel, out_shape=(jax.ShapeDtypeStruct((32, 64, NZ), BF16...]
    reshape x3 -> x0, local copies, waits for them, and re-layouts: 73.6 us -> none  [the longest x2 47.1 us: local(): d_outer = d_outer.reshape(number, block, PROJ_DIM, PROJ_DIM)]
    dot_general x13 -> x0, matrix products: 71.9 us -> none  [the longest x1 13.9 us: local(): jnp.einsum('sic,sje->ijce', lblock, right_cols, preferred_element_type=jn...]
    psum x1 -> x0, blocking collectives: 27.3 us -> none  [broadcast(): return lax.psum(jnp.where(mine, value, jnp.zeros_like(value)), axis)]
    all_gather x2 -> x0, waiting for transfers between devices: 22.8 us -> none  [the longest x1 22.8 us: local(): piece = lax.all_gather(scaled, 'seq', axis=0, tiled=True)]
    all_gather x1 -> x0, blocking collectives: 15.3 us -> none  [local(): lax.all_gather(occupancy_matrix.astype(jnp.bfloat16), 'col', axis=1, tile...]
  transfers between devices with their start and end apart: 8 -> 0, of which waited for: 7 -> 0; matrix products, arithmetic and copies ran while one was open for 19% -> 0% of each run, Pallas kernels for 0% -> 0%
where the time goes in v1:
time: 139 us
  Pallas kernels  129 us (93%)
  local copies, waits for them, and re-layouts  9.26 us (7%)
    pallas_call x1, Pallas kernels, local(): pl.pallas_call(kernel, out_shape=(jax.ShapeDtypeStruct((32, 64, NZ), BF16...  129 us
    unnamed x16, local copies, waits for them, and re-layouts  6.94 us

profile of v1, /device:TPU:1, one launch (start us, length us, event | category | flops | bytes accessed | tf_op | source)
XLA Modules:
  0.0 138.6 jit_solution(18337351831655442045)
XLA Ops:
  0.6 0.0 copy-start.3
  0.6 1.5 %copy.12.w1_ref = bf16[256,32]{1,0:T(8,128)(2,1)} copy(bf16[256,32]{0,1:T(8,128)(2,1)} %param.8) | data formatting | bytes 32768 | tf_op args[2]
  2.1 0.0 copy-done.3
  2.1 0.0 copy-start.4
  2.1 0.7 copy.13.w2_ref
  2.8 0.0 copy-done.4
  2.8 0.8 copy.11.occ_ref
  3.6 128.7 %shard_map.101 = (bf16[32,64,128]{2,1,0:T(8,128)(2,1)}, bf16[128,8,256]{2,1,0:T(8,128)(2,1)}, f32[256,32]{1,0:T(8,128)}, f32[256,32]{1,0:T(8,128)}, f32[1024,128]{1,0:T(8,128)}) custom-call(bf16[128,8,256]{2,1,0:T(8,128)(2,1)} %x_ref.1, s32[256,8]{1,0:T(8,128)} %copy.11.occ_ref, bf16[256,32]{1,0:T(8,128)(2,1)} %copy.12.w1_ref, bf16[256,32]{1,0:T(8,128)(2,1)} %copy.13.w2_ref, ...), custom_call_target="tpu_custom_call" | custom-call | tf_op jit(solution)/shard_map/pallas_call | solution.py:583
  132.4 0.0 copy-start.2
  132.4 1.6 %copy.14 = f32[256,32]{0,1:T(8,128)} copy(f32[256,32]{1,0:T(8,128)} %get-tuple-element.7) | data formatting | bytes 65536 | tf_op jit(solution)/shard_map/pallas_call | solution.py:583
  134.0 0.0 copy-done.2
  134.0 0.7 copy.15
  134.7 0.0 copy-start.1
  134.7 1.9 %copy.19 = bf16[32,64,128]{2,1,0:T(8,128)(2,1)} copy(bf16[32,64,128]{2,1,0:T(8,128)(2,1)} %get-tuple-element.15) | data formatting | bytes 1048576
  136.6 0.0 copy-done.1
  136.6 0.0 copy-start
  136.6 0.8 copy.20
  137.4 0.4 copy-done
  137.9 0.8 copy.21
Async XLA Ops:
  0.6 1.5 %copy-start.3 = (bf16[256,32]{0,1:T(8,128)(2,1)S(1)}, bf16[256,32]{0,1:T(8,128)(2,1)}, u32[]{:S(2)}) copy-start(bf16[256,32]{0,1:T(8,128)(2,1)} %param.9) | copy-start | bytes 49156
  2.1 0.7 copy-start.4
  132.4 1.6 %copy-start.2 = (f32[256,32]{1,0:T(8,128)S(1)}, f32[256,32]{1,0:T(8,128)}, u32[]{:S(2)}) copy-start(f32[256,32]{1,0:T(8,128)} %get-tuple-element.8) | copy-start | bytes 98308
  134.7 1.9 %copy-start.1 = (bf16[128,8,256]{2,1,0:T(8,128)(2,1)S(1)}, bf16[128,8,256]{2,1,0:T(8,128)(2,1)}, u32[]{:S(2)}) copy-start(bf16[128,8,256]{2,1,0:T(8,128)(2,1)} %get-tuple-element.16) | copy-start | bytes 1572868
  136.6 1.2 copy-start

commit v2 on v1

--- a/solution.py
+++ b/solution.py
@@ -59,9 +59,15 @@
     rscr,
     beo,
     grsend,
-    glsend,
-    glrecv,
     grrecv,
+    grt,
+    grown,
+    glp,
+    gls,
+    gly,
+    glz,
+    gla,
+    glown,
     dwf,
     dwsend,
     dwrecv,
@@ -83,13 +89,21 @@
     ss_mc,
     rs_mc,
     ss_l,
-    rs_l,
+    rs_lx,
+    rs_ly,
+    rs_lsx,
+    rs_lsy,
     ss_r,
     rs_r,
     ss_gl,
-    rs_gl,
+    rs_gs,
+    rs_gz,
+    rs_ga,
+    rs_go,
     ss_gr,
     rs_gr,
+    ss_gt,
+    rs_gt,
     ss_dw,
     rs_dw,
     ss_f,
@@ -106,8 +120,26 @@
     rs_e3,
 ):
     r, c, q = lax.axis_index("row"), lax.axis_index("col"), lax.axis_index("seq")
-    qd = c // 4
+    inner = q == c // 4
+    outside = jnp.logical_not(inner)
+    diagonal = r == c
+    me = r * 2 + q
+    core, z = lax.rem(c, 2), c // 2
+    parity = lax.rem(z, 2)
+    sibling = (r, c + 1 - 2 * core, q)
+    beside = (r, (z + 1 - 2 * parity) * 2 + core, q)
+    across = (r, lax.rem(z + 3 - 2 * parity, 4) * 2 + core, q)
+    turned = (c, r, q)
+    opposite = (r, c, 1 - q)
     other = (r, lax.rem(c + 1, 8), q)
+
+    def plane(t):
+        m = lax.rem(me + t, 16)
+        return m, (m // 2, c, lax.rem(m, 2))
+
+    def line(t):
+        m = lax.rem(c + t, 8)
+        return m, (r, m, q)
 
     def far(src, dst, ssem, rsem, dev):
         return pltpu.make_async_remote_copy(
@@ -129,28 +161,24 @@
     def sent(slot, ssem, rsem):
         far(slot, slot, ssem, rsem, other).wait_send()
 
-    occ = occ_ref[...].astype(F32).astype(BF16)
-    eye = (
-        lax.broadcasted_iota(jnp.int32, (16, NQ), 0) == lax.broadcasted_iota(jnp.int32, (16, NQ), 1)
-    ).astype(F32).astype(BF16)
+    barrier = pltpu.get_barrier_semaphore()
+
+    @pl.loop(1, 16)
+    def _(t):
+        pl.semaphore_signal(barrier, inc=1, device_id=plane(t)[1], device_id_type=MESH)
+
+    @pl.loop(1, 8)
+    def _(t):
+        pl.semaphore_signal(barrier, inc=1, device_id=line(t)[1], device_id_type=MESH)
+
+    @pl.when(jnp.logical_not(diagonal))
+    def _():
+        pl.semaphore_signal(barrier, inc=1, device_id=turned, device_id_type=MESH)
+
+    occ = occ_ref[...].astype(F32)
+    occ = jnp.concatenate([occ, jnp.zeros((8, 2 * NS), F32)], axis=0).astype(BF16)
     for h in range(2):
-        msend[h] = dot(eye, occ[h * NS : (h + 1) * NS], 1, 1).astype(BF16)
-
-    @pl.when(q == qd)
-    def _():
-        pltpu.make_async_copy(msend, mrow.at[lax.rem(c, 4)], rs_mr.at[lax.rem(c, 4)]).start()
-
-        @pl.loop(1, 8)
-        def _(t):
-            far(
-                msend, mrow.at[lax.rem(c, 4)], ss_mr.at[t], rs_mr.at[lax.rem(c, 4)], (r, lax.rem(c + t, 8), q)
-            ).start()
-
-    put(c == r, msend, mcol.at[c], ss_mc.at[0], rs_mc.at[c], (r, r, q))
-
-    @pl.loop(1, 8)
-    def _(t):
-        far(msend, mcol.at[c], ss_mc.at[t], rs_mc.at[c], (lax.rem(r + t, 8), r, q)).start()
+        msend[h] = occ[:, h * NS : (h + 1) * NS]
 
     @pl.loop(0, 8)
     def _(t):
@@ -162,8 +190,20 @@
         xh[1, pl.ds(t * 128, 128), :] = z[:, 128:]
         rs[pl.ds(t * 128, 128), :] = jnp.broadcast_to(rstd, (128, 128))
 
-    wt[0:NP, :] = w1_ref[...].astype(F32).T.astype(BF16)
-    wt[NP:, :] = w2_ref[...].astype(F32).T.astype(BF16)
+    pl.semaphore_wait(barrier, jnp.where(diagonal, 22, 23))
+    put(diagonal, msend, mcol.at[c], ss_mc.at[0], rs_mc.at[c], turned)
+
+    @pl.when(inner)
+    def _():
+        m = lax.rem(c, 4)
+        pltpu.make_async_copy(msend, mrow.at[m], rs_mr.at[m]).start()
+
+        @pl.loop(1, 8)
+        def _(t):
+            far(msend, mrow.at[m], ss_mr.at[t], rs_mr.at[m], line(t)[1]).start()
+
+    wt[0:NP, :] = w1_ref[...]
+    wt[NP:, :] = w2_ref[...]
     mine = msend[q].astype(F32)
     for k in range(NQ):
         n = both_halves(xh, pl.ds(k, NS, stride=NQ)).astype(BF16)
@@ -173,28 +213,54 @@
         tmp[pl.ds(k, NP, stride=NQ), :] = p[NP:]
     rsend[...] = tmp[...].astype(BF16)
 
-    put(jnp.logical_and(c == r, True), rsend, rrecv.at[q, c], ss_r.at[0], rs_r.at[q, c], (r, r, q))
-
-    @pl.loop(1, 16)
-    def _(t):
-        dev = (lax.rem(r + t // 2, 8), r, lax.rem(q + t, 2))
-        far(rsend, rrecv.at[q, c], ss_r.at[t], rs_r.at[q, c], dev).start()
-
-    put(q == qd, lsend, lrecv.at[q, lax.rem(c, 4)], ss_l.at[0], rs_l.at[q, lax.rem(c, 4)], (r, c, qd))
-
-    @pl.loop(1, 8)
-    def _(t):
-        dev = (r, lax.rem(c + t, 8), qd)
-        far(lsend, lrecv.at[q, lax.rem(c, 4)], ss_l.at[t], rs_l.at[q, lax.rem(c, 4)], dev).start()
+    put(diagonal, rsend, rrecv.at[q, c], ss_r.at[0], rs_r.at[q, c], turned)
+    put(inner, lsend, lrecv.at[lax.rem(c, 4), q], ss_l.at[0], rs_lx.at[q], opposite)
 
     wide[...] = wo_ref[...].astype(F32)
     for e in range(NP):
         wsplit[e % 2, (e // 2) * NP : (e // 2 + 1) * NP, :] = wide[pl.ds(e, NP, stride=NP), :].astype(BF16)
 
+    arrived(mcol.at[r], ss_mc.at[0], rs_mc.at[r])
+
+    @pl.loop(1, 8)
+    def _(t):
+        far(mcol.at[r], mcol.at[r], ss_mc.at[t], rs_mc.at[r], (lax.rem(r + t, 8), c, q)).start()
+
+    arrived(rrecv.at[q, r], ss_r.at[0], rs_r.at[q, r])
+
+    @pl.loop(1, 16)
+    def _(t):
+        far(rrecv.at[q, r], rrecv.at[q, r], ss_r.at[t], rs_r.at[q, r], plane(t)[1]).start()
+
+    xslot = lax.rem(lax.rem(c, 4) + jnp.where(inner, 0, 2), 4)
+    yslot = lax.rem(xslot + 2, 4)
+    flip = 1 - 2 * core
+
+    def left_on(t):
+        h = lax.rem(q + t, 2)
+        slot = lrecv.at[xslot, h]
+        arrived(slot, ss_l.at[0], rs_lx.at[h])
+
+        @pl.when(inner)
+        def _():
+            far(slot, slot, ss_l.at[1 + t], rs_lx.at[h], across).start()
+
+        far(slot, slot, ss_l.at[3 + t], rs_ly.at[h], beside).start()
+        far(slot, slot, ss_l.at[5 + t], rs_lsx.at[h], sibling).start()
+
+    @pl.when(inner)
+    def _():
+        left_on(0)
+        left_on(1)
+
     for m in range(4):
         arrived(mrow.at[m], ss_mr.at[m], rs_mr.at[m])
     for m in range(8):
-        arrived(mcol.at[m], ss_mc.at[m], rs_mc.at[m])
+
+        @pl.when(r != m)
+        def _(m=m):
+            arrived(mcol.at[m], ss_mc.at[m], rs_mc.at[m])
+
     count = jnp.zeros((64, 32), F32)
     for h in range(2):
         rows = jnp.concatenate([mrow[m, h].astype(F32)[:NQ] for m in range(4)], axis=0).astype(BF16)
@@ -212,6 +278,11 @@
         s12[1, k * 128 : k * 128 + 64, :] = parts[1]
         s12[1, k * 128 + 64 : (k + 1) * 128, :] = parts[0]
 
+    @pl.when(outside)
+    def _():
+        left_on(0)
+        left_on(1)
+
     low = lax.broadcasted_iota(jnp.int32, (NP, 128), 1) < 64
 
     @pl.loop(0, 8)
@@ -227,10 +298,18 @@
                 d2[0, pl.ds(at, NP), p * 128 : (p + 1) * 128] = jnp.where(low, a, b).astype(BF16)
                 d2[1, pl.ds(at, NP), p * 128 : (p + 1) * 128] = jnp.where(low, b, a).astype(BF16)
 
+    for t in range(2):
+        h = lax.rem(q + t, 2)
+        slot = lrecv.at[yslot, h]
+        arrived(slot, ss_l.at[0], rs_ly.at[h])
+        far(slot, slot, ss_l.at[7 + t], rs_lsy.at[h], sibling).start()
+
+    for h in range(2):
+        arrived(lrecv.at[xslot + flip, h], ss_l.at[0], rs_lsx.at[h])
+        arrived(lrecv.at[yslot + flip, h], ss_l.at[0], rs_lsy.at[h])
     for h in range(2):
         for m in range(4):
-            arrived(lrecv.at[h, m], ss_l.at[m], rs_l.at[h, m])
-            lscr[m // 2, (m % 2) * 256 : (m % 2 + 1) * 256, h * NS : (h + 1) * NS] = lrecv[h, m]
+            lscr[m // 2, (m % 2) * 256 : (m % 2 + 1) * 256, h * NS : (h + 1) * NS] = lrecv[m, h]
 
     @pl.loop(0, 8)
     def _(t):
@@ -247,23 +326,17 @@
                     both = jnp.concatenate([gt[m * 8 : m * 8 + 8], gt[64 + m * 8 : 72 + m * 8]], axis=0)
                     grsend[m, h, pl.ds(at, 16), :] = both.astype(BF16)
 
-    put(
-        r == c,
-        grsend.at[c, q],
-        grrecv.at[r, q],
-        ss_gr.at[0],
-        rs_gr.at[r, q],
-        (c, c, q),
-    )
-
     @pl.loop(1, 16)
     def _(t):
-        m, h = lax.rem(c + t // 2, 8), lax.rem(q + t, 2)
-        far(grsend.at[m, h], grrecv.at[r, q], ss_gr.at[t], rs_gr.at[r, q], (c, m, h)).start()
+        m, dev = plane(t)
+        far(grsend.at[m // 2, lax.rem(m, 2)], grrecv.at[t], ss_gr.at[t], rs_gr.at[t], dev).start()
 
     for h in range(2):
         for m in range(8):
-            arrived(rrecv.at[h, m], ss_r.at[m], rs_r.at[h, m])
+
+            @pl.when(jnp.logical_or(q != h, r != m))
+            def _(h=h, m=m):
+                arrived(rrecv.at[h, m], ss_r.at[m], rs_r.at[h, m])
 
     @pl.loop(0, 16)
     def _(p):
@@ -280,21 +353,17 @@
             rscr[1, first, lanes] = two
             rscr[1, second, lanes] = one
 
-    @pl.loop(0, 4)
-    def _(t):
-        m = lax.rem(c + t, 4)
-        rows = pl.ds(pl.multiple_of(lax.rem(m, 2) * 256, 256), 256)
-        g = dot(d2[m // 2, rows, :], rscr[m // 2], 1, 0)
+    def left_piece(pp, k):
+        rows = pl.ds(pl.multiple_of(k * 256, 256), 256)
+        g = dot(d2[pp, rows, :], rscr[pp], 1, 0)
         for h in range(2):
-            glsend[m, h] = g[:, h * NS : (h + 1) * NS].astype(BF16)
-            put(
-                jnp.logical_and(4 * q + m == c, q == h),
-                glsend.at[m, h],
-                glrecv.at[c],
-                ss_gl.at[m, h],
-                rs_gl.at[c],
-                (r, 4 * q + m, h),
-            )
+            glp[pp * 2 + k, h] = g[:, h * NS : (h + 1) * NS].astype(BF16)
+
+    for pp in range(2):
+        left_piece(pp, 1 - core)
+        far(glp.at[pp * 2 + 1 - core], gls.at[pp], ss_gl.at[pp], rs_gs.at[pp], sibling).start()
+    for pp in range(2):
+        left_piece(pp, core)
 
     @pl.loop(0, 8)
     def _(t):
@@ -309,6 +378,11 @@
                 beo[0, at, k * 128 : (k + 1) * 128] = jnp.where(low, va, vb).astype(BF16)
                 beo[1, at, k * 128 : (k + 1) * 128] = jnp.where(low, vb, va).astype(BF16)
 
+    for pp in range(2):
+        arrived(gls.at[pp], ss_gl.at[pp], rs_gs.at[pp])
+    gly[...] = (glp[yslot].astype(F32) + gls[yslot // 2].astype(F32)).astype(BF16)
+    far(gly, glz, ss_gl.at[2], rs_gz.at[0], beside).start()
+
     for h in range(2):
         part = dot(beo[h], s12[h], 1, 0)
         for p in range(16):
@@ -321,6 +395,15 @@
     def _(t):
         m = lax.rem(c + t, 8)
         far(dwsend.at[m], dwrecv.at[c], ss_dw.at[t], rs_dw.at[c], (r, m, q)).start()
+
+    arrived(glz, ss_gl.at[2], rs_gz.at[0])
+    gls[xslot // 2] = (
+        glp[xslot].astype(F32) + gls[xslot // 2].astype(F32) + glz[...].astype(F32)
+    ).astype(BF16)
+
+    @pl.when(outside)
+    def _():
+        far(gls.at[xslot // 2], gla, ss_gl.at[3], rs_ga.at[0], across).start()
 
     @pl.loop(0, 8)
     def _(t):
@@ -334,13 +417,26 @@
             inc_ref[k] = (o[:64] * inv[k]).astype(BF16)
             inc_ref[k + 16] = (o[64:] * inv[k + 16]).astype(BF16)
 
+    @pl.when(inner)
+    def _():
+        arrived(gla, ss_gl.at[3], rs_ga.at[0])
+        glz[...] = (gls[xslot // 2].astype(F32) + gla[...].astype(F32)).astype(BF16)
+        pltpu.make_async_copy(glz.at[q], glown, rs_go.at[0]).start()
+        far(glz.at[1 - q], glown, ss_gl.at[4], rs_go.at[0], opposite).start()
+
+    total = grsend[r, q].astype(F32)
+    for t in range(1, 16):
+        arrived(grrecv.at[t], ss_gr.at[t], rs_gr.at[t])
+        total = total + grrecv[t].astype(F32)
+    grt[...] = total.astype(BF16)
+    put(diagonal, grt, grown, ss_gt.at[0], rs_gt.at[0], turned)
+
     for m in range(8):
         arrived(dwrecv.at[m], ss_dw.at[m], rs_dw.at[m])
     total = dwrecv[0].astype(F32)
     for m in range(1, 8):
         total = total + dwrecv[m].astype(F32)
     e1[...] = total
-    me = r * 2 + q
     pltpu.make_async_copy(e1.at[pl.ds(pl.multiple_of(me * 8, 8), 8), :], e1recv.at[me], rs_e1.at[me]).start()
 
     @pl.loop(1, 16)
@@ -354,19 +450,10 @@
             (m // 2, c, lax.rem(m, 2)),
         ).start()
 
-    for m in range(8):
-        arrived(glrecv.at[m], ss_gl.at[0, 0], rs_gl.at[m])
-    for m in range(8):
-        for h in range(2):
-            arrived(grrecv.at[m, h], ss_gr.at[0], rs_gr.at[m, h])
-    gl = glrecv[0].astype(F32)
-    for m in range(1, 8):
-        gl = gl + glrecv[m].astype(F32)
-    gr = jnp.zeros((256, NS), F32)
-    for m in range(8):
-        for h in range(2):
-            gr = gr + grrecv[m, h].astype(F32)
-    tmp[...] = gr
+    arrived(glown, ss_gl.at[4], rs_go.at[0])
+    arrived(grown, ss_gt.at[0], rs_gt.at[0])
+    gl = glown[...].astype(F32)
+    tmp[...] = grown[...].astype(F32)
     fsum = jnp.zeros((128, NCH), F32)
     for k in range(NQ):
         g = jnp.concatenate([gl[k * NP : (k + 1) * NP], tmp[pl.ds(k, NP, stride=NQ), :]], axis=0)
@@ -463,21 +550,34 @@
 
     for m in range(8):
         arrived(f2recv.at[m], ss_f2.at[m], rs_f2.at[m])
-    fa_ref[...] = jnp.concatenate([f2recv[m] for m in range(4)], axis=0).T
-    sa_ref[...] = jnp.concatenate([f2recv[m] for m in range(4, 8)], axis=0).T
+    fa_ref[...] = jnp.concatenate([f2recv[m] for m in range(4)], axis=0)
+    sa_ref[...] = jnp.concatenate([f2recv[m] for m in range(4, 8)], axis=0)
     for m in range(8):
         arrived(dwo_ref.at[pl.ds(m * 128, 128), :], ss_e3.at[m], rs_e3.at[m])
 
-    @pl.when(q == qd)
+    @pl.when(inner)
     def _():
         @pl.loop(1, 8)
         def _(t):
             sent(msend, ss_mr.at[t], rs_mr.at[0])
 
+        for t in range(2):
+            sent(lsend, ss_l.at[1 + t], rs_lx.at[0])
+        sent(glown, ss_gl.at[4], rs_go.at[0])
+
+    @pl.when(outside)
+    def _():
+        sent(lsend, ss_l.at[0], rs_lx.at[0])
+        sent(glz, ss_gl.at[3], rs_ga.at[0])
+
+    for t in range(3, 9):
+        sent(lsend, ss_l.at[t], rs_lx.at[0])
+    for t in range(3):
+        sent(glz, ss_gl.at[t], rs_gz.at[0])
+
     @pl.loop(1, 8)
     def _(t):
         sent(msend, ss_mc.at[t], rs_mc.at[0])
-        sent(lsend, ss_l.at[t], rs_l.at[0, 0])
         sent(dwsend.at[0], ss_dw.at[t], rs_dw.at[0])
         sent(fsend.at[0], ss_f.at[t], rs_f.at[0])
         sent(f2, ss_f2.at[t], rs_f2.at[0])
@@ -486,27 +586,16 @@
     @pl.loop(1, 16)
     def _(t):
         sent(rsend, ss_r.at[t], rs_r.at[0, 0])
-        sent(grsend.at[0, 0], ss_gr.at[t], rs_gr.at[0, 0])
+        sent(rsend, ss_gr.at[t], rs_gr.at[0])
         sent(f1, ss_f1.at[t], rs_f1.at[0])
         sent(e2, ss_e2.at[t], rs_e2.at[0])
         sent(e2, ss_e1.at[t], rs_e1.at[0])
 
-    @pl.when(c != r)
+    @pl.when(jnp.logical_not(diagonal))
     def _():
         sent(msend, ss_mc.at[0], rs_mc.at[0])
         sent(rsend, ss_r.at[0], rs_r.at[0, 0])
-        sent(grsend.at[0, 0], ss_gr.at[0], rs_gr.at[0, 0])
-
-    @pl.when(q != qd)
-    def _():
-        sent(lsend, ss_l.at[0], rs_l.at[0, 0])
-
-    for m in range(4):
-        for h in range(2):
-
-            @pl.when(jnp.logical_not(jnp.logical_and(4 * q + m == c, q == h)))
-            def _(m=m, h=h):
-                sent(glsend.at[0, 0], ss_gl.at[m, h], rs_gl.at[0])
+        sent(grt, ss_gt.at[0], rs_gt.at[0])
 
 
 def local(x, occ, w1, w2, wo, cot):
@@ -522,7 +611,7 @@
         pltpu.VMEM((256, NS), F32),
         pltpu.VMEM((256, NS), BF16),
         pltpu.VMEM((256, NS), BF16),
-        pltpu.VMEM((2, 4, 256, NS), BF16),
+        pltpu.VMEM((4, 2, 256, NS), BF16),
         pltpu.VMEM((2, 8, 256, NS), BF16),
         pltpu.VMEM((64, NCH), BF16),
         pltpu.VMEM((2, HALF, NZ), BF16),
@@ -534,9 +623,15 @@
         pltpu.VMEM((2, PAIRS, 256), BF16),
         pltpu.VMEM((2, HALF, PAIRS), BF16),
         pltpu.VMEM((8, 2, 256, NS), BF16),
+        pltpu.VMEM((16, 256, NS), BF16),
+        pltpu.VMEM((256, NS), BF16),
+        pltpu.VMEM((256, NS), BF16),
         pltpu.VMEM((4, 2, 256, NS), BF16),
-        pltpu.VMEM((8, 256, NS), BF16),
-        pltpu.VMEM((8, 2, 256, NS), BF16),
+        pltpu.VMEM((2, 2, 256, NS), BF16),
+        pltpu.VMEM((2, 256, NS), BF16),
+        pltpu.VMEM((2, 256, NS), BF16),
+        pltpu.VMEM((2, 256, NS), BF16),
+        pltpu.VMEM((256, NS), BF16),
         pltpu.VMEM((1024, NZ), F32),
         pltpu.VMEM((8, 128, NZ), BF16),
         pltpu.VMEM((8, 128, NZ), BF16),
@@ -557,14 +652,22 @@
         dma((4,)),
         dma((8,)),
         dma((8,)),
-        dma((8,)),
-        dma((2, 4)),
+        dma((9,)),
+        dma((2,)),
+        dma((2,)),
+        dma((2,)),
+        dma((2,)),
         dma((16,)),
         dma((2, 8)),
-        dma((4, 2)),
-        dma((8,)),
-        dma((16,)),
-        dma((8, 2)),
+        dma((5,)),
+        dma((2,)),
+        dma((1,)),
+        dma((1,)),
+        dma((1,)),
+        dma((16,)),
+        dma((16,)),
+        dma((1,)),
+        dma((1,)),
         dma((8,)),
         dma((8,)),
         dma((8,)),
@@ -580,20 +683,21 @@
         dma((8,)),
         dma((8,)),
     ]
-    return pl.pallas_call(
+    inc, aadj, fa, sa, dwo = pl.pallas_call(
         kernel,
         out_shape=(
             jax.ShapeDtypeStruct((32, 64, NZ), BF16),
             jax.ShapeDtypeStruct((NS, NQ, NCH), BF16),
-            jax.ShapeDtypeStruct((NCH, NP), F32),
-            jax.ShapeDtypeStruct((NCH, NP), F32),
+            jax.ShapeDtypeStruct((NP, NCH), F32),
+            jax.ShapeDtypeStruct((NP, NCH), F32),
             jax.ShapeDtypeStruct((1024, NZ), F32),
         ),
         in_specs=[vmem] * 6,
         out_specs=(vmem,) * 5,
         scratch_shapes=scratch,
-        compiler_params=pltpu.CompilerParams(vmem_limit_bytes=56 * 1024 * 1024, has_side_effects=True),
-    )(x, occ, w1, w2, wo, cot)
+        compiler_params=pltpu.CompilerParams(vmem_limit_bytes=56 * 1024 * 1024, has_side_effects=True, collective_id=0),
+    )(x, occ.T, w1.T, w2.T, wo, cot)
+    return inc, aadj, fa.T, sa.T, dwo
 
 
 def solution(mesh):

time: 139 us -> 81.9 us (0.59)
  Pallas kernels: 129 us -> 76.2 us
  local copies, waits for them, and re-layouts: 9.26 us -> 4.91 us
    pallas_call x1, Pallas kernels: 129 us -> 76.2 us  [local(): pl.pallas_call(kernel, out_shape=(jax.ShapeDtypeStruct((32, 64, NZ), BF16...]
    pallas_call x2 -> x0, local copies, waits for them, and re-layouts: 2.32 us -> none  [local(): pl.pallas_call(kernel, out_shape=(jax.ShapeDtypeStruct((32, 64, NZ), BF16...]
    unnamed x16 -> x13, local copies, waits for them, and re-layouts: 6.94 us -> 4.91 us
where the time goes in v2:
time: 81.9 us; the launch traced here: 81.7 us
  Pallas kernels  76.2 us (93%)
  local copies, waits for them, and re-layouts  4.91 us (6%)
    pallas_call x1, Pallas kernels, local(): pl.pallas_call(kernel, out_shape=(jax.ShapeDtypeStruct((32, 64, NZ), BF16...  76.2 us
    unnamed x13, local copies, waits for them, and re-layouts  4.91 us

profile of v2, /device:TPU:1, one launch (start us, length us, event | category | flops | bytes accessed | tf_op | source)
XLA Modules:
  0.0 81.7 jit_solution(12437606902735498200)
XLA Ops:
  0.6 76.2 %shard_map.101 = (bf16[32,64,128]{2,1,0:T(8,128)(2,1)}, bf16[128,8,256]{2,1,0:T(8,128)(2,1)}, f32[32,256]{1,0:T(8,128)}, f32[32,256]{1,0:T(8,128)}, f32[1024,128]{1,0:T(8,128)}) custom-call(bf16[128,8,256]{2,1,0:T(8,128)(2,1)} %x_ref.1, s32[8,256]{1,0:T(8,128)} %bitcast.9, bf16[32,256]{1,0:T(8,128)(2,1)} %bitcast.7, bf16[32,256]{1,0:T(8,128)(2,1)} %bitcast.8, ...), custom_call_target="tpu_custom_call" | custom-call | tf_op jit(solution)/shard_map/pallas_call | solution.py:686
  76.8 0.0 copy-start.1
  76.8 1.9 %copy.16 = bf16[32,64,128]{2,1,0:T(8,128)(2,1)} copy(bf16[32,64,128]{2,1,0:T(8,128)(2,1)} %get-tuple-element.20) | data formatting | bytes 1048576
  78.7 0.0 copy-done.1
  78.7 0.0 copy-start.3
  78.7 0.0 copy-start
  78.7 0.8 copy.17
  79.5 0.0 copy-done.3
  79.5 0.0 copy-start.2
  79.5 0.6 copy.18
  80.2 0.2 copy-done.2
  80.3 0.6 copy.19
  80.9 0.0 copy-done
  80.9 0.8 copy.20
Async XLA Ops:
  76.8 1.9 %copy-start.1 = (bf16[128,8,256]{2,1,0:T(8,128)(2,1)S(1)}, bf16[128,8,256]{2,1,0:T(8,128)(2,1)}, u32[]{:S(2)}) copy-start(bf16[128,8,256]{2,1,0:T(8,128)(2,1)} %get-tuple-element.21) | copy-start | bytes 1572868
  78.7 0.8 copy-start.3
  78.7 2.2 %copy-start = (f32[1024,128]{1,0:T(8,128)S(1)}, f32[1024,128]{1,0:T(8,128)}, u32[]{:S(2)}) copy-start(f32[1024,128]{1,0:T(8,128)} %get-tuple-element.24) | copy-start | bytes 1572868
  79.5 0.8 copy-start.2

commit v3 on v2

v3 whole, which is shorter than its diff:
```python
import jax
import jax.numpy as jnp
from jax import lax
from jax.experimental import pallas as pl
from jax.experimental.pallas import tpu as pltpu
from jax.sharding import PartitionSpec as P

F32 = jnp.float32
BF16 = jnp.bfloat16
MESH = pl.DeviceIdType.MESH

NS = 128
NQ = 8
NCH = 256
NP = 32
NZ = 128
HALF = 512
PAIRS = 2048


def dot(a, b, ca, cb):
    return lax.dot_general(a, b, (((ca,), (cb,)), ((), ())), preferred_element_type=F32)


def both_halves(ref, rows):
    return jnp.concatenate([ref[0, rows, :], ref[1, rows, :]], axis=1)


def kernel(
    x_ref,
    occ_ref,
    w1_ref,
    w2_ref,
    wo_hbm,
    cot_hbm,
    inc_hbm,
    aadj_ref,
    fa_ref,
    sa_ref,
    dwo_ref,
    wo_ref,
    cot_ref,
    inc_ref,
    msend,
    mrow,
    mcol,
    xh,
    rs,
    nres,
    tmp,
    lsend,
    rsend,
    lrecv,
    rrecv,
    wt,
    wsplit,
    wide,
    inv,
    s12,
    d2,
    lscr,
    lturn,
    wturn,
    rscr,
    beo,
    grsend,
    grrecv,
    grt,
    grown,
    glp,
    gls,
    glown,
    dwf,
    dwsend,
    dwrecv,
    fsend,
    frecv,
    f1,
    f1recv,
    f2,
    f2recv,
    e1,
    e1recv,
    e2,
    e3,
    gown,
    oscr,
    io_sem,
    ss_mr,
    rs_mr,
    ss_mc,
    rs_mc,
    ss_l,
    rs_l,
    rs_ls,
    ss_r,
    rs_r,
    ss_gl,
    rs_gs,
    rs_go,
    ss_gr,
    rs_gr,
    ss_gt,
    rs_gt,
    ss_dw,
    rs_dw,
    ss_f,
    rs_f,
    ss_f1,
    rs_f1,
    ss_f2,
    rs_f2,
    ss_e1,
    rs_e1,
    ss_e2,
    rs_e2,
    ss_e3,
    rs_e3,
):
    r, c, q = lax.axis_index("row"), lax.axis_index("col"), lax.axis_index("seq")
    inner = q == c // 4
    diagonal = r == c
    me = r * 2 + q
    core, z = lax.rem(c, 2), c // 2
    sibling = (r, c + 1 - 2 * core, q)
    turned = (c, r, q)
    other = (r, lax.rem(c + 1, 8), q)

    def plane(t):
        m = lax.rem(me + t, 16)
        return m, (m // 2, c, lax.rem(m, 2))

    def line(t):
        m = lax.rem(c + t, 8)
        return m, (r, m, q)

    def far(src, dst, ssem, rsem, dev):
        return pltpu.make_async_remote_copy(
            src_ref=src, dst_ref=dst, send_sem=ssem, recv_sem=rsem, device_id=dev, device_id_type=MESH
        )

    def put(own, src, dst, ssem, rsem, dev):
        @pl.when(own)
        def _():
            pltpu.make_async_copy(src, dst, rsem).start()

        @pl.when(jnp.logical_not(own))
        def _():
            far(src, dst, ssem, rsem, dev).start()

    def arrived(slot, ssem, rsem):
        far(slot, slot, ssem, rsem, other).wait_recv()

    def sent(slot, ssem, rsem):
        far(slot, slot, ssem, rsem, other).wait_send()

    load_wo = pltpu.make_async_copy(wo_hbm, wo_ref, io_sem.at[0])
    load_cot = pltpu.make_async_copy(cot_hbm, cot_ref, io_sem.at[1])
    save_inc = pltpu.make_async_copy(inc_ref, inc_hbm, io_sem.at[2])
    load_wo.start()
    load_cot.start()

    barrier = pltpu.get_barrier_semaphore()

    @pl.loop(1, 16)
    def _(t):
        pl.semaphore_signal(barrier, inc=1, device_id=plane(t)[1], device_id_type=MESH)

    @pl.loop(1, 8)
    def _(t):
        pl.semaphore_signal(barrier, inc=1, device_id=line(t)[1], device_id_type=MESH)

    y0, x0 = q * 2 + r // 4, lax.rem(r, 4)
    across = (r, lax.rem(z + 3 - 2 * lax.rem(z, 2), 4) * 2 + core, 1 - q)

    def at(y, x):
        return (lax.rem(y, 2) * 4 + x, c, y // 2)

    def along_x(t):
        return at(y0, lax.rem(x0 + t, 4))

    def along_y(t):
        return at(lax.rem(y0 + t, 4), x0)

    def along_z(t):
        return (r, lax.rem(z + t, 4) * 2 + core, q)

    def block(dy, dx, first, last):
        y, x = lax.rem(y0 + dy, 4), lax.rem(x0 + dx, 4)
        h, m = y // 2, lax.rem(y, 2) * 4 + x
        return rrecv.at[h, m, first:last, :], rs_r.at[h, m, first // 128]

    def mask_to(t):
        return (lax.rem(r + t, 8), r, q)

    def mask_from(t):
        return (c, lax.rem(c + t, 8), q)

    @pl.loop(1, 4)
    def _(t):
        dev = (r, lax.rem(z + t, 4) * 2 + core, 1 - q)
        pl.semaphore_signal(barrier, inc=1, device_id=dev, device_id_type=MESH)

    @pl.loop(1, 8)
    def _(t):
        pl.semaphore_signal(barrier, inc=1, device_id=mask_to(t), device_id_type=MESH)
        pl.semaphore_signal(barrier, inc=1, device_id=mask_from(t), device_id_type=MESH)

    @pl.when(jnp.logical_not(diagonal))
    def _():
        for dev in (mask_to(0), mask_from(0), turned):
            pl.semaphore_signal(barrier, inc=1, device_id=dev, device_id_type=MESH)

    occ = occ_ref[...].astype(F32)
    msend[...] = jnp.concatenate([occ[:, :NS], occ[:, NS:]], axis=0).astype(BF16)

    @pl.loop(0, 8)
    def _(t):
        xb = x_ref[pl.ds(t * 16, 16)].astype(F32).reshape(128, NCH)
        xc = xb - jnp.mean(xb, axis=-1, keepdims=True)
        rstd = lax.rsqrt(jnp.mean(xc * xc, axis=-1, keepdims=True) + 1e-05)
        z = xc * rstd
        xh[0, pl.ds(t * 128, 128), :] = z[:, :128]
        xh[1, pl.ds(t * 128, 128), :] = z[:, 128:]
        rs[pl.ds(t * 128, 128), :] = jnp.broadcast_to(rstd, (128, 128))

    pl.semaphore_wait(barrier, jnp.where(diagonal, 39, 42))
    put(diagonal, msend, mcol.at[c], ss_mc.at[0], rs_mc.at[c], mask_to(0))

    @pl.loop(1, 8)
    def _(t):
        far(msend, mcol.at[c], ss_mc.at[t], rs_mc.at[c], mask_to(t)).start()

    @pl.when(inner)
    def _():
        m = lax.rem(c, 4)
        pltpu.make_async_copy(msend, mrow.at[m], rs_mr.at[m]).start()

        @pl.loop(1, 8)
        def _(t):
            far(msend, mrow.at[m], ss_mr.at[t], rs_mr.at[m], line(t)[1]).start()

    wt[0:NP, :] = w1_ref[...]
    wt[NP:, :] = w2_ref[...]
    mine = msend[...].astype(F32)
    mine = jnp.where(q == 0, mine[:NQ], mine[NQ:])
    for k in range(NQ):
        n = both_halves(xh, pl.ds(k, NS, stride=NQ)).astype(BF16)
        nres[k] = n
        p = dot(wt[...], n, 1, 1) * mine[k : k + 1, :]
        lsend[k * NP : (k + 1) * NP, :] = p[:NP].astype(BF16)
        tmp[pl.ds(k, NP, stride=NQ), :] = p[NP:]
    rsend[...] = tmp[...].astype(BF16)

    mine_of_line = lax.rem(jnp.where(inner, z, z + 3 - 2 * lax.rem(z, 2)), 2)
    seq_of_line = jnp.where(inner, q, 1 - q)
    given = lrecv.at[mine_of_line * 2 + core, seq_of_line]
    given_mark = rs_l.at[mine_of_line, seq_of_line]

    def left_along():
        for t in range(1, 4):
            far(given, given, ss_l.at[t], given_mark, along_z(t)).start()
        far(given, given, ss_l.at[4], rs_ls.at[mine_of_line, seq_of_line], sibling).start()

    @pl.when(inner)
    def _():
        lrecv[lax.rem(c, 4), q] = lsend[...]
        left_along()

    @pl.when(jnp.logical_not(inner))
    def _():
        far(lsend, lrecv.at[lax.rem(c, 4), q], ss_l.at[0], rs_l.at[lax.rem(c, 4) // 2, q], across).start()

    put(diagonal, rsend, rrecv.at[q, c], ss_r.at[0], rs_r.at[q, c, 0], turned)

    load_wo.wait()
    wide[...] = wo_ref[...].astype(F32)
    for e in range(NP):
        wsplit[(e % 2) * HALF + (e // 2) * NP : (e % 2) * HALF + (e // 2 + 1) * NP, :] = wide[pl.ds(e, NP, stride=NP), :].astype(BF16)

    wturn[...] = wsplit[...].T

    @pl.when(jnp.logical_not(inner))
    def _():
        arrived(given, ss_l.at[0], given_mark)
        left_along()

    came, mark = block(0, 0, 0, 256)
    arrived(came, ss_r.at[0], mark)
    for t in range(1, 4):
        far(came, came, ss_r.at[t], mark, along_x(t)).start()
        far(came, came, ss_r.at[3 + t], mark, along_y(t)).start()

    for m in range(4):
        arrived(mrow.at[m], ss_mr.at[m], rs_mr.at[m])
    for m in range(8):
        arrived(mcol.at[m], ss_mc.at[m], rs_mc.at[m])

    count = jnp.zeros((64, 32), F32)
    across_lo = jnp.zeros((16, 128), F32)
    across_hi = jnp.zeros((16, 128), F32)
    for h in range(2):
        rows = jnp.concatenate([mrow[m].astype(F32)[h * NQ : (h + 1) * NQ] for m in range(4)], axis=0).astype(BF16)
        groups = [mcol[m].astype(F32)[h * NQ : (h + 1) * NQ] for m in range(8)]
        cols = jnp.concatenate(groups, axis=0).astype(BF16)
        twice = jnp.concatenate([g for g in groups for _ in range(2)], axis=0).astype(BF16)
        count = count + dot(cols, rows, 1, 1)
        across_lo = across_lo + dot(rows[:16], twice, 1, 1)
        across_hi = across_hi + dot(rows[16:], twice, 1, 1)
    lane = lax.broadcasted_iota(jnp.int32, (NP, 128), 1)
    low = lax.rem(lane // 8, 2) == 0
    inv[...] = 1.0 / (jnp.where(low[:16], across_lo, across_hi) + 0.001)
    over = 1.0 / (count + 0.001)
    load_cot.wait()
    for k in range(16):
        lo, hi = [
            cot_ref[i].astype(F32) * jnp.broadcast_to(over[:, i : i + 1], (64, NZ)) for i in (k, k + 16)
        ]
        pairs = [(lo[m * 8 : m * 8 + 8], hi[m * 8 : m * 8 + 8]) for m in range(8)]
        here = slice(k * 128, (k + 1) * 128)
        s12[0, here, :] = jnp.concatenate([g for a, b in pairs for g in (a, b)], axis=0).astype(BF16)
        s12[1, here, :] = jnp.concatenate([g for a, b in pairs for g in (b, a)], axis=0).astype(BF16)

    def outer_adjoint(t):
        here = pl.ds(pl.multiple_of(t * 256, 256), 256)
        even, odd = wsplit[:HALF], wsplit[HALF:]
        plain, turned_s = s12[0, here, :], s12[1, here, :]
        halves = (
            (dot(even, plain, 1, 1), dot(odd, turned_s, 1, 1)),
            (dot(even, turned_s, 1, 1), dot(odd, plain, 1, 1)),
        )
        for u in range(2):
            for half, (a, b) in enumerate(halves):
                at = pl.ds(pl.multiple_of(half * HALF + (t * 2 + u) * NP, NP), NP)
                for p in range(16):
                    va = a[p * NP : (p + 1) * NP, u * 128 : (u + 1) * 128]
                    vb = b[p * NP : (p + 1) * NP, u * 128 : (u + 1) * 128]
                    d2[at, p * 128 : (p + 1) * 128] = jnp.where(low, va, vb).astype(BF16)

    pl.loop(0, 4)(outer_adjoint)

    for t in range(1, 4):
        zt = lax.rem(z + t, 4)
        in_half = zt // 2 == q
        pp = lax.rem(jnp.where(in_half, zt, zt + 3 - 2 * lax.rem(zt, 2)), 2)
        h = jnp.where(in_half, q, 1 - q)
        slot = lrecv.at[pp * 2 + core, h]
        arrived(slot, ss_l.at[0], rs_l.at[pp, h])
        far(slot, slot, ss_l.at[4 + t], rs_ls.at[pp, h], sibling).start()

    for t in range(1, 4):
        whole, mark = block(0, t, 0, 256)
        arrived(whole, ss_r.at[0], mark)
        half, mark = block(0, t, 0, 128)
        for u in range(1, 4):
            far(half, half, ss_r.at[3 + t * 3 + u], mark, along_y(u)).start()
        whole, mark = block(t, 0, 0, 256)
        arrived(whole, ss_r.at[0], mark)
        half, mark = block(t, 0, 128, 256)
        for u in range(1, 4):
            far(half, half, ss_r.at[12 + t * 3 + u], mark, along_x(u)).start()

    pl.loop(4, 8)(outer_adjoint)

    for pp in range(2):
        for h in range(2):
            arrived(lrecv.at[pp * 2 + 1 - core, h], ss_l.at[0], rs_ls.at[pp, h])
    for h in range(2):
        for m in range(4):
            lscr[m * 256 : (m + 1) * 256, h * NS : (h + 1) * NS] = lrecv[m, h]
            lturn[h * NS : (h + 1) * NS, m * 256 : (m + 1) * 256] = lrecv[m, h].T

    @pl.loop(0, 8)
    def _(t):
        here = pl.ds(pl.multiple_of(t * 256, 256), 256)
        a = dot(lturn[...], d2[:, here], 1, 0).astype(BF16)
        for u in range(2):
            at = pl.ds(pl.multiple_of((t * 2 + u) * 16, 16), 16)
            for h in range(2):
                gt = a[h * NS : (h + 1) * NS, u * 128 : (u + 1) * 128].T
                for m in range(8):
                    grsend[m, h, at, :] = gt[m * 16 : (m + 1) * 16]

    @pl.loop(1, 16)
    def _(t):
        m, dev = plane(t)
        far(grsend.at[m // 2, lax.rem(m, 2)], grrecv.at[t], ss_gr.at[t], rs_gr.at[t], dev).start()

    for t in range(1, 4):
        for u in range(1, 4):
            for first in (0, 128):
                half, mark = block(t, u, first, first + 128)
                arrived(half, ss_r.at[0], mark)

    @pl.loop(0, 16)
    def _(p):
        rows = pl.ds(pl.multiple_of(p * 16, 16), 16)
        for h in range(2):
            lanes = slice(h * NS, (h + 1) * NS)
            for m in range(8):
                at = pl.ds(pl.multiple_of(p * 128 + m * 16, 16), 16)
                v = rrecv[h, m, rows, :]
                w = v.astype(F32)
                rscr[0, at, lanes] = v
                rscr[1, at, lanes] = jnp.concatenate([w[8:], w[:8]], axis=0).astype(BF16)

    def outer_product(t):
        here = pl.ds(pl.multiple_of(t * 256, 256), 256)
        a = dot(lscr[...], rscr[0, here, :], 1, 1)
        b = dot(lscr[...], rscr[1, here, :], 1, 1)
        for u in range(2):
            lanes = slice(u * 128, (u + 1) * 128)
            even = pl.ds(pl.multiple_of((t * 2 + u) * NP, NP), NP)
            odd = pl.ds(pl.multiple_of(HALF + (t * 2 + u) * NP, NP), NP)
            for k in range(16):
                lo = slice(k * NP, (k + 1) * NP)
                hi = slice(HALF + k * NP, HALF + (k + 1) * NP)
                beo[even, k * 128 : (k + 1) * 128] = jnp.where(low, a[lo, lanes], b[hi, lanes]).astype(BF16)
                beo[odd, k * 128 : (k + 1) * 128] = jnp.where(low, b[lo, lanes], a[hi, lanes]).astype(BF16)

    pl.loop(0, 4)(outer_product)

    pl.loop(4, 8)(outer_product)

    part = dot(beo[...], s12[0], 1, 0)
    for h in range(2):
        for p in range(16):
            dwf[pl.ds(2 * p + h, NP, stride=NP), :] = part[h * HALF + p * NP : h * HALF + (p + 1) * NP]
    for m in range(8):
        dwsend[m] = dwf[m * 128 : (m + 1) * 128, :].astype(BF16)
    pltpu.make_async_copy(dwsend.at[c], dwrecv.at[c], rs_dw.at[c]).start()

    @pl.loop(1, 8)
    def _(t):
        m = lax.rem(c + t, 8)
        far(dwsend.at[m], dwrecv.at[c], ss_dw.at[t], rs_dw.at[c], (r, m, q)).start()

    def left_piece(pp, k):
        rows = pl.ds(pl.multiple_of((pp * 2 + k) * 256, 256), 256)
        g = dot(d2[rows, :], rscr[0], 1, 0)
        for h in range(2):
            glp[pp * 2 + k, h] = g[:, h * NS : (h + 1) * NS].astype(BF16)

    for pp in range(2):
        left_piece(pp, 1 - core)
        far(glp.at[pp * 2 + 1 - core], gls.at[pp], ss_gl.at[pp], rs_gs.at[pp], sibling).start()
    for pp in range(2):
        left_piece(pp, core)

    def update(t):
        here = pl.ds(pl.multiple_of(t * 256, 256), 256)
        a = dot(wturn[...], beo[:, here], 1, 0)
        for u in range(2):
            k = t * 2 + u
            o = (a[:, u * 128 : (u + 1) * 128] * inv[pl.ds(k, 1), :]).astype(BF16).T.astype(F32)
            inc_ref[k] = jnp.concatenate([o[m * 16 : m * 16 + 8] for m in range(8)], axis=0).astype(BF16)
            inc_ref[k + 16] = jnp.concatenate([o[m * 16 + 8 : m * 16 + 16] for m in range(8)], axis=0).astype(BF16)

    pl.loop(0, 4)(update)

    for pp in range(2):
        arrived(gls.at[pp], ss_gl.at[pp], rs_gs.at[pp])
        m = pp * 2 + core
        for h in range(2):
            glp[m, h] = (glp[m, h].astype(F32) + gls[pp, h].astype(F32)).astype(BF16)
            put(
                jnp.logical_and(2 * q + pp == z, q == h),
                glp.at[m, h],
                glown.at[z],
                ss_gl.at[2 + pp * 2 + h],
                rs_go.at[z],
                (r, 4 * q + m, h),
            )

    total = grsend[r, q].astype(F32)
    for t in range(1, 16):
        arrived(grrecv.at[t], ss_gr.at[t], rs_gr.at[t])
        total = total + grrecv[t].astype(F32)
    grt[...] = total.astype(BF16)
    put(diagonal, grt, grown, ss_gt.at[0], rs_gt.at[0], turned)

    pl.loop(4, 8)(update)
    save_inc.start()

    for m in range(8):
        arrived(dwrecv.at[m], ss_dw.at[m], rs_dw.at[m])
    total = dwrecv[0].astype(F32)
    for m in range(1, 8):
        total = total + dwrecv[m].astype(F32)
    e1[...] = total

    @pl.loop(1, 16)
    def _(t):
        m, dev = plane(t)
        far(e1.at[pl.ds(pl.multiple_of(m * 8, 8), 8), :], e1recv.at[t], ss_e1.at[t], rs_e1.at[t], dev).start()

    for m in range(4):
        arrived(glown.at[m], ss_gl.at[2], rs_go.at[m])
    arrived(grown, ss_gt.at[0], rs_gt.at[0])
    gl = glown[0].astype(F32)
    for m in range(1, 4):
        gl = gl + glown[m].astype(F32)
    tmp[...] = grown[...].astype(F32)
    fsum = jnp.zeros((128, NCH), F32)
    for k in range(NQ):
        g = jnp.concatenate([gl[k * NP : (k + 1) * NP], tmp[pl.ds(k, NP, stride=NQ), :]], axis=0)
        g = g * mine[k : k + 1, :]
        high = g.astype(BF16)
        rest = (g - high.astype(F32)).astype(BF16)
        g2 = jnp.concatenate([high, rest], axis=0)
        gown[k] = g2
        fsum = fsum + dot(g2, nres[k], 1, 0)
    fsum = fsum[:64] + fsum[64:]
    for m in range(8):
        fsend[m] = fsum[m * 8 : (m + 1) * 8]
    pltpu.make_async_copy(fsend.at[c], frecv.at[c], rs_f.at[c]).start()

    @pl.loop(1, 8)
    def _(t):
        m = lax.rem(c + t, 8)
        far(fsend.at[m], frecv.at[c], ss_f.at[t], rs_f.at[c], (r, m, q)).start()

    total = e1[pl.ds(pl.multiple_of(me * 8, 8), 8), :]
    for t in range(1, 16):
        arrived(e1recv.at[t], ss_e1.at[t], rs_e1.at[t])
        total = total + e1recv[t]
    e2[...] = total
    e3[pl.ds(pl.multiple_of(me * 8, 8), 8), :] = total

    @pl.loop(1, 16)
    def _(t):
        m, dev = plane(t)
        far(e2, e3.at[pl.ds(pl.multiple_of(me * 8, 8), 8), :], ss_e2.at[t], rs_e2.at[me], dev).start()

    w2x = jnp.concatenate([wt[...], wt[...]], axis=0)

    def adjoint(k):
        d = dot(gown[k], w2x, 0, 0)
        at = pl.ds(k, NS, stride=NQ)
        z = both_halves(xh, at)
        scale = rs[at, :]
        m1 = jnp.mean(d, axis=-1, keepdims=True)
        m2 = jnp.mean(d * z, axis=-1, keepdims=True)
        o = d - m1 - z * m2
        oscr[0, at, :] = scale * o[:, :128]
        oscr[1, at, :] = scale * o[:, 128:]

    for k in range(0, 3):
        adjoint(k)

    for m in range(8):
        arrived(frecv.at[m], ss_f.at[m], rs_f.at[m])
    total = frecv[0]
    for m in range(1, 8):
        total = total + frecv[m]
    f1[...] = total
    pltpu.make_async_copy(f1, f1recv.at[me], rs_f1.at[me]).start()

    @pl.loop(1, 16)
    def _(t):
        m = lax.rem(me + t, 16)
        far(f1, f1recv.at[me], ss_f1.at[t], rs_f1.at[me], (m // 2, c, lax.rem(m, 2))).start()

    for m in range(16):

        @pl.when(me != m)
        def _(m=m):
            arrived(e3.at[m * 8 : (m + 1) * 8, :], ss_e2.at[m], rs_e2.at[m])

    chunk = dwo_ref.at[pl.ds(pl.multiple_of(c * 128, 128), 128), :]
    pltpu.make_async_copy(e3, chunk, rs_e3.at[c]).start()
    far(e3, chunk, ss_e3.at[0], rs_e3.at[c], sibling).start()

    @pl.loop(1, 4)
    def _(t):
        far(e3, chunk, ss_e3.at[t], rs_e3.at[c], (r, lax.rem(z + t, 4) * 2 + core, q)).start()

    for k in range(3, 5):
        adjoint(k)

    for m in range(16):
        arrived(f1recv.at[m], ss_f1.at[m], rs_f1.at[m])
    total = f1recv[0]
    for m in range(1, 16):
        total = total + f1recv[m]
    f2[...] = total
    pltpu.make_async_copy(f2, f2recv.at[c], rs_f2.at[c]).start()

    @pl.loop(1, 8)
    def _(t):
        far(f2, f2recv.at[c], ss_f2.at[t], rs_f2.at[c], (r, lax.rem(c + t, 8), q)).start()

    for k in range(5, 8):
        adjoint(k)

    @pl.loop(0, 8)
    def _(t):
        aadj_ref[pl.ds(t * 16, 16)] = both_halves(oscr, pl.ds(t * 128, 128)).reshape(16, NQ, NCH).astype(BF16)

    for m in range(8):
        arrived(f2recv.at[m], ss_f2.at[m], rs_f2.at[m])
    fa_ref[...] = jnp.concatenate([f2recv[m] for m in range(4)], axis=0)
    sa_ref[...] = jnp.concatenate([f2recv[m] for m in range(4, 8)], axis=0)
    for t in range(1, 4):
        m = lax.rem(z + t, 4) * 2 + core
        chunk = dwo_ref.at[pl.ds(pl.multiple_of(m * 128, 128), 128), :]
        arrived(chunk, ss_e3.at[0], rs_e3.at[m])
        far(chunk, chunk, ss_e3.at[3 + t], rs_e3.at[m], sibling).start()

    for t in range(4):
        m = lax.rem(z + t, 4) * 2 + 1 - core
        arrived(dwo_ref.at[pl.ds(pl.multiple_of(m * 128, 128), 128), :], ss_e3.at[0], rs_e3.at[m])
    arrived(e3, ss_e3.at[0], rs_e3.at[c])
    save_inc.wait()

    @pl.when(inner)
    def _():
        @pl.loop(1, 8)
        def _(t):
            sent(msend, ss_mr.at[t], rs_mr.at[0])

    for t in range(1, 8):
        sent(lsend, ss_l.at[t], rs_l.at[0, 0])
    for t in range(1, 7):
        sent(rsend, ss_r.at[t], rs_r.at[0, 0, 0])
    for t in range(7, 25):
        sent(rsend.at[0:128, :], ss_r.at[t], rs_r.at[0, 0, 0])
    for t in range(2):
        sent(gls.at[0], ss_gl.at[t], rs_gs.at[0])
    for pp in range(2):
        for h in range(2):

            @pl.when(jnp.logical_not(jnp.logical_and(2 * q + pp == z, q == h)))
            def _(pp=pp, h=h):
                sent(lsend, ss_gl.at[2 + pp * 2 + h], rs_go.at[0])

    @pl.when(jnp.logical_not(inner))
    def _():
        sent(lsend, ss_l.at[0], rs_l.at[0, 0])

    for t in range(7):
        sent(e3, ss_e3.at[t], rs_e3.at[0])

    @pl.loop(1, 8)
    def _(t):
        sent(msend, ss_mc.at[t], rs_mc.at[0])
        sent(dwsend.at[0], ss_dw.at[t], rs_dw.at[0])
        sent(fsend.at[0], ss_f.at[t], rs_f.at[0])
        sent(f2, ss_f2.at[t], rs_f2.at[0])

    @pl.loop(1, 16)
    def _(t):
        sent(rsend, ss_gr.at[t], rs_gr.at[0])
        sent(f1, ss_f1.at[t], rs_f1.at[0])
        sent(e2, ss_e2.at[t], rs_e2.at[0])
        sent(e2, ss_e1.at[t], rs_e1.at[0])

    @pl.when(jnp.logical_not(diagonal))
    def _():
        sent(msend, ss_mc.at[0], rs_mc.at[0])
        sent(rsend, ss_r.at[0], rs_r.at[0, 0, 0])
        sent(grt, ss_gt.at[0], rs_gt.at[0])


def hand_over(*refs):
    into = [pltpu.make_async_copy(refs[i], refs[10 + i], refs[15].at[i]) for i in range(5)]
    out = [pltpu.make_async_copy(refs[10 + i], refs[5 + i], refs[16].at[i]) for i in range(5)]
    for copy in into:
        copy.start()
    for i in range(5):
        into[i].wait()
        out[i].start()
    for copy in out:
        copy.wait()


def local(x, occ, w1, w2, wo, cot):
    vmem = pl.BlockSpec(memory_space=pltpu.VMEM)
    hbm = pl.BlockSpec(memory_space=pl.ANY)
    dma = pltpu.SemaphoreType.DMA
    scratch = [
        pltpu.VMEM((1024, NZ), BF16),
        pltpu.VMEM((32, 64, NZ), BF16),
        pltpu.VMEM((32, 64, NZ), BF16),
        pltpu.VMEM((16, NS), BF16),
        pltpu.VMEM((4, 16, NS), BF16),
        pltpu.VMEM((8, 16, NS), BF16),
        pltpu.VMEM((2, 1024, 128), F32),
        pltpu.VMEM((1024, 128), F32),
        pltpu.VMEM((NQ, NS, NCH), BF16),
        pltpu.VMEM((256, NS), F32),
        pltpu.VMEM((256, NS), BF16),
        pltpu.VMEM((256, NS), BF16),
        pltpu.VMEM((4, 2, 256, NS), BF16),
        pltpu.VMEM((2, 8, 256, NS), BF16),
        pltpu.VMEM((64, NCH), BF16),
        pltpu.VMEM((1024, NZ), BF16),
        pltpu.VMEM((1024, NZ), F32),
        pltpu.VMEM((16, 128), F32),
        pltpu.VMEM((2, PAIRS, NZ), BF16),
        pltpu.VMEM((1024, PAIRS), BF16),
        pltpu.VMEM((1024, 256), BF16),
        pltpu.VMEM((256, 1024), BF16),
        pltpu.VMEM((NZ, 1024), BF16),
        pltpu.VMEM((2, PAIRS, 256), BF16),
        pltpu.VMEM((1024, PAIRS), BF16),
        pltpu.VMEM((8, 2, 256, NS), BF16),
        pltpu.VMEM((16, 256, NS), BF16),
        pltpu.VMEM((256, NS), BF16),
        pltpu.VMEM((256, NS), BF16),
        pltpu.VMEM((4, 2, 256, NS), BF16),
        pltpu.VMEM((2, 2, 256, NS), BF16),
        pltpu.VMEM((4, 256, NS), BF16),
        pltpu.VMEM((1024, NZ), F32),
        pltpu.VMEM((8, 128, NZ), BF16),
        pltpu.VMEM((8, 128, NZ), BF16),
        pltpu.VMEM((8, 8, NCH), F32),
        pltpu.VMEM((8, 8, NCH), F32),
        pltpu.VMEM((8, NCH), F32),
        pltpu.VMEM((16, 8, NCH), F32),
        pltpu.VMEM((8, NCH), F32),
        pltpu.VMEM((8, 8, NCH), F32),
        pltpu.VMEM((128, NZ), F32),
        pltpu.VMEM((16, 8, NZ), F32),
        pltpu.VMEM((8, NZ), F32),
        pltpu.VMEM((128, NZ), F32),
        pltpu.VMEM((NQ, 128, NS), BF16),
        pltpu.VMEM((2, 1024, 128), F32),
        dma((3,)),
        dma((8,)),
        dma((4,)),
        dma((8,)),
        dma((8,)),
        dma((8,)),
        dma((2, 2)),
        dma((2, 2)),
        dma((25,)),
        dma((2, 8, 2)),
        dma((6,)),
        dma((2,)),
        dma((4,)),
        dma((16,)),
        dma((16,)),
        dma((1,)),
        dma((1,)),
        dma((8,)),
        dma((8,)),
        dma((8,)),
        dma((8,)),
        dma((16,)),
        dma((16,)),
        dma((8,)),
        dma((8,)),
        dma((16,)),
        dma((16,)),
        dma((16,)),
        dma((16,)),
        dma((8,)),
        dma((8,)),
    ]
    inc, aadj, fa, sa, dwo = pl.pallas_call(
        kernel,
        out_shape=(
            jax.ShapeDtypeStruct((32, 64, NZ), BF16),
            jax.ShapeDtypeStruct((NS, NQ, NCH), BF16),
            jax.ShapeDtypeStruct((NP, NCH), F32),
            jax.ShapeDtypeStruct((NP, NCH), F32),
            jax.ShapeDtypeStruct((1024, NZ), F32),
        ),
        in_specs=[vmem] * 4 + [hbm] * 2,
        out_specs=(hbm,) + (vmem,) * 4,
        scratch_shapes=scratch,
        compiler_params=pltpu.CompilerParams(vmem_limit_bytes=56 * 1024 * 1024, has_side_effects=True, collective_id=0),
    )(x, occ.T, w1.T, w2.T, wo, cot)
    outs = (inc, aadj, fa, sa, dwo)
    inc, aadj, fa, sa, dwo = pl.pallas_call(
        hand_over,
        out_shape=tuple(jax.ShapeDtypeStruct(o.shape, o.dtype) for o in outs),
        in_specs=[hbm] * 5,
        out_specs=(hbm,) * 5,
        scratch_shapes=[pltpu.VMEM(o.shape, o.dtype) for o in outs] + [dma((5,)), dma((5,))],
        compiler_params=pltpu.CompilerParams(vmem_limit_bytes=56 * 1024 * 1024),
    )(*outs)
    return inc, aadj, fa.T, sa.T, dwo


def solution(mesh):
    placed = (
        P("seq", ("row", "col"), None),
        P(None, ("row", "col")),
        P(),
        P(),
        P(),
        P(("row", "seq"), "col", None),
    )
    return jax.shard_map(
        local,
        mesh=mesh,
        in_specs=placed,
        out_specs=(P(("row", "seq"), "col", None), P("seq", ("row", "col"), None), P(), P(), P()),
        check_vma=False,
    )
```

time: 81.9 us -> 70.5 us (0.86)
  Pallas kernels: 76.2 us -> 69.7 us
  local copies, waits for them, and re-layouts: 4.91 us -> 0 us
    pallas_call x1, Pallas kernels: 76.2 us -> 67.4 us  [local(): pl.pallas_call(kernel, out_shape=(jax.ShapeDtypeStruct((32, 64, NZ), BF16...]
    unnamed x13 -> x0, local copies, waits for them, and re-layouts: 4.91 us -> none
    pallas_call x0 -> x1, Pallas kernels: none -> 2.29 us  [local(): pl.pallas_call(hand_over, out_shape=tuple((jax.ShapeDtypeStruct(o.shape,...]
where the time goes in v3:
time: 70.5 us; the launch traced here: 70.4 us
  Pallas kernels  69.7 us (99%)
    pallas_call x1, Pallas kernels, local(): pl.pallas_call(kernel, out_shape=(jax.ShapeDtypeStruct((32, 64, NZ), BF16...  67.4 us
    pallas_call x1, Pallas kernels, local(): pl.pallas_call(hand_over, out_shape=tuple((jax.ShapeDtypeStruct(o.shape,...  2.29 us

profile of v3, /device:TPU:1, one launch (start us, length us, event | category | flops | bytes accessed | tf_op | source)
XLA Modules:
  0.0 70.4 jit_solution(17729768991540111030)
XLA Ops:
  0.6 67.4 %shard_map.101 = (bf16[32,64,128]{2,1,0:T(8,128)(2,1)}, bf16[128,8,256]{2,1,0:T(8,128)(2,1)}, f32[32,256]{1,0:T(8,128)}, f32[32,256]{1,0:T(8,128)}, f32[1024,128]{1,0:T(8,128)}) custom-call(bf16[128,8,256]{2,1,0:T(8,128)(2,1)} %x_ref.1, s32[8,256]{1,0:T(8,128)} %bitcast.7, bf16[32,256]{1,0:T(8,128)(2,1)} %bitcast.5, bf16[32,256]{1,0:T(8,128)(2,1)} %bitcast.6, ...), custom_call_target="tpu_custom_call" | custom-call | tf_op jit(solution)/shard_map/pallas_call | solution.py:761
  68.1 2.3 %shard_map.102 = (bf16[32,64,128]{2,1,0:T(8,128)(2,1)}, bf16[128,8,256]{2,1,0:T(8,128)(2,1)}, f32[32,256]{1,0:T(8,128)}, f32[32,256]{1,0:T(8,128)}, f32[1024,128]{1,0:T(8,128)}) custom-call(bf16[32,64,128]{2,1,0:T(8,128)(2,1)} %get-tuple-element.15.refs_0_, bf16[128,8,256]{2,1,0:T(8,128)(2,1)} %get-tuple-element.16.refs_1_, ...), custom_call_target="tpu_custom_call" | custom-call | tf_op jit(solution)/shard_map/pallas_call | solution.py:776

commit v4 on v3

--- a/solution.py
+++ b/solution.py
@@ -27,20 +27,25 @@
 
 
 def kernel(
+    x_hbm,
+    occ_hbm,
+    w1_hbm,
+    w2_hbm,
+    wo_hbm,
+    cot_hbm,
+    inc_hbm,
+    aadj_hbm,
+    fa_ref,
+    sa_ref,
+    dwo_ref,
     x_ref,
     occ_ref,
     w1_ref,
     w2_ref,
-    wo_hbm,
-    cot_hbm,
-    inc_hbm,
-    aadj_ref,
-    fa_ref,
-    sa_ref,
-    dwo_ref,
     wo_ref,
     cot_ref,
     inc_ref,
+    aadj_ref,
     msend,
     mrow,
     mcol,
@@ -56,6 +61,8 @@
     wsplit,
     wide,
     inv,
+    over_lanes,
+    dpre,
     s12,
     d2,
     lscr,
@@ -64,7 +71,9 @@
     rscr,
     beo,
     grsend,
-    grrecv,
+    gra,
+    grb,
+    grc,
     grt,
     grown,
     glp,
@@ -123,7 +132,21 @@
     me = r * 2 + q
     core, z = lax.rem(c, 2), c // 2
     sibling = (r, c + 1 - 2 * core, q)
-    turned = (c, r, q)
+    holder = (
+        lax.rem(r // 4 + core, 2) * 4 + lax.rem(lax.rem(r, 4) + 2 - z + r // 2 + 4, 4),
+        r,
+        q,
+    )
+
+    def held(m):
+        dz = lax.rem(2 - lax.rem(m, 4) + lax.rem(c, 4) + 4, 4)
+        return lax.rem(c // 2 + dz, 4) * 2 + lax.rem(m // 4 + c // 4, 2)
+
+    def holder_row(m):
+        dz = lax.rem(m // 2 - c // 2 + 4, 4)
+        return lax.rem(c // 4 + lax.rem(m, 2), 2) * 4 + lax.rem(lax.rem(c, 4) + 2 - dz + 4, 4)
+
+    owner = (c, held(r), q)
     other = (r, lax.rem(c + 1, 8), q)
 
     def plane(t):
@@ -157,8 +180,13 @@
     load_wo = pltpu.make_async_copy(wo_hbm, wo_ref, io_sem.at[0])
     load_cot = pltpu.make_async_copy(cot_hbm, cot_ref, io_sem.at[1])
     save_inc = pltpu.make_async_copy(inc_ref, inc_hbm, io_sem.at[2])
-    load_wo.start()
-    load_cot.start()
+    save_aadj = pltpu.make_async_copy(aadj_ref, aadj_hbm, io_sem.at[7])
+    load_x = pltpu.make_async_copy(x_hbm, x_ref, io_sem.at[3])
+    load_occ = pltpu.make_async_copy(occ_hbm, occ_ref, io_sem.at[4])
+    load_w1 = pltpu.make_async_copy(w1_hbm, w1_ref, io_sem.at[5])
+    load_w2 = pltpu.make_async_copy(w2_hbm, w2_ref, io_sem.at[6])
+    for load in (load_x, load_occ, load_w1, load_w2, load_wo, load_cot):
+        load.start()
 
     barrier = pltpu.get_barrier_semaphore()
 
@@ -206,14 +234,19 @@
         pl.semaphore_signal(barrier, inc=1, device_id=mask_to(t), device_id_type=MESH)
         pl.semaphore_signal(barrier, inc=1, device_id=mask_from(t), device_id_type=MESH)
 
+    for dev in (holder, owner):
+        pl.semaphore_signal(barrier, inc=1, device_id=dev, device_id_type=MESH)
+
     @pl.when(jnp.logical_not(diagonal))
     def _():
-        for dev in (mask_to(0), mask_from(0), turned):
+        for dev in (mask_to(0), mask_from(0)):
             pl.semaphore_signal(barrier, inc=1, device_id=dev, device_id_type=MESH)
 
+    load_occ.wait()
     occ = occ_ref[...].astype(F32)
     msend[...] = jnp.concatenate([occ[:, :NS], occ[:, NS:]], axis=0).astype(BF16)
 
+    load_x.wait()
     @pl.loop(0, 8)
     def _(t):
         xb = x_ref[pl.ds(t * 16, 16)].astype(F32).reshape(128, NCH)
@@ -224,7 +257,7 @@
         xh[1, pl.ds(t * 128, 128), :] = z[:, 128:]
         rs[pl.ds(t * 128, 128), :] = jnp.broadcast_to(rstd, (128, 128))
 
-    pl.semaphore_wait(barrier, jnp.where(diagonal, 39, 42))
+    pl.semaphore_wait(barrier, jnp.where(diagonal, 41, 43))
     put(diagonal, msend, mcol.at[c], ss_mc.at[0], rs_mc.at[c], mask_to(0))
 
     @pl.loop(1, 8)
@@ -240,6 +273,8 @@
         def _(t):
             far(msend, mrow.at[m], ss_mr.at[t], rs_mr.at[m], line(t)[1]).start()
 
+    load_w1.wait()
+    load_w2.wait()
     wt[0:NP, :] = w1_ref[...]
     wt[NP:, :] = w2_ref[...]
     mine = msend[...].astype(F32)
@@ -271,7 +306,7 @@
     def _():
         far(lsend, lrecv.at[lax.rem(c, 4), q], ss_l.at[0], rs_l.at[lax.rem(c, 4) // 2, q], across).start()
 
-    put(diagonal, rsend, rrecv.at[q, c], ss_r.at[0], rs_r.at[q, c, 0], turned)
+    far(rsend, rrecv.at[q, holder[0]], ss_r.at[0], rs_r.at[q, holder[0], 0], holder).start()
 
     load_wo.wait()
     wide[...] = wo_ref[...].astype(F32)
@@ -280,46 +315,17 @@
 
     wturn[...] = wsplit[...].T
 
-    @pl.when(jnp.logical_not(inner))
-    def _():
-        arrived(given, ss_l.at[0], given_mark)
-        left_along()
-
-    came, mark = block(0, 0, 0, 256)
-    arrived(came, ss_r.at[0], mark)
-    for t in range(1, 4):
-        far(came, came, ss_r.at[t], mark, along_x(t)).start()
-        far(came, came, ss_r.at[3 + t], mark, along_y(t)).start()
-
-    for m in range(4):
-        arrived(mrow.at[m], ss_mr.at[m], rs_mr.at[m])
-    for m in range(8):
-        arrived(mcol.at[m], ss_mc.at[m], rs_mc.at[m])
-
-    count = jnp.zeros((64, 32), F32)
-    across_lo = jnp.zeros((16, 128), F32)
-    across_hi = jnp.zeros((16, 128), F32)
-    for h in range(2):
-        rows = jnp.concatenate([mrow[m].astype(F32)[h * NQ : (h + 1) * NQ] for m in range(4)], axis=0).astype(BF16)
-        groups = [mcol[m].astype(F32)[h * NQ : (h + 1) * NQ] for m in range(8)]
-        cols = jnp.concatenate(groups, axis=0).astype(BF16)
-        twice = jnp.concatenate([g for g in groups for _ in range(2)], axis=0).astype(BF16)
-        count = count + dot(cols, rows, 1, 1)
-        across_lo = across_lo + dot(rows[:16], twice, 1, 1)
-        across_hi = across_hi + dot(rows[16:], twice, 1, 1)
     lane = lax.broadcasted_iota(jnp.int32, (NP, 128), 1)
     low = lax.rem(lane // 8, 2) == 0
-    inv[...] = 1.0 / (jnp.where(low[:16], across_lo, across_hi) + 0.001)
-    over = 1.0 / (count + 0.001)
+
+    def in_turn(lo, hi):
+        return jnp.concatenate([v[m * 8 : m * 8 + 8] for m in range(8) for v in (lo, hi)], axis=0).astype(BF16)
+
     load_cot.wait()
     for k in range(16):
-        lo, hi = [
-            cot_ref[i].astype(F32) * jnp.broadcast_to(over[:, i : i + 1], (64, NZ)) for i in (k, k + 16)
-        ]
-        pairs = [(lo[m * 8 : m * 8 + 8], hi[m * 8 : m * 8 + 8]) for m in range(8)]
-        here = slice(k * 128, (k + 1) * 128)
-        s12[0, here, :] = jnp.concatenate([g for a, b in pairs for g in (a, b)], axis=0).astype(BF16)
-        s12[1, here, :] = jnp.concatenate([g for a, b in pairs for g in (b, a)], axis=0).astype(BF16)
+        lo, hi = cot_ref[k].astype(F32), cot_ref[k + 16].astype(F32)
+        s12[0, k * 128 : (k + 1) * 128, :] = in_turn(lo, hi)
+        s12[1, k * 128 : (k + 1) * 128, :] = in_turn(hi, lo)
 
     def outer_adjoint(t):
         here = pl.ds(pl.multiple_of(t * 256, 256), 256)
@@ -335,9 +341,44 @@
                 for p in range(16):
                     va = a[p * NP : (p + 1) * NP, u * 128 : (u + 1) * 128]
                     vb = b[p * NP : (p + 1) * NP, u * 128 : (u + 1) * 128]
-                    d2[at, p * 128 : (p + 1) * 128] = jnp.where(low, va, vb).astype(BF16)
+                    dpre[at, p * 128 : (p + 1) * 128] = jnp.where(low, va, vb)
 
     pl.loop(0, 4)(outer_adjoint)
+
+    @pl.when(jnp.logical_not(inner))
+    def _():
+        arrived(given, ss_l.at[0], given_mark)
+        left_along()
+
+    came, mark = block(0, 0, 0, 256)
+    arrived(came, ss_r.at[0], mark)
+    for t in range(1, 4):
+        far(came, came, ss_r.at[t], mark, along_x(t)).start()
+        far(came, came, ss_r.at[3 + t], mark, along_y(t)).start()
+
+    pl.loop(4, 8)(outer_adjoint)
+
+    for m in range(4):
+        arrived(mrow.at[m], ss_mr.at[m], rs_mr.at[m])
+    for m in range(8):
+        arrived(mcol.at[m], ss_mc.at[m], rs_mc.at[m])
+
+    count = jnp.zeros((64, 32), F32)
+    count_lanes = jnp.zeros((32, 128), F32)
+    for h in range(2):
+        rows = jnp.concatenate([mrow[m].astype(F32)[h * NQ : (h + 1) * NQ] for m in range(4)], axis=0).astype(BF16)
+        groups = [mcol[m].astype(F32)[h * NQ : (h + 1) * NQ] for m in range(8)]
+        cols = jnp.concatenate(groups, axis=0).astype(BF16)
+        twice = jnp.concatenate([g for g in groups for _ in range(2)], axis=0).astype(BF16)
+        count = count + dot(cols, rows, 1, 1)
+        count_lanes = count_lanes + dot(rows, twice, 1, 1)
+    over_lanes[...] = 1.0 / (count_lanes + 0.001)
+    inv[...] = jnp.where(low[:16], over_lanes[:16], over_lanes[16:])
+
+    @pl.loop(0, 32)
+    def _(i):
+        rows = pl.ds(pl.multiple_of(i * NP, NP), NP)
+        d2[rows, :] = (dpre[rows, :] * jnp.concatenate([over_lanes[pl.ds(i, 1), :]] * 16, axis=1)).astype(BF16)
 
     for t in range(1, 4):
         zt = lax.rem(z + t, 4)
@@ -360,8 +401,6 @@
         for u in range(1, 4):
             far(half, half, ss_r.at[12 + t * 3 + u], mark, along_x(u)).start()
 
-    pl.loop(4, 8)(outer_adjoint)
-
     for pp in range(2):
         for h in range(2):
             arrived(lrecv.at[pp * 2 + 1 - core, h], ss_l.at[0], rs_ls.at[pp, h])
@@ -379,12 +418,21 @@
             for h in range(2):
                 gt = a[h * NS : (h + 1) * NS, u * 128 : (u + 1) * 128].T
                 for m in range(8):
-                    grsend[m, h, at, :] = gt[m * 16 : (m + 1) * 16]
-
-    @pl.loop(1, 16)
-    def _(t):
-        m, dev = plane(t)
-        far(grsend.at[m // 2, lax.rem(m, 2)], grrecv.at[t], ss_gr.at[t], rs_gr.at[t], dev).start()
+                    row = holder_row(m)
+                    grsend[h * 2 + row // 4, lax.rem(row, 4), at, :] = gt[m * 16 : (m + 1) * 16]
+
+    for t in range(1, 4):
+        y, x = lax.rem(y0 + t, 4), lax.rem(x0 + t, 4)
+        far(grsend.at[y, :, 0:128, :], gra.at[0, t], ss_gr.at[t], rs_gr.at[0, t], along_y(t)).start()
+        far(grsend.at[:, x, 128:256, :], gra.at[1, t], ss_gr.at[3 + t], rs_gr.at[1, t], along_x(t)).start()
+
+    over = 1.0 / (count + 0.001)
+    for k in range(16):
+        lo, hi = [
+            cot_ref[i].astype(F32) * jnp.broadcast_to(over[:, i : i + 1], (64, NZ)) for i in (k, k + 16)
+        ]
+        s12[0, k * 128 : (k + 1) * 128, :] = in_turn(lo, hi)
+        s12[1, k * 128 : (k + 1) * 128, :] = in_turn(hi, lo)
 
     for t in range(1, 4):
         for u in range(1, 4):
@@ -398,7 +446,7 @@
         for h in range(2):
             lanes = slice(h * NS, (h + 1) * NS)
             for m in range(8):
-                at = pl.ds(pl.multiple_of(p * 128 + m * 16, 16), 16)
+                at = pl.ds(pl.multiple_of(p * 128 + held(m) * 16, 16), 16)
                 v = rrecv[h, m, rows, :]
                 w = v.astype(F32)
                 rscr[0, at, lanes] = v
@@ -406,26 +454,41 @@
 
     def outer_product(t):
         here = pl.ds(pl.multiple_of(t * 256, 256), 256)
-        a = dot(lscr[...], rscr[0, here, :], 1, 1)
-        b = dot(lscr[...], rscr[1, here, :], 1, 1)
+        a = dot(lscr[:HALF], rscr[0, here, :], 1, 1)
+        b = dot(lscr[HALF:], rscr[1, here, :], 1, 1)
         for u in range(2):
             lanes = slice(u * 128, (u + 1) * 128)
             even = pl.ds(pl.multiple_of((t * 2 + u) * NP, NP), NP)
             odd = pl.ds(pl.multiple_of(HALF + (t * 2 + u) * NP, NP), NP)
             for k in range(16):
-                lo = slice(k * NP, (k + 1) * NP)
-                hi = slice(HALF + k * NP, HALF + (k + 1) * NP)
-                beo[even, k * 128 : (k + 1) * 128] = jnp.where(low, a[lo, lanes], b[hi, lanes]).astype(BF16)
-                beo[odd, k * 128 : (k + 1) * 128] = jnp.where(low, b[lo, lanes], a[hi, lanes]).astype(BF16)
+                lo = a[k * NP : (k + 1) * NP, lanes]
+                hi = b[k * NP : (k + 1) * NP, lanes]
+                beo[even, k * 128 : (k + 1) * 128] = jnp.where(low, lo, hi).astype(BF16)
+                beo[odd, k * 128 : (k + 1) * 128] = jnp.where(low, hi, lo).astype(BF16)
 
     pl.loop(0, 4)(outer_product)
 
     pl.loop(4, 8)(outer_product)
 
-    part = dot(beo[...], s12[0], 1, 0)
+    for i in range(2):
+        for t in range(1, 4):
+            arrived(gra.at[i, t], ss_gr.at[1], rs_gr.at[i, t])
+        for n in range(4):
+            own = grsend[n, x0, 128:256, :] if i else grsend[y0, n, 0:128, :]
+            total = own.astype(F32)
+            for t in range(1, 4):
+                total = total + gra[i, t, n].astype(F32)
+            grb[i, n] = total.astype(BF16)
+        for t in range(1, 4):
+            if i:
+                far(grb.at[i, lax.rem(y0 + t, 4)], grc.at[i, t], ss_gr.at[9 + t], rs_gr.at[2 + i, t], along_y(t)).start()
+            else:
+                far(grb.at[i, lax.rem(x0 + t, 4)], grc.at[i, t], ss_gr.at[6 + t], rs_gr.at[2 + i, t], along_x(t)).start()
+
     for h in range(2):
+        part = dot(beo[h * HALF : (h + 1) * HALF], s12[h], 1, 0)
         for p in range(16):
-            dwf[pl.ds(2 * p + h, NP, stride=NP), :] = part[h * HALF + p * NP : h * HALF + (p + 1) * NP]
+            dwf[pl.ds(2 * p + h, NP, stride=NP), :] = part[p * NP : (p + 1) * NP]
     for m in range(8):
         dwsend[m] = dwf[m * 128 : (m + 1) * 128, :].astype(BF16)
     pltpu.make_async_copy(dwsend.at[c], dwrecv.at[c], rs_dw.at[c]).start()
@@ -446,17 +509,6 @@
         far(glp.at[pp * 2 + 1 - core], gls.at[pp], ss_gl.at[pp], rs_gs.at[pp], sibling).start()
     for pp in range(2):
         left_piece(pp, core)
-
-    def update(t):
-        here = pl.ds(pl.multiple_of(t * 256, 256), 256)
-        a = dot(wturn[...], beo[:, here], 1, 0)
-        for u in range(2):
-            k = t * 2 + u
-            o = (a[:, u * 128 : (u + 1) * 128] * inv[pl.ds(k, 1), :]).astype(BF16).T.astype(F32)
-            inc_ref[k] = jnp.concatenate([o[m * 16 : m * 16 + 8] for m in range(8)], axis=0).astype(BF16)
-            inc_ref[k + 16] = jnp.concatenate([o[m * 16 + 8 : m * 16 + 16] for m in range(8)], axis=0).astype(BF16)
-
-    pl.loop(0, 4)(update)
 
     for pp in range(2):
         arrived(gls.at[pp], ss_gl.at[pp], rs_gs.at[pp])
@@ -472,15 +524,30 @@
                 (r, 4 * q + m, h),
             )
 
-    total = grsend[r, q].astype(F32)
-    for t in range(1, 16):
-        arrived(grrecv.at[t], ss_gr.at[t], rs_gr.at[t])
-        total = total + grrecv[t].astype(F32)
-    grt[...] = total.astype(BF16)
-    put(diagonal, grt, grown, ss_gt.at[0], rs_gt.at[0], turned)
-
-    pl.loop(4, 8)(update)
-    save_inc.start()
+    for i in range(2):
+        own = grb[i, y0] if i else grb[i, x0]
+        total = own.astype(F32)
+        for t in range(1, 4):
+            arrived(grc.at[i, t], ss_gr.at[7], rs_gr.at[2 + i, t])
+            total = total + grc[i, t].astype(F32)
+        grt[i * 128 : (i + 1) * 128, :] = total.astype(BF16)
+    far(grt, grown, ss_gt.at[0], rs_gt.at[0], owner).start()
+
+    low_rows = lax.rem(lax.broadcasted_iota(jnp.int32, (NZ, 128), 1) // 8, 2) == 0
+
+    def update(t):
+        here = pl.ds(pl.multiple_of(t * 256, 256), 256)
+        a = dot(wturn[:, :HALF], beo[:HALF, here], 1, 0)
+        b = dot(wturn[:, HALF:], beo[HALF:, here], 1, 0)
+        for u in range(2):
+            k = t * 2 + u
+            odd = b[:, u * 128 : (u + 1) * 128]
+            odd = jnp.where(low_rows, pltpu.roll(odd, 120, 1), pltpu.roll(odd, 8, 1))
+            o = ((a[:, u * 128 : (u + 1) * 128] + odd) * inv[pl.ds(k, 1), :]).astype(BF16).T.astype(F32)
+            inc_ref[k] = jnp.concatenate([o[m * 16 : m * 16 + 8] for m in range(8)], axis=0).astype(BF16)
+            inc_ref[k + 16] = jnp.concatenate([o[m * 16 + 8 : m * 16 + 16] for m in range(8)], axis=0).astype(BF16)
+
+    pl.loop(0, 4)(update)
 
     for m in range(8):
         arrived(dwrecv.at[m], ss_dw.at[m], rs_dw.at[m])
@@ -493,6 +560,9 @@
     def _(t):
         m, dev = plane(t)
         far(e1.at[pl.ds(pl.multiple_of(m * 8, 8), 8), :], e1recv.at[t], ss_e1.at[t], rs_e1.at[t], dev).start()
+
+    pl.loop(4, 8)(update)
+    save_inc.start()
 
     for m in range(4):
         arrived(glown.at[m], ss_gl.at[2], rs_go.at[m])
@@ -520,18 +590,6 @@
         m = lax.rem(c + t, 8)
         far(fsend.at[m], frecv.at[c], ss_f.at[t], rs_f.at[c], (r, m, q)).start()
 
-    total = e1[pl.ds(pl.multiple_of(me * 8, 8), 8), :]
-    for t in range(1, 16):
-        arrived(e1recv.at[t], ss_e1.at[t], rs_e1.at[t])
-        total = total + e1recv[t]
-    e2[...] = total
-    e3[pl.ds(pl.multiple_of(me * 8, 8), 8), :] = total
-
-    @pl.loop(1, 16)
-    def _(t):
-        m, dev = plane(t)
-        far(e2, e3.at[pl.ds(pl.multiple_of(me * 8, 8), 8), :], ss_e2.at[t], rs_e2.at[me], dev).start()
-
     w2x = jnp.concatenate([wt[...], wt[...]], axis=0)
 
     def adjoint(k):
@@ -545,8 +603,26 @@
         oscr[0, at, :] = scale * o[:, :128]
         oscr[1, at, :] = scale * o[:, 128:]
 
-    for k in range(0, 3):
+    for k in range(NQ):
         adjoint(k)
+
+    @pl.loop(0, 8)
+    def _(t):
+        aadj_ref[pl.ds(t * 16, 16)] = both_halves(oscr, pl.ds(t * 128, 128)).reshape(16, NQ, NCH).astype(BF16)
+
+    save_aadj.start()
+
+    total = e1[pl.ds(pl.multiple_of(me * 8, 8), 8), :]
+    for t in range(1, 16):
+        arrived(e1recv.at[t], ss_e1.at[t], rs_e1.at[t])
+        total = total + e1recv[t]
+    e2[...] = total
+    e3[pl.ds(pl.multiple_of(me * 8, 8), 8), :] = total
+
+    @pl.loop(1, 16)
+    def _(t):
+        m, dev = plane(t)
+        far(e2, e3.at[pl.ds(pl.multiple_of(me * 8, 8), 8), :], ss_e2.at[t], rs_e2.at[me], dev).start()
 
     for m in range(8):
         arrived(frecv.at[m], ss_f.at[m], rs_f.at[m])
@@ -575,9 +651,6 @@
     def _(t):
         far(e3, chunk, ss_e3.at[t], rs_e3.at[c], (r, lax.rem(z + t, 4) * 2 + core, q)).start()
 
-    for k in range(3, 5):
-        adjoint(k)
-
     for m in range(16):
         arrived(f1recv.at[m], ss_f1.at[m], rs_f1.at[m])
     total = f1recv[0]
@@ -590,28 +663,22 @@
     def _(t):
         far(f2, f2recv.at[c], ss_f2.at[t], rs_f2.at[c], (r, lax.rem(c + t, 8), q)).start()
 
-    for k in range(5, 8):
-        adjoint(k)
-
-    @pl.loop(0, 8)
-    def _(t):
-        aadj_ref[pl.ds(t * 16, 16)] = both_halves(oscr, pl.ds(t * 128, 128)).reshape(16, NQ, NCH).astype(BF16)
-
-    for m in range(8):
-        arrived(f2recv.at[m], ss_f2.at[m], rs_f2.at[m])
-    fa_ref[...] = jnp.concatenate([f2recv[m] for m in range(4)], axis=0)
-    sa_ref[...] = jnp.concatenate([f2recv[m] for m in range(4, 8)], axis=0)
     for t in range(1, 4):
         m = lax.rem(z + t, 4) * 2 + core
         chunk = dwo_ref.at[pl.ds(pl.multiple_of(m * 128, 128), 128), :]
         arrived(chunk, ss_e3.at[0], rs_e3.at[m])
         far(chunk, chunk, ss_e3.at[3 + t], rs_e3.at[m], sibling).start()
 
+    for m in range(8):
+        arrived(f2recv.at[m], ss_f2.at[m], rs_f2.at[m])
+    fa_ref[...] = jnp.concatenate([f2recv[m] for m in range(4)], axis=0)
+    sa_ref[...] = jnp.concatenate([f2recv[m] for m in range(4, 8)], axis=0)
     for t in range(4):
         m = lax.rem(z + t, 4) * 2 + 1 - core
         arrived(dwo_ref.at[pl.ds(pl.multiple_of(m * 128, 128), 128), :], ss_e3.at[0], rs_e3.at[m])
     arrived(e3, ss_e3.at[0], rs_e3.at[c])
     save_inc.wait()
+    save_aadj.wait()
 
     @pl.when(inner)
     def _():
@@ -650,7 +717,6 @@
 
     @pl.loop(1, 16)
     def _(t):
-        sent(rsend, ss_gr.at[t], rs_gr.at[0])
         sent(f1, ss_f1.at[t], rs_f1.at[0])
         sent(e2, ss_e2.at[t], rs_e2.at[0])
         sent(e2, ss_e1.at[t], rs_e1.at[0])
@@ -658,8 +724,13 @@
     @pl.when(jnp.logical_not(diagonal))
     def _():
         sent(msend, ss_mc.at[0], rs_mc.at[0])
-        sent(rsend, ss_r.at[0], rs_r.at[0, 0, 0])
-        sent(grt, ss_gt.at[0], rs_gt.at[0])
+
+    sent(rsend, ss_r.at[0], rs_r.at[0, 0, 0])
+    sent(grt, ss_gt.at[0], rs_gt.at[0])
+    for t in range(1, 7):
+        sent(gra.at[0, 1], ss_gr.at[t], rs_gr.at[0, 1])
+    for t in range(7, 13):
+        sent(grc.at[0, 1], ss_gr.at[t], rs_gr.at[0, 1])
 
 
 def hand_over(*refs):
@@ -679,9 +750,14 @@
     hbm = pl.BlockSpec(memory_space=pl.ANY)
     dma = pltpu.SemaphoreType.DMA
     scratch = [
+        pltpu.VMEM((NS, NQ, NCH), BF16),
+        pltpu.VMEM((NQ, 2 * NS), jnp.int32),
+        pltpu.VMEM((NP, NCH), BF16),
+        pltpu.VMEM((NP, NCH), BF16),
         pltpu.VMEM((1024, NZ), BF16),
         pltpu.VMEM((32, 64, NZ), BF16),
         pltpu.VMEM((32, 64, NZ), BF16),
+        pltpu.VMEM((NS, NQ, NCH), BF16),
         pltpu.VMEM((16, NS), BF16),
         pltpu.VMEM((4, 16, NS), BF16),
         pltpu.VMEM((8, 16, NS), BF16),
@@ -697,6 +773,8 @@
         pltpu.VMEM((1024, NZ), BF16),
         pltpu.VMEM((1024, NZ), F32),
         pltpu.VMEM((16, 128), F32),
+        pltpu.VMEM((32, 128), F32),
+        pltpu.VMEM((1024, PAIRS), F32),
         pltpu.VMEM((2, PAIRS, NZ), BF16),
         pltpu.VMEM((1024, PAIRS), BF16),
         pltpu.VMEM((1024, 256), BF16),
@@ -704,8 +782,10 @@
         pltpu.VMEM((NZ, 1024), BF16),
         pltpu.VMEM((2, PAIRS, 256), BF16),
         pltpu.VMEM((1024, PAIRS), BF16),
-        pltpu.VMEM((8, 2, 256, NS), BF16),
-        pltpu.VMEM((16, 256, NS), BF16),
+        pltpu.VMEM((4, 4, 256, NS), BF16),
+        pltpu.VMEM((2, 4, 4, 128, NS), BF16),
+        pltpu.VMEM((2, 4, 128, NS), BF16),
+        pltpu.VMEM((2, 4, 128, NS), BF16),
         pltpu.VMEM((256, NS), BF16),
         pltpu.VMEM((256, NS), BF16),
         pltpu.VMEM((4, 2, 256, NS), BF16),
@@ -726,7 +806,7 @@
         pltpu.VMEM((128, NZ), F32),
         pltpu.VMEM((NQ, 128, NS), BF16),
         pltpu.VMEM((2, 1024, 128), F32),
-        dma((3,)),
+        dma((8,)),
         dma((8,)),
         dma((4,)),
         dma((8,)),
@@ -739,8 +819,8 @@
         dma((6,)),
         dma((2,)),
         dma((4,)),
-        dma((16,)),
-        dma((16,)),
+        dma((13,)),
+        dma((4, 4)),
         dma((1,)),
         dma((1,)),
         dma((8,)),
@@ -767,10 +847,10 @@
             jax.ShapeDtypeStruct((NP, NCH), F32),
             jax.ShapeDtypeStruct((1024, NZ), F32),
         ),
-        in_specs=[vmem] * 4 + [hbm] * 2,
-        out_specs=(hbm,) + (vmem,) * 4,
+        in_specs=[hbm] * 6,
+        out_specs=(hbm, hbm, vmem, vmem, vmem),
         scratch_shapes=scratch,
-        compiler_params=pltpu.CompilerParams(vmem_limit_bytes=56 * 1024 * 1024, has_side_effects=True, collective_id=0),
+        compiler_params=pltpu.CompilerParams(vmem_limit_bytes=60 * 1024 * 1024, has_side_effects=True, collective_id=0),
     )(x, occ.T, w1.T, w2.T, wo, cot)
     outs = (inc, aadj, fa, sa, dwo)
     inc, aadj, fa, sa, dwo = pl.pallas_call(
@@ -779,7 +859,7 @@
         in_specs=[hbm] * 5,
         out_specs=(hbm,) * 5,
         scratch_shapes=[pltpu.VMEM(o.shape, o.dtype) for o in outs] + [dma((5,)), dma((5,))],
-        compiler_params=pltpu.CompilerParams(vmem_limit_bytes=56 * 1024 * 1024),
+        compiler_params=pltpu.CompilerParams(vmem_limit_bytes=60 * 1024 * 1024),
     )(*outs)
     return inc, aadj, fa.T, sa.T, dwo
 

time: 70.5 us -> 66.7 us (0.946)
  Pallas kernels: 69.7 us -> 65.9 us
    pallas_call x1, Pallas kernels: 67.4 us -> 63.6 us  [local(): pl.pallas_call(kernel, out_shape=(jax.ShapeDtypeStruct((32, 64, NZ), BF16...]
where the time goes in v4:
time: 66.7 us; the launch traced here: 66.6 us
  Pallas kernels  65.9 us (99%)
    pallas_call x1, Pallas kernels, local(): pl.pallas_call(kernel, out_shape=(jax.ShapeDtypeStruct((32, 64, NZ), BF16...  63.6 us
    pallas_call x1, Pallas kernels, local(): pl.pallas_call(hand_over, out_shape=tuple((jax.ShapeDtypeStruct(o.shape,...  2.29 us

profile of v4, /device:TPU:1, one launch (start us, length us, event | category | flops | bytes accessed | tf_op | source)
XLA Modules:
  0.0 66.6 jit_solution(1138952618033943700)
XLA Ops:
  0.6 63.6 %shard_map.101 = (bf16[32,64,128]{2,1,0:T(8,128)(2,1)}, bf16[128,8,256]{2,1,0:T(8,128)(2,1)}, f32[32,256]{1,0:T(8,128)}, f32[32,256]{1,0:T(8,128)}, f32[1024,128]{1,0:T(8,128)}) custom-call(bf16[128,8,256]{2,1,0:T(8,128)(2,1)} %x_hbm.1, s32[8,256]{1,0:T(8,128)} %bitcast.7, bf16[32,256]{1,0:T(8,128)(2,1)} %bitcast.5, bf16[32,256]{1,0:T(8,128)(2,1)} %bitcast.6, ...), custom_call_target="tpu_custom_call" | custom-call | tf_op jit(solution)/shard_map/pallas_call | solution.py:841
  64.3 2.3 %shard_map.102 = (bf16[32,64,128]{2,1,0:T(8,128)(2,1)}, bf16[128,8,256]{2,1,0:T(8,128)(2,1)}, f32[32,256]{1,0:T(8,128)}, f32[32,256]{1,0:T(8,128)}, f32[1024,128]{1,0:T(8,128)}) custom-call(bf16[32,64,128]{2,1,0:T(8,128)(2,1)} %get-tuple-element.15.refs_0_, bf16[128,8,256]{2,1,0:T(8,128)(2,1)} %get-tuple-element.16.refs_1_, ...), custom_call_target="tpu_custom_call" | custom-call | tf_op jit(solution)/shard_map/pallas_call | solution.py:856

commit v5 on v4

--- a/solution.py
+++ b/solution.py
@@ -35,9 +35,9 @@
     cot_hbm,
     inc_hbm,
     aadj_hbm,
-    fa_ref,
-    sa_ref,
-    dwo_ref,
+    fa_hbm,
+    sa_hbm,
+    dwo_hbm,
     x_ref,
     occ_ref,
     w1_ref,
@@ -46,6 +46,9 @@
     cot_ref,
     inc_ref,
     aadj_ref,
+    fa_ref,
+    sa_ref,
+    dwo_ref,
     msend,
     mrow,
     mcol,
@@ -95,35 +98,22 @@
     gown,
     oscr,
     io_sem,
-    ss_mr,
+    ss,
     rs_mr,
-    ss_mc,
     rs_mc,
-    ss_l,
     rs_l,
     rs_ls,
-    ss_r,
     rs_r,
-    ss_gl,
     rs_gs,
     rs_go,
-    ss_gr,
     rs_gr,
-    ss_gt,
     rs_gt,
-    ss_dw,
     rs_dw,
-    ss_f,
     rs_f,
-    ss_f1,
     rs_f1,
-    ss_f2,
     rs_f2,
-    ss_e1,
     rs_e1,
-    ss_e2,
     rs_e2,
-    ss_e3,
     rs_e3,
 ):
     r, c, q = lax.axis_index("row"), lax.axis_index("col"), lax.axis_index("seq")
@@ -171,16 +161,23 @@
         def _():
             far(src, dst, ssem, rsem, dev).start()
 
-    def arrived(slot, ssem, rsem):
-        far(slot, slot, ssem, rsem, other).wait_recv()
-
-    def sent(slot, ssem, rsem):
-        far(slot, slot, ssem, rsem, other).wait_send()
+    def arrived(size, mark):
+        far(size, size, ss.at[0], mark, other).wait_recv()
+
+    def sent(size, step):
+        far(size, size, ss.at[step], rs_r.at[0], other).wait_send()
 
     load_wo = pltpu.make_async_copy(wo_hbm, wo_ref, io_sem.at[0])
     load_cot = pltpu.make_async_copy(cot_hbm, cot_ref, io_sem.at[1])
+    save_fa = pltpu.make_async_copy(fa_ref, fa_hbm, io_sem.at[16])
+    save_sa = pltpu.make_async_copy(sa_ref, sa_hbm, io_sem.at[17])
     save_inc = pltpu.make_async_copy(inc_ref, inc_hbm, io_sem.at[2])
     save_aadj = pltpu.make_async_copy(aadj_ref, aadj_hbm, io_sem.at[7])
+
+    def save_chunk(m):
+        rows = pl.ds(pl.multiple_of(m * 128, 128), 128)
+        return pltpu.make_async_copy(dwo_ref.at[rows, :], dwo_hbm.at[rows, :], io_sem.at[8 + m])
+
     load_x = pltpu.make_async_copy(x_hbm, x_ref, io_sem.at[3])
     load_occ = pltpu.make_async_copy(occ_hbm, occ_ref, io_sem.at[4])
     load_w1 = pltpu.make_async_copy(w1_hbm, w1_ref, io_sem.at[5])
@@ -190,6 +187,17 @@
 
     barrier = pltpu.get_barrier_semaphore()
 
+    def mask_to(t):
+        return (lax.rem(r + t, 8), r, q)
+
+    def mask_from(t):
+        return (c, lax.rem(c + t, 8), q)
+
+    @pl.loop(1, 8)
+    def _(t):
+        pl.semaphore_signal(barrier, inc=1, device_id=mask_to(t), device_id_type=MESH)
+        pl.semaphore_signal(barrier, inc=1, device_id=mask_from(t), device_id_type=MESH)
+
     @pl.loop(1, 16)
     def _(t):
         pl.semaphore_signal(barrier, inc=1, device_id=plane(t)[1], device_id_type=MESH)
@@ -216,23 +224,12 @@
     def block(dy, dx, first, last):
         y, x = lax.rem(y0 + dy, 4), lax.rem(x0 + dx, 4)
         h, m = y // 2, lax.rem(y, 2) * 4 + x
-        return rrecv.at[h, m, first:last, :], rs_r.at[h, m, first // 128]
-
-    def mask_to(t):
-        return (lax.rem(r + t, 8), r, q)
-
-    def mask_from(t):
-        return (c, lax.rem(c + t, 8), q)
+        return rrecv.at[h, m, first:last, :]
 
     @pl.loop(1, 4)
     def _(t):
         dev = (r, lax.rem(z + t, 4) * 2 + core, 1 - q)
         pl.semaphore_signal(barrier, inc=1, device_id=dev, device_id_type=MESH)
-
-    @pl.loop(1, 8)
-    def _(t):
-        pl.semaphore_signal(barrier, inc=1, device_id=mask_to(t), device_id_type=MESH)
-        pl.semaphore_signal(barrier, inc=1, device_id=mask_from(t), device_id_type=MESH)
 
     for dev in (holder, owner):
         pl.semaphore_signal(barrier, inc=1, device_id=dev, device_id_type=MESH)
@@ -256,22 +253,6 @@
         xh[0, pl.ds(t * 128, 128), :] = z[:, :128]
         xh[1, pl.ds(t * 128, 128), :] = z[:, 128:]
         rs[pl.ds(t * 128, 128), :] = jnp.broadcast_to(rstd, (128, 128))
-
-    pl.semaphore_wait(barrier, jnp.where(diagonal, 41, 43))
-    put(diagonal, msend, mcol.at[c], ss_mc.at[0], rs_mc.at[c], mask_to(0))
-
-    @pl.loop(1, 8)
-    def _(t):
-        far(msend, mcol.at[c], ss_mc.at[t], rs_mc.at[c], mask_to(t)).start()
-
-    @pl.when(inner)
-    def _():
-        m = lax.rem(c, 4)
-        pltpu.make_async_copy(msend, mrow.at[m], rs_mr.at[m]).start()
-
-        @pl.loop(1, 8)
-        def _(t):
-            far(msend, mrow.at[m], ss_mr.at[t], rs_mr.at[m], line(t)[1]).start()
 
     load_w1.wait()
     load_w2.wait()
@@ -287,6 +268,8 @@
         tmp[pl.ds(k, NP, stride=NQ), :] = p[NP:]
     rsend[...] = tmp[...].astype(BF16)
 
+    pl.semaphore_wait(barrier, jnp.where(diagonal, 41, 43))
+
     mine_of_line = lax.rem(jnp.where(inner, z, z + 3 - 2 * lax.rem(z, 2)), 2)
     seq_of_line = jnp.where(inner, q, 1 - q)
     given = lrecv.at[mine_of_line * 2 + core, seq_of_line]
@@ -294,8 +277,8 @@
 
     def left_along():
         for t in range(1, 4):
-            far(given, given, ss_l.at[t], given_mark, along_z(t)).start()
-        far(given, given, ss_l.at[4], rs_ls.at[mine_of_line, seq_of_line], sibling).start()
+            far(given, given, ss.at[2], given_mark, along_z(t)).start()
+        far(given, given, ss.at[2], rs_ls.at[0], sibling).start()
 
     @pl.when(inner)
     def _():
@@ -304,9 +287,24 @@
 
     @pl.when(jnp.logical_not(inner))
     def _():
-        far(lsend, lrecv.at[lax.rem(c, 4), q], ss_l.at[0], rs_l.at[lax.rem(c, 4) // 2, q], across).start()
-
-    far(rsend, rrecv.at[q, holder[0]], ss_r.at[0], rs_r.at[q, holder[0], 0], holder).start()
+        far(lsend, lrecv.at[lax.rem(c, 4), q], ss.at[2], rs_l.at[lax.rem(c, 4) // 2, q], across).start()
+
+    far(rsend, rrecv.at[q, holder[0]], ss.at[3], rs_r.at[0], holder).start()
+
+    put(diagonal, msend, mcol.at[c], ss.at[1], rs_mc.at[0], mask_to(0))
+
+    @pl.loop(1, 8)
+    def _(t):
+        far(msend, mcol.at[c], ss.at[1], rs_mc.at[0], mask_to(t)).start()
+
+    @pl.when(inner)
+    def _():
+        m = lax.rem(c, 4)
+        pltpu.make_async_copy(msend, mrow.at[m], rs_mr.at[0]).start()
+
+        @pl.loop(1, 8)
+        def _(t):
+            far(msend, mrow.at[m], ss.at[0], rs_mr.at[0], line(t)[1]).start()
 
     load_wo.wait()
     wide[...] = wo_ref[...].astype(F32)
@@ -347,21 +345,19 @@
 
     @pl.when(jnp.logical_not(inner))
     def _():
-        arrived(given, ss_l.at[0], given_mark)
+        arrived(given, given_mark)
         left_along()
 
-    came, mark = block(0, 0, 0, 256)
-    arrived(came, ss_r.at[0], mark)
+    came = block(0, 0, 0, 256)
+    arrived(came, rs_r.at[0])
     for t in range(1, 4):
-        far(came, came, ss_r.at[t], mark, along_x(t)).start()
-        far(came, came, ss_r.at[3 + t], mark, along_y(t)).start()
+        far(came, came, ss.at[3], rs_r.at[4 - t], along_x(t)).start()
+        far(came, came, ss.at[3], rs_r.at[7 - t], along_y(t)).start()
 
     pl.loop(4, 8)(outer_adjoint)
 
-    for m in range(4):
-        arrived(mrow.at[m], ss_mr.at[m], rs_mr.at[m])
-    for m in range(8):
-        arrived(mcol.at[m], ss_mc.at[m], rs_mc.at[m])
+    arrived(mrow, rs_mr.at[0])
+    arrived(mcol, rs_mc.at[0])
 
     count = jnp.zeros((64, 32), F32)
     count_lanes = jnp.zeros((32, 128), F32)
@@ -386,31 +382,43 @@
         pp = lax.rem(jnp.where(in_half, zt, zt + 3 - 2 * lax.rem(zt, 2)), 2)
         h = jnp.where(in_half, q, 1 - q)
         slot = lrecv.at[pp * 2 + core, h]
-        arrived(slot, ss_l.at[0], rs_l.at[pp, h])
-        far(slot, slot, ss_l.at[4 + t], rs_ls.at[pp, h], sibling).start()
+        arrived(slot, rs_l.at[pp, h])
+        far(slot, slot, ss.at[2], rs_ls.at[0], sibling).start()
 
     for t in range(1, 4):
-        whole, mark = block(0, t, 0, 256)
-        arrived(whole, ss_r.at[0], mark)
-        half, mark = block(0, t, 0, 128)
+        arrived(block(0, t, 0, 256), rs_r.at[t])
+        half = block(0, t, 0, 128)
         for u in range(1, 4):
-            far(half, half, ss_r.at[3 + t * 3 + u], mark, along_y(u)).start()
-        whole, mark = block(t, 0, 0, 256)
-        arrived(whole, ss_r.at[0], mark)
-        half, mark = block(t, 0, 128, 256)
+            far(half, half, ss.at[3], rs_r.at[7], along_y(u)).start()
+        arrived(block(t, 0, 0, 256), rs_r.at[3 + t])
+        half = block(t, 0, 128, 256)
         for u in range(1, 4):
-            far(half, half, ss_r.at[12 + t * 3 + u], mark, along_x(u)).start()
-
-    for pp in range(2):
-        for h in range(2):
-            arrived(lrecv.at[pp * 2 + 1 - core, h], ss_l.at[0], rs_ls.at[pp, h])
+            far(half, half, ss.at[3], rs_r.at[7], along_x(u)).start()
+
+    def put_right(dy, dx):
+        y, x = lax.rem(y0 + dy, 4), lax.rem(x0 + dx, 4)
+        h, m = y // 2, lax.rem(y, 2) * 4 + x
+        lanes = pl.ds(pl.multiple_of(h * NS, NS), NS)
+        first = held(m) * 16
+        for p in range(16):
+            at = pl.ds(pl.multiple_of(p * 128 + first, 16), 16)
+            v = rrecv[h, m, p * 16 : (p + 1) * 16, :]
+            w = v.astype(F32)
+            rscr[0, at, lanes] = v
+            rscr[1, at, lanes] = jnp.concatenate([w[8:], w[:8]], axis=0).astype(BF16)
+
+    put_right(0, 0)
+    for t in range(1, 4):
+        put_right(0, t)
+        put_right(t, 0)
+
+    arrived(lrecv.at[0:2], rs_ls.at[0])
     for h in range(2):
         for m in range(4):
             lscr[m * 256 : (m + 1) * 256, h * NS : (h + 1) * NS] = lrecv[m, h]
             lturn[h * NS : (h + 1) * NS, m * 256 : (m + 1) * 256] = lrecv[m, h].T
 
-    @pl.loop(0, 8)
-    def _(t):
+    def right_part(t):
         here = pl.ds(pl.multiple_of(t * 256, 256), 256)
         a = dot(lturn[...], d2[:, here], 1, 0).astype(BF16)
         for u in range(2):
@@ -421,10 +429,14 @@
                     row = holder_row(m)
                     grsend[h * 2 + row // 4, lax.rem(row, 4), at, :] = gt[m * 16 : (m + 1) * 16]
 
-    for t in range(1, 4):
-        y, x = lax.rem(y0 + t, 4), lax.rem(x0 + t, 4)
-        far(grsend.at[y, :, 0:128, :], gra.at[0, t], ss_gr.at[t], rs_gr.at[0, t], along_y(t)).start()
-        far(grsend.at[:, x, 128:256, :], gra.at[1, t], ss_gr.at[3 + t], rs_gr.at[1, t], along_x(t)).start()
+    for n in range(4):
+        pl.loop(2 * n, 2 * n + 2)(right_part)
+        rows = slice(n * 64, (n + 1) * 64)
+        for t in range(1, 4):
+            y, x = lax.rem(y0 + t, 4), lax.rem(x0 + t, 4)
+            part = grsend.at[:, x, rows, :] if n % 2 else grsend.at[y, :, rows, :]
+            to = along_x(t) if n % 2 else along_y(t)
+            far(part, gra.at[n, t], ss.at[5], rs_gr.at[n], to).start()
 
     over = 1.0 / (count + 0.001)
     for k in range(16):
@@ -434,23 +446,10 @@
         s12[0, k * 128 : (k + 1) * 128, :] = in_turn(lo, hi)
         s12[1, k * 128 : (k + 1) * 128, :] = in_turn(hi, lo)
 
+    arrived(grsend.at[0:3, 0:3], rs_r.at[7])
     for t in range(1, 4):
         for u in range(1, 4):
-            for first in (0, 128):
-                half, mark = block(t, u, first, first + 128)
-                arrived(half, ss_r.at[0], mark)
-
-    @pl.loop(0, 16)
-    def _(p):
-        rows = pl.ds(pl.multiple_of(p * 16, 16), 16)
-        for h in range(2):
-            lanes = slice(h * NS, (h + 1) * NS)
-            for m in range(8):
-                at = pl.ds(pl.multiple_of(p * 128 + held(m) * 16, 16), 16)
-                v = rrecv[h, m, rows, :]
-                w = v.astype(F32)
-                rscr[0, at, lanes] = v
-                rscr[1, at, lanes] = jnp.concatenate([w[8:], w[:8]], axis=0).astype(BF16)
+            put_right(t, u)
 
     def outer_product(t):
         here = pl.ds(pl.multiple_of(t * 256, 256), 256)
@@ -470,33 +469,35 @@
 
     pl.loop(4, 8)(outer_product)
 
-    for i in range(2):
-        for t in range(1, 4):
-            arrived(gra.at[i, t], ss_gr.at[1], rs_gr.at[i, t])
-        for n in range(4):
-            own = grsend[n, x0, 128:256, :] if i else grsend[y0, n, 0:128, :]
-            total = own.astype(F32)
-            for t in range(1, 4):
-                total = total + gra[i, t, n].astype(F32)
-            grb[i, n] = total.astype(BF16)
-        for t in range(1, 4):
-            if i:
-                far(grb.at[i, lax.rem(y0 + t, 4)], grc.at[i, t], ss_gr.at[9 + t], rs_gr.at[2 + i, t], along_y(t)).start()
-            else:
-                far(grb.at[i, lax.rem(x0 + t, 4)], grc.at[i, t], ss_gr.at[6 + t], rs_gr.at[2 + i, t], along_x(t)).start()
-
     for h in range(2):
         part = dot(beo[h * HALF : (h + 1) * HALF], s12[h], 1, 0)
         for p in range(16):
             dwf[pl.ds(2 * p + h, NP, stride=NP), :] = part[p * NP : (p + 1) * NP]
     for m in range(8):
         dwsend[m] = dwf[m * 128 : (m + 1) * 128, :].astype(BF16)
-    pltpu.make_async_copy(dwsend.at[c], dwrecv.at[c], rs_dw.at[c]).start()
+    pltpu.make_async_copy(dwsend.at[c], dwrecv.at[c], rs_dw.at[0]).start()
 
     @pl.loop(1, 8)
     def _(t):
         m = lax.rem(c + t, 8)
-        far(dwsend.at[m], dwrecv.at[c], ss_dw.at[t], rs_dw.at[c], (r, m, q)).start()
+        far(dwsend.at[m], dwrecv.at[c], ss.at[8], rs_dw.at[0], (r, m, q)).start()
+
+    for i in range(2):
+        for half in range(2):
+            part = 2 * half + i
+            rows = slice(part * 64, (part + 1) * 64)
+            arrived(gra.at[part, 1:4], rs_gr.at[part])
+            for n in range(4):
+                own = grsend[n, x0, rows, :] if i else grsend[y0, n, rows, :]
+                total = own.astype(F32)
+                for t in range(1, 4):
+                    total = total + gra[part, t, n].astype(F32)
+                grb[i, n, half] = total.astype(BF16)
+        for t in range(1, 4):
+            if i:
+                far(grb.at[i, lax.rem(y0 + t, 4)], grc.at[i, t], ss.at[6], rs_gr.at[4 + i], along_y(t)).start()
+            else:
+                far(grb.at[i, lax.rem(x0 + t, 4)], grc.at[i, t], ss.at[6], rs_gr.at[4 + i], along_x(t)).start()
 
     def left_piece(pp, k):
         rows = pl.ds(pl.multiple_of((pp * 2 + k) * 256, 256), 256)
@@ -506,12 +507,12 @@
 
     for pp in range(2):
         left_piece(pp, 1 - core)
-        far(glp.at[pp * 2 + 1 - core], gls.at[pp], ss_gl.at[pp], rs_gs.at[pp], sibling).start()
+        far(glp.at[pp * 2 + 1 - core], gls.at[pp], ss.at[4], rs_gs.at[pp], sibling).start()
     for pp in range(2):
         left_piece(pp, core)
 
     for pp in range(2):
-        arrived(gls.at[pp], ss_gl.at[pp], rs_gs.at[pp])
+        arrived(gls.at[pp], rs_gs.at[pp])
         m = pp * 2 + core
         for h in range(2):
             glp[m, h] = (glp[m, h].astype(F32) + gls[pp, h].astype(F32)).astype(BF16)
@@ -519,19 +520,10 @@
                 jnp.logical_and(2 * q + pp == z, q == h),
                 glp.at[m, h],
                 glown.at[z],
-                ss_gl.at[2 + pp * 2 + h],
-                rs_go.at[z],
+                ss.at[4],
+                rs_go.at[0],
                 (r, 4 * q + m, h),
             )
-
-    for i in range(2):
-        own = grb[i, y0] if i else grb[i, x0]
-        total = own.astype(F32)
-        for t in range(1, 4):
-            arrived(grc.at[i, t], ss_gr.at[7], rs_gr.at[2 + i, t])
-            total = total + grc[i, t].astype(F32)
-        grt[i * 128 : (i + 1) * 128, :] = total.astype(BF16)
-    far(grt, grown, ss_gt.at[0], rs_gt.at[0], owner).start()
 
     low_rows = lax.rem(lax.broadcasted_iota(jnp.int32, (NZ, 128), 1) // 8, 2) == 0
 
@@ -549,8 +541,18 @@
 
     pl.loop(0, 4)(update)
 
-    for m in range(8):
-        arrived(dwrecv.at[m], ss_dw.at[m], rs_dw.at[m])
+    for i in range(2):
+        own = grb[i, y0] if i else grb[i, x0]
+        total = own.astype(F32)
+        arrived(grc.at[i, 1:4], rs_gr.at[4 + i])
+        for t in range(1, 4):
+            total = total + grc[i, t].astype(F32)
+        for half in range(2):
+            part = 2 * half + i
+            grt[part * 64 : (part + 1) * 64, :] = total[half].astype(BF16)
+    far(grt, grown, ss.at[7], rs_gt.at[0], owner).start()
+
+    arrived(dwrecv, rs_dw.at[0])
     total = dwrecv[0].astype(F32)
     for m in range(1, 8):
         total = total + dwrecv[m].astype(F32)
@@ -559,14 +561,13 @@
     @pl.loop(1, 16)
     def _(t):
         m, dev = plane(t)
-        far(e1.at[pl.ds(pl.multiple_of(m * 8, 8), 8), :], e1recv.at[t], ss_e1.at[t], rs_e1.at[t], dev).start()
+        far(e1.at[pl.ds(pl.multiple_of(m * 8, 8), 8), :], e1recv.at[t], ss.at[12], rs_e1.at[0], dev).start()
 
     pl.loop(4, 8)(update)
     save_inc.start()
 
-    for m in range(4):
-        arrived(glown.at[m], ss_gl.at[2], rs_go.at[m])
-    arrived(grown, ss_gt.at[0], rs_gt.at[0])
+    arrived(glown, rs_go.at[0])
+    arrived(grown, rs_gt.at[0])
     gl = glown[0].astype(F32)
     for m in range(1, 4):
         gl = gl + glown[m].astype(F32)
@@ -583,12 +584,24 @@
     fsum = fsum[:64] + fsum[64:]
     for m in range(8):
         fsend[m] = fsum[m * 8 : (m + 1) * 8]
-    pltpu.make_async_copy(fsend.at[c], frecv.at[c], rs_f.at[c]).start()
+    pltpu.make_async_copy(fsend.at[c], frecv.at[c], rs_f.at[0]).start()
 
     @pl.loop(1, 8)
     def _(t):
         m = lax.rem(c + t, 8)
-        far(fsend.at[m], frecv.at[c], ss_f.at[t], rs_f.at[c], (r, m, q)).start()
+        far(fsend.at[m], frecv.at[c], ss.at[9], rs_f.at[0], (r, m, q)).start()
+
+    arrived(e1recv.at[1:16], rs_e1.at[0])
+    total = e1[pl.ds(pl.multiple_of(me * 8, 8), 8), :]
+    for t in range(1, 16):
+        total = total + e1recv[t]
+    e2[...] = total
+    pltpu.make_async_copy(e2, e3.at[pl.ds(pl.multiple_of(me * 8, 8), 8), :], rs_e2.at[0]).start()
+
+    @pl.loop(1, 16)
+    def _(t):
+        m, dev = plane(t)
+        far(e2, e3.at[pl.ds(pl.multiple_of(me * 8, 8), 8), :], ss.at[13], rs_e2.at[0], dev).start()
 
     w2x = jnp.concatenate([wt[...], wt[...]], axis=0)
 
@@ -612,125 +625,92 @@
 
     save_aadj.start()
 
-    total = e1[pl.ds(pl.multiple_of(me * 8, 8), 8), :]
-    for t in range(1, 16):
-        arrived(e1recv.at[t], ss_e1.at[t], rs_e1.at[t])
-        total = total + e1recv[t]
-    e2[...] = total
-    e3[pl.ds(pl.multiple_of(me * 8, 8), 8), :] = total
-
-    @pl.loop(1, 16)
-    def _(t):
-        m, dev = plane(t)
-        far(e2, e3.at[pl.ds(pl.multiple_of(me * 8, 8), 8), :], ss_e2.at[t], rs_e2.at[me], dev).start()
-
-    for m in range(8):
-        arrived(frecv.at[m], ss_f.at[m], rs_f.at[m])
+    arrived(frecv, rs_f.at[0])
     total = frecv[0]
     for m in range(1, 8):
         total = total + frecv[m]
     f1[...] = total
-    pltpu.make_async_copy(f1, f1recv.at[me], rs_f1.at[me]).start()
+    pltpu.make_async_copy(f1, f1recv.at[me], rs_f1.at[0]).start()
 
     @pl.loop(1, 16)
     def _(t):
         m = lax.rem(me + t, 16)
-        far(f1, f1recv.at[me], ss_f1.at[t], rs_f1.at[me], (m // 2, c, lax.rem(m, 2))).start()
-
-    for m in range(16):
-
-        @pl.when(me != m)
-        def _(m=m):
-            arrived(e3.at[m * 8 : (m + 1) * 8, :], ss_e2.at[m], rs_e2.at[m])
-
+        far(f1, f1recv.at[me], ss.at[10], rs_f1.at[0], (m // 2, c, lax.rem(m, 2))).start()
+
+    arrived(e3, rs_e2.at[0])
     chunk = dwo_ref.at[pl.ds(pl.multiple_of(c * 128, 128), 128), :]
-    pltpu.make_async_copy(e3, chunk, rs_e3.at[c]).start()
-    far(e3, chunk, ss_e3.at[0], rs_e3.at[c], sibling).start()
-
-    @pl.loop(1, 4)
-    def _(t):
-        far(e3, chunk, ss_e3.at[t], rs_e3.at[c], (r, lax.rem(z + t, 4) * 2 + core, q)).start()
-
-    for m in range(16):
-        arrived(f1recv.at[m], ss_f1.at[m], rs_f1.at[m])
+    dwo_ref[pl.ds(pl.multiple_of(c * 128, 128), 128), :] = e3[...]
+    save_chunk(c).start()
+    far(e3, chunk, ss.at[14], rs_e3.at[0], sibling).start()
+
+    for t in range(1, 4):
+        far(e3, chunk, ss.at[14], rs_e3.at[4 - t], (r, lax.rem(z + t, 4) * 2 + core, q)).start()
+
+    arrived(f1recv, rs_f1.at[0])
     total = f1recv[0]
     for m in range(1, 16):
         total = total + f1recv[m]
     f2[...] = total
-    pltpu.make_async_copy(f2, f2recv.at[c], rs_f2.at[c]).start()
+    pltpu.make_async_copy(f2, f2recv.at[c], rs_f2.at[0]).start()
 
     @pl.loop(1, 8)
     def _(t):
-        far(f2, f2recv.at[c], ss_f2.at[t], rs_f2.at[c], (r, lax.rem(c + t, 8), q)).start()
+        far(f2, f2recv.at[c], ss.at[11], rs_f2.at[0], (r, lax.rem(c + t, 8), q)).start()
 
     for t in range(1, 4):
         m = lax.rem(z + t, 4) * 2 + core
         chunk = dwo_ref.at[pl.ds(pl.multiple_of(m * 128, 128), 128), :]
-        arrived(chunk, ss_e3.at[0], rs_e3.at[m])
-        far(chunk, chunk, ss_e3.at[3 + t], rs_e3.at[m], sibling).start()
-
-    for m in range(8):
-        arrived(f2recv.at[m], ss_f2.at[m], rs_f2.at[m])
+        arrived(chunk, rs_e3.at[t])
+        save_chunk(m).start()
+        far(chunk, chunk, ss.at[14], rs_e3.at[0], sibling).start()
+
+    arrived(dwo_ref.at[0:512, :], rs_e3.at[0])
+    for t in range(4):
+        save_chunk(2 * t + 1 - core).start()
+
+    arrived(f2recv, rs_f2.at[0])
     fa_ref[...] = jnp.concatenate([f2recv[m] for m in range(4)], axis=0)
     sa_ref[...] = jnp.concatenate([f2recv[m] for m in range(4, 8)], axis=0)
-    for t in range(4):
-        m = lax.rem(z + t, 4) * 2 + 1 - core
-        arrived(dwo_ref.at[pl.ds(pl.multiple_of(m * 128, 128), 128), :], ss_e3.at[0], rs_e3.at[m])
-    arrived(e3, ss_e3.at[0], rs_e3.at[c])
+    save_fa.start()
+    save_sa.start()
+    for m in range(8):
+        save_chunk(m).wait()
     save_inc.wait()
     save_aadj.wait()
 
     @pl.when(inner)
     def _():
-        @pl.loop(1, 8)
-        def _(t):
-            sent(msend, ss_mr.at[t], rs_mr.at[0])
-
-    for t in range(1, 8):
-        sent(lsend, ss_l.at[t], rs_l.at[0, 0])
-    for t in range(1, 7):
-        sent(rsend, ss_r.at[t], rs_r.at[0, 0, 0])
-    for t in range(7, 25):
-        sent(rsend.at[0:128, :], ss_r.at[t], rs_r.at[0, 0, 0])
-    for t in range(2):
-        sent(gls.at[0], ss_gl.at[t], rs_gs.at[0])
-    for pp in range(2):
-        for h in range(2):
-
-            @pl.when(jnp.logical_not(jnp.logical_and(2 * q + pp == z, q == h)))
-            def _(pp=pp, h=h):
-                sent(lsend, ss_gl.at[2 + pp * 2 + h], rs_go.at[0])
+        sent(mcol.at[0:7], 0)
+        sent(rrecv.at[0, 0:7], 2)
+        sent(rrecv.at[0, 0:7], 4)
 
     @pl.when(jnp.logical_not(inner))
     def _():
-        sent(lsend, ss_l.at[0], rs_l.at[0, 0])
-
-    for t in range(7):
-        sent(e3, ss_e3.at[t], rs_e3.at[0])
-
-    @pl.loop(1, 8)
-    def _(t):
-        sent(msend, ss_mc.at[t], rs_mc.at[0])
-        sent(dwsend.at[0], ss_dw.at[t], rs_dw.at[0])
-        sent(fsend.at[0], ss_f.at[t], rs_f.at[0])
-        sent(f2, ss_f2.at[t], rs_f2.at[0])
-
-    @pl.loop(1, 16)
-    def _(t):
-        sent(f1, ss_f1.at[t], rs_f1.at[0])
-        sent(e2, ss_e2.at[t], rs_e2.at[0])
-        sent(e2, ss_e1.at[t], rs_e1.at[0])
+        sent(rrecv.at[0], 2)
+        sent(rrecv.at[0], 4)
+
+    @pl.when(diagonal)
+    def _():
+        sent(mcol.at[0:7], 1)
 
     @pl.when(jnp.logical_not(diagonal))
     def _():
-        sent(msend, ss_mc.at[0], rs_mc.at[0])
-
-    sent(rsend, ss_r.at[0], rs_r.at[0, 0, 0])
-    sent(grt, ss_gt.at[0], rs_gt.at[0])
-    for t in range(1, 7):
-        sent(gra.at[0, 1], ss_gr.at[t], rs_gr.at[0, 1])
-    for t in range(7, 13):
-        sent(grc.at[0, 1], ss_gr.at[t], rs_gr.at[0, 1])
+        sent(mcol, 1)
+
+    sent(rrecv, 3)
+    sent(gra.at[0:3], 5)
+    sent(gra.at[0, 0:3], 6)
+    sent(grt, 7)
+    sent(dwrecv.at[0:7], 8)
+    sent(frecv.at[0:7], 9)
+    sent(f1recv.at[0:15], 10)
+    sent(f2recv.at[0:7], 11)
+    sent(e1recv.at[0:15], 12)
+    sent(e1recv.at[0:15], 13)
+    sent(dwo_ref.at[0:896, :], 14)
+
+    save_fa.wait()
+    save_sa.wait()
 
 
 def hand_over(*refs):
@@ -746,7 +726,6 @@
 
 
 def local(x, occ, w1, w2, wo, cot):
-    vmem = pl.BlockSpec(memory_space=pltpu.VMEM)
     hbm = pl.BlockSpec(memory_space=pl.ANY)
     dma = pltpu.SemaphoreType.DMA
     scratch = [
@@ -758,6 +737,9 @@
         pltpu.VMEM((32, 64, NZ), BF16),
         pltpu.VMEM((32, 64, NZ), BF16),
         pltpu.VMEM((NS, NQ, NCH), BF16),
+        pltpu.VMEM((NP, NCH), F32),
+        pltpu.VMEM((NP, NCH), F32),
+        pltpu.VMEM((1024, NZ), F32),
         pltpu.VMEM((16, NS), BF16),
         pltpu.VMEM((4, 16, NS), BF16),
         pltpu.VMEM((8, 16, NS), BF16),
@@ -783,9 +765,9 @@
         pltpu.VMEM((2, PAIRS, 256), BF16),
         pltpu.VMEM((1024, PAIRS), BF16),
         pltpu.VMEM((4, 4, 256, NS), BF16),
-        pltpu.VMEM((2, 4, 4, 128, NS), BF16),
-        pltpu.VMEM((2, 4, 128, NS), BF16),
-        pltpu.VMEM((2, 4, 128, NS), BF16),
+        pltpu.VMEM((4, 4, 4, 64, NS), BF16),
+        pltpu.VMEM((2, 4, 2, 64, NS), BF16),
+        pltpu.VMEM((2, 4, 2, 64, NS), BF16),
         pltpu.VMEM((256, NS), BF16),
         pltpu.VMEM((256, NS), BF16),
         pltpu.VMEM((4, 2, 256, NS), BF16),
@@ -806,37 +788,24 @@
         pltpu.VMEM((128, NZ), F32),
         pltpu.VMEM((NQ, 128, NS), BF16),
         pltpu.VMEM((2, 1024, 128), F32),
+        dma((18,)),
+        dma((15,)),
+        dma((1,)),
+        dma((1,)),
+        dma((2, 2)),
+        dma((1,)),
         dma((8,)),
-        dma((8,)),
+        dma((2,)),
+        dma((1,)),
+        dma((6,)),
+        dma((1,)),
+        dma((1,)),
+        dma((1,)),
+        dma((1,)),
+        dma((1,)),
+        dma((1,)),
+        dma((1,)),
         dma((4,)),
-        dma((8,)),
-        dma((8,)),
-        dma((8,)),
-        dma((2, 2)),
-        dma((2, 2)),
-        dma((25,)),
-        dma((2, 8, 2)),
-        dma((6,)),
-        dma((2,)),
-        dma((4,)),
-        dma((13,)),
-        dma((4, 4)),
-        dma((1,)),
-        dma((1,)),
-        dma((8,)),
-        dma((8,)),
-        dma((8,)),
-        dma((8,)),
-        dma((16,)),
-        dma((16,)),
-        dma((8,)),
-        dma((8,)),
-        dma((16,)),
-        dma((16,)),
-        dma((16,)),
-        dma((16,)),
-        dma((8,)),
-        dma((8,)),
     ]
     inc, aadj, fa, sa, dwo = pl.pallas_call(
         kernel,
@@ -848,7 +817,7 @@
             jax.ShapeDtypeStruct((1024, NZ), F32),
         ),
         in_specs=[hbm] * 6,
-        out_specs=(hbm, hbm, vmem, vmem, vmem),
+        out_specs=(hbm,) * 5,
         scratch_shapes=scratch,
         compiler_params=pltpu.CompilerParams(vmem_limit_bytes=60 * 1024 * 1024, has_side_effects=True, collective_id=0),
     )(x, occ.T, w1.T, w2.T, wo, cot)

time: 66.7 us -> 61.7 us (0.925)
  Pallas kernels: 65.9 us -> 60.9 us
    pallas_call x1, Pallas kernels: 63.6 us -> 58.6 us  [local(): pl.pallas_call(kernel, out_shape=(jax.ShapeDtypeStruct((32, 64, NZ), BF16...]
where the time goes in v5:
time: 61.7 us; the launch traced here: 61.6 us
  Pallas kernels  60.9 us (99%)
  between operations  0.64 us (1%)
    pallas_call x1, Pallas kernels, local(): pl.pallas_call(kernel, out_shape=(jax.ShapeDtypeStruct((32, 64, NZ), BF16...  58.6 us
    pallas_call x1, Pallas kernels, local(): pl.pallas_call(hand_over, out_shape=tuple((jax.ShapeDtypeStruct(o.shape,...  2.29 us

profile of v5, /device:TPU:1, one launch (start us, length us, event | category | flops | bytes accessed | tf_op | source)
XLA Modules:
  0.0 61.6 jit_solution(6315429144975350922)
XLA Ops:
  0.6 58.6 %shard_map.101 = (bf16[32,64,128]{2,1,0:T(8,128)(2,1)}, bf16[128,8,256]{2,1,0:T(8,128)(2,1)}, f32[32,256]{1,0:T(8,128)}, f32[32,256]{1,0:T(8,128)}, f32[1024,128]{1,0:T(8,128)}) custom-call(bf16[128,8,256]{2,1,0:T(8,128)(2,1)} %x_hbm.1, s32[8,256]{1,0:T(8,128)} %bitcast.7, bf16[32,256]{1,0:T(8,128)(2,1)} %bitcast.5, bf16[32,256]{1,0:T(8,128)(2,1)} %bitcast.6, ...), custom_call_target="tpu_custom_call" | custom-call | tf_op jit(solution)/shard_map/pallas_call | solution.py:810
  59.3 2.3 %shard_map.102 = (bf16[32,64,128]{2,1,0:T(8,128)(2,1)}, bf16[128,8,256]{2,1,0:T(8,128)(2,1)}, f32[32,256]{1,0:T(8,128)}, f32[32,256]{1,0:T(8,128)}, f32[1024,128]{1,0:T(8,128)}) custom-call(bf16[32,64,128]{2,1,0:T(8,128)(2,1)} %get-tuple-element.15.refs_0_, bf16[128,8,256]{2,1,0:T(8,128)(2,1)} %get-tuple-element.16.refs_1_, ...), custom_call_target="tpu_custom_call" | custom-call | tf_op jit(solution)/shard_map/pallas_call | solution.py:825

commit v6 on v5

--- a/solution.py
+++ b/solution.py
@@ -33,22 +33,17 @@
     w2_hbm,
     wo_hbm,
     cot_hbm,
-    inc_hbm,
-    aadj_hbm,
-    fa_hbm,
-    sa_hbm,
-    dwo_hbm,
+    inc_ref,
+    aadj_ref,
+    fa_ref,
+    sa_ref,
+    dwo_ref,
     x_ref,
     occ_ref,
     w1_ref,
     w2_ref,
     wo_ref,
     cot_ref,
-    inc_ref,
-    aadj_ref,
-    fa_ref,
-    sa_ref,
-    dwo_ref,
     msend,
     mrow,
     mcol,
@@ -169,14 +164,6 @@
 
     load_wo = pltpu.make_async_copy(wo_hbm, wo_ref, io_sem.at[0])
     load_cot = pltpu.make_async_copy(cot_hbm, cot_ref, io_sem.at[1])
-    save_fa = pltpu.make_async_copy(fa_ref, fa_hbm, io_sem.at[16])
-    save_sa = pltpu.make_async_copy(sa_ref, sa_hbm, io_sem.at[17])
-    save_inc = pltpu.make_async_copy(inc_ref, inc_hbm, io_sem.at[2])
-    save_aadj = pltpu.make_async_copy(aadj_ref, aadj_hbm, io_sem.at[7])
-
-    def save_chunk(m):
-        rows = pl.ds(pl.multiple_of(m * 128, 128), 128)
-        return pltpu.make_async_copy(dwo_ref.at[rows, :], dwo_hbm.at[rows, :], io_sem.at[8 + m])
 
     load_x = pltpu.make_async_copy(x_hbm, x_ref, io_sem.at[3])
     load_occ = pltpu.make_async_copy(occ_hbm, occ_ref, io_sem.at[4])
@@ -564,7 +551,6 @@
         far(e1.at[pl.ds(pl.multiple_of(m * 8, 8), 8), :], e1recv.at[t], ss.at[12], rs_e1.at[0], dev).start()
 
     pl.loop(4, 8)(update)
-    save_inc.start()
 
     arrived(glown, rs_go.at[0])
     arrived(grown, rs_gt.at[0])
@@ -623,7 +609,6 @@
     def _(t):
         aadj_ref[pl.ds(t * 16, 16)] = both_halves(oscr, pl.ds(t * 128, 128)).reshape(16, NQ, NCH).astype(BF16)
 
-    save_aadj.start()
 
     arrived(frecv, rs_f.at[0])
     total = frecv[0]
@@ -640,7 +625,6 @@
     arrived(e3, rs_e2.at[0])
     chunk = dwo_ref.at[pl.ds(pl.multiple_of(c * 128, 128), 128), :]
     dwo_ref[pl.ds(pl.multiple_of(c * 128, 128), 128), :] = e3[...]
-    save_chunk(c).start()
     far(e3, chunk, ss.at[14], rs_e3.at[0], sibling).start()
 
     for t in range(1, 4):
@@ -661,22 +645,13 @@
         m = lax.rem(z + t, 4) * 2 + core
         chunk = dwo_ref.at[pl.ds(pl.multiple_of(m * 128, 128), 128), :]
         arrived(chunk, rs_e3.at[t])
-        save_chunk(m).start()
         far(chunk, chunk, ss.at[14], rs_e3.at[0], sibling).start()
 
     arrived(dwo_ref.at[0:512, :], rs_e3.at[0])
-    for t in range(4):
-        save_chunk(2 * t + 1 - core).start()
 
     arrived(f2recv, rs_f2.at[0])
     fa_ref[...] = jnp.concatenate([f2recv[m] for m in range(4)], axis=0)
     sa_ref[...] = jnp.concatenate([f2recv[m] for m in range(4, 8)], axis=0)
-    save_fa.start()
-    save_sa.start()
-    for m in range(8):
-        save_chunk(m).wait()
-    save_inc.wait()
-    save_aadj.wait()
 
     @pl.when(inner)
     def _():
@@ -709,24 +684,18 @@
     sent(e1recv.at[0:15], 13)
     sent(dwo_ref.at[0:896, :], 14)
 
-    save_fa.wait()
-    save_sa.wait()
-
 
 def hand_over(*refs):
-    into = [pltpu.make_async_copy(refs[i], refs[10 + i], refs[15].at[i]) for i in range(5)]
-    out = [pltpu.make_async_copy(refs[10 + i], refs[5 + i], refs[16].at[i]) for i in range(5)]
-    for copy in into:
+    copies = [pltpu.make_async_copy(refs[i], refs[5 + i], refs[10].at[i]) for i in range(5)]
+    for copy in copies:
         copy.start()
-    for i in range(5):
-        into[i].wait()
-        out[i].start()
-    for copy in out:
+    for copy in copies:
         copy.wait()
 
 
 def local(x, occ, w1, w2, wo, cot):
     hbm = pl.BlockSpec(memory_space=pl.ANY)
+    vmem = pl.BlockSpec(memory_space=pltpu.VMEM)
     dma = pltpu.SemaphoreType.DMA
     scratch = [
         pltpu.VMEM((NS, NQ, NCH), BF16),
@@ -735,11 +704,6 @@
         pltpu.VMEM((NP, NCH), BF16),
         pltpu.VMEM((1024, NZ), BF16),
         pltpu.VMEM((32, 64, NZ), BF16),
-        pltpu.VMEM((32, 64, NZ), BF16),
-        pltpu.VMEM((NS, NQ, NCH), BF16),
-        pltpu.VMEM((NP, NCH), F32),
-        pltpu.VMEM((NP, NCH), F32),
-        pltpu.VMEM((1024, NZ), F32),
         pltpu.VMEM((16, NS), BF16),
         pltpu.VMEM((4, 16, NS), BF16),
         pltpu.VMEM((8, 16, NS), BF16),
@@ -788,7 +752,7 @@
         pltpu.VMEM((128, NZ), F32),
         pltpu.VMEM((NQ, 128, NS), BF16),
         pltpu.VMEM((2, 1024, 128), F32),
-        dma((18,)),
+        dma((7,)),
         dma((15,)),
         dma((1,)),
         dma((1,)),
@@ -810,25 +774,24 @@
     inc, aadj, fa, sa, dwo = pl.pallas_call(
         kernel,
         out_shape=(
-            jax.ShapeDtypeStruct((32, 64, NZ), BF16),
-            jax.ShapeDtypeStruct((NS, NQ, NCH), BF16),
-            jax.ShapeDtypeStruct((NP, NCH), F32),
-            jax.ShapeDtypeStruct((NP, NCH), F32),
-            jax.ShapeDtypeStruct((1024, NZ), F32),
+            pltpu.VMEM((32, 64, NZ), BF16),
+            pltpu.VMEM((NS, NQ, NCH), BF16),
+            pltpu.VMEM((NP, NCH), F32),
+            pltpu.VMEM((NP, NCH), F32),
+            pltpu.VMEM((1024, NZ), F32),
         ),
         in_specs=[hbm] * 6,
-        out_specs=(hbm,) * 5,
+        out_specs=(vmem,) * 5,
         scratch_shapes=scratch,
         compiler_params=pltpu.CompilerParams(vmem_limit_bytes=60 * 1024 * 1024, has_side_effects=True, collective_id=0),
     )(x, occ.T, w1.T, w2.T, wo, cot)
-    outs = (inc, aadj, fa, sa, dwo)
+    outs = [pltpu.with_memory_space_constraint(o, pltpu.VMEM) for o in (inc, aadj, fa, sa, dwo)]
     inc, aadj, fa, sa, dwo = pl.pallas_call(
         hand_over,
         out_shape=tuple(jax.ShapeDtypeStruct(o.shape, o.dtype) for o in outs),
-        in_specs=[hbm] * 5,
+        in_specs=[vmem] * 5,
         out_specs=(hbm,) * 5,
-        scratch_shapes=[pltpu.VMEM(o.shape, o.dtype) for o in outs] + [dma((5,)), dma((5,))],
-        compiler_params=pltpu.CompilerParams(vmem_limit_bytes=60 * 1024 * 1024),
+        scratch_shapes=[dma((5,))],
     )(*outs)
     return inc, aadj, fa.T, sa.T, dwo
 

time: 61.7 us -> 59.9 us (0.971)
  Pallas kernels: 60.9 us -> 59.2 us
    pallas_call x1, Pallas kernels: 2.29 us -> 1.21 us  [local(): pl.pallas_call(hand_over, out_shape=tuple((jax.ShapeDtypeStruct(o.shape,...]
    pallas_call x1, Pallas kernels: 58.6 us -> 58 us  [local(): pl.pallas_call(kernel, out_shape=(pltpu.VMEM((32, 64, NZ), BF16), pltpu.V...]
where the time goes in v6:
time: 59.9 us; the launch traced here: 59.8 us
  Pallas kernels  59.2 us (99%)
  between operations  0.64 us (1%)
    pallas_call x1, Pallas kernels, local(): pl.pallas_call(kernel, out_shape=(pltpu.VMEM((32, 64, NZ), BF16), pltpu.V...  58 us
    pallas_call x1, Pallas kernels, local(): pl.pallas_call(hand_over, out_shape=tuple((jax.ShapeDtypeStruct(o.shape,...  1.21 us

profile of v6, /device:TPU:1, one launch (start us, length us, event | category | flops | bytes accessed | tf_op | source)
XLA Modules:
  0.0 59.8 jit_solution(1231127750305806520)
XLA Ops:
  0.6 58.0 %shard_map.101 = (bf16[32,64,128]{2,1,0:T(8,128)(2,1)S(1)}, bf16[128,8,256]{2,1,0:T(8,128)(2,1)S(1)}, f32[32,256]{1,0:T(8,128)S(1)}, f32[32,256]{1,0:T(8,128)S(1)}, f32[1024,128]{1,0:T(8,128)S(1)}) custom-call(bf16[128,8,256]{2,1,0:T(8,128)(2,1)} %x_hbm.1, s32[8,256]{1,0:T(8,128)} %bitcast.7, bf16[32,256]{1,0:T(8,128)(2,1)} %bitcast.5, ...), custom_call_target="tpu_custom_call" | custom-call | tf_op jit(solution)/shard_map/pallas_call | solution.py:774
  58.6 1.2 %shard_map.102 = (bf16[32,64,128]{2,1,0:T(8,128)(2,1)}, bf16[128,8,256]{2,1,0:T(8,128)(2,1)}, f32[32,256]{1,0:T(8,128)}, f32[32,256]{1,0:T(8,128)}, f32[1024,128]{1,0:T(8,128)}) custom-call(bf16[32,64,128]{2,1,0:T(8,128)(2,1)S(1)} %get-tuple-element.15.refs_0_, bf16[128,8,256]{2,1,0:T(8,128)(2,1)S(1)} %get-tuple-element.16.refs_1_, ...), custom_call_target="tpu_custom_call" | custom-call | tf_op jit(solution)/shard_map/pallas_call | solution.py:789

commit v7 on v6

--- a/solution.py
+++ b/solution.py
@@ -90,6 +90,7 @@
     e1recv,
     e2,
     e3,
+    e3out,
     gown,
     oscr,
     io_sem,
@@ -117,21 +118,22 @@
     me = r * 2 + q
     core, z = lax.rem(c, 2), c // 2
     sibling = (r, c + 1 - 2 * core, q)
-    holder = (
-        lax.rem(r // 4 + core, 2) * 4 + lax.rem(lax.rem(r, 4) + 2 - z + r // 2 + 4, 4),
-        r,
-        q,
-    )
-
-    def held(m):
-        dz = lax.rem(2 - lax.rem(m, 4) + lax.rem(c, 4) + 4, 4)
-        return lax.rem(c // 2 + dz, 4) * 2 + lax.rem(m // 4 + c // 4, 2)
-
-    def holder_row(m):
-        dz = lax.rem(m // 2 - c // 2 + 4, 4)
-        return lax.rem(c // 4 + lax.rem(m, 2), 2) * 4 + lax.rem(lax.rem(c, 4) + 2 - dz + 4, 4)
-
-    owner = (c, held(r), q)
+    def place(col, m, h):
+        dz = lax.rem(m // 2 - col // 2 + 4, 4)
+        down = lax.rem(m, 2) * (1 + 2 * (dz // 2))
+        return lax.rem(col // 4 + 2 * h + down, 4), lax.rem(lax.rem(col, 4) + 6 - dz, 4)
+
+    def held(y, x):
+        dz = lax.rem(6 - x + lax.rem(c, 4), 4)
+        down = lax.rem(y - c // 4 + 4, 4)
+        odd = lax.rem(down, 2)
+        return lax.rem(c // 2 + dz, 4) * 2 + odd, lax.rem(down // 2 + odd * (dz // 2), 2)
+
+    holder_y, holder_x = place(r, c, q)
+    holder_slot = (holder_y // 2, lax.rem(holder_y, 2) * 4 + holder_x)
+    holder = (holder_slot[1], r, holder_slot[0])
+    y0, x0 = q * 2 + r // 4, lax.rem(r, 4)
+    owner = (c, *held(y0, x0))
     other = (r, lax.rem(c + 1, 8), q)
 
     def plane(t):
@@ -193,7 +195,6 @@
     def _(t):
         pl.semaphore_signal(barrier, inc=1, device_id=line(t)[1], device_id_type=MESH)
 
-    y0, x0 = q * 2 + r // 4, lax.rem(r, 4)
     across = (r, lax.rem(z + 3 - 2 * lax.rem(z, 2), 4) * 2 + core, 1 - q)
 
     def at(y, x):
@@ -276,7 +277,7 @@
     def _():
         far(lsend, lrecv.at[lax.rem(c, 4), q], ss.at[2], rs_l.at[lax.rem(c, 4) // 2, q], across).start()
 
-    far(rsend, rrecv.at[q, holder[0]], ss.at[3], rs_r.at[0], holder).start()
+    far(rsend, rrecv.at[holder_slot[0], holder_slot[1]], ss.at[3], rs_r.at[0], holder).start()
 
     put(diagonal, msend, mcol.at[c], ss.at[1], rs_mc.at[0], mask_to(0))
 
@@ -337,9 +338,13 @@
 
     came = block(0, 0, 0, 256)
     arrived(came, rs_r.at[0])
+    upper, lower = block(0, 0, 0, 128), block(0, 0, 128, 256)
     for t in range(1, 4):
-        far(came, came, ss.at[3], rs_r.at[4 - t], along_x(t)).start()
-        far(came, came, ss.at[3], rs_r.at[7 - t], along_y(t)).start()
+        far(upper, upper, ss.at[3], rs_r.at[4 - t], along_x(t)).start()
+        far(lower, lower, ss.at[3], rs_r.at[7 - t], along_y(t)).start()
+    for t in range(1, 4):
+        far(upper, upper, ss.at[3], rs_r.at[7], along_y(t)).start()
+        far(lower, lower, ss.at[3], rs_r.at[7], along_x(t)).start()
 
     pl.loop(4, 8)(outer_adjoint)
 
@@ -373,31 +378,32 @@
         far(slot, slot, ss.at[2], rs_ls.at[0], sibling).start()
 
     for t in range(1, 4):
-        arrived(block(0, t, 0, 256), rs_r.at[t])
         half = block(0, t, 0, 128)
+        arrived(half, rs_r.at[t])
         for u in range(1, 4):
             far(half, half, ss.at[3], rs_r.at[7], along_y(u)).start()
-        arrived(block(t, 0, 0, 256), rs_r.at[3 + t])
         half = block(t, 0, 128, 256)
+        arrived(half, rs_r.at[3 + t])
         for u in range(1, 4):
             far(half, half, ss.at[3], rs_r.at[7], along_x(u)).start()
 
-    def put_right(dy, dx):
+    def put_right(dy, dx, pairs):
         y, x = lax.rem(y0 + dy, 4), lax.rem(x0 + dx, 4)
         h, m = y // 2, lax.rem(y, 2) * 4 + x
-        lanes = pl.ds(pl.multiple_of(h * NS, NS), NS)
-        first = held(m) * 16
-        for p in range(16):
+        col, seq = held(y, x)
+        lanes = pl.ds(pl.multiple_of(seq * NS, NS), NS)
+        first = col * 16
+        for p in pairs:
             at = pl.ds(pl.multiple_of(p * 128 + first, 16), 16)
             v = rrecv[h, m, p * 16 : (p + 1) * 16, :]
             w = v.astype(F32)
             rscr[0, at, lanes] = v
             rscr[1, at, lanes] = jnp.concatenate([w[8:], w[:8]], axis=0).astype(BF16)
 
-    put_right(0, 0)
+    put_right(0, 0, range(16))
     for t in range(1, 4):
-        put_right(0, t)
-        put_right(t, 0)
+        put_right(0, t, range(8))
+        put_right(t, 0, range(8, 16))
 
     arrived(lrecv.at[0:2], rs_ls.at[0])
     for h in range(2):
@@ -413,8 +419,8 @@
             for h in range(2):
                 gt = a[h * NS : (h + 1) * NS, u * 128 : (u + 1) * 128].T
                 for m in range(8):
-                    row = holder_row(m)
-                    grsend[h * 2 + row // 4, lax.rem(row, 4), at, :] = gt[m * 16 : (m + 1) * 16]
+                    y, x = place(c, m, h)
+                    grsend[y, x, at, :] = gt[m * 16 : (m + 1) * 16]
 
     for n in range(4):
         pl.loop(2 * n, 2 * n + 2)(right_part)
@@ -433,10 +439,12 @@
         s12[0, k * 128 : (k + 1) * 128, :] = in_turn(lo, hi)
         s12[1, k * 128 : (k + 1) * 128, :] = in_turn(hi, lo)
 
-    arrived(grsend.at[0:3, 0:3], rs_r.at[7])
+    arrived(grsend.at[0:3], rs_r.at[7])
     for t in range(1, 4):
+        put_right(0, t, range(8, 16))
+        put_right(t, 0, range(8))
         for u in range(1, 4):
-            put_right(t, u)
+            put_right(t, u, range(16))
 
     def outer_product(t):
         here = pl.ds(pl.multiple_of(t * 256, 256), 256)
@@ -526,7 +534,7 @@
             inc_ref[k] = jnp.concatenate([o[m * 16 : m * 16 + 8] for m in range(8)], axis=0).astype(BF16)
             inc_ref[k + 16] = jnp.concatenate([o[m * 16 + 8 : m * 16 + 16] for m in range(8)], axis=0).astype(BF16)
 
-    pl.loop(0, 4)(update)
+    pl.loop(0, 2)(update)
 
     for i in range(2):
         own = grb[i, y0] if i else grb[i, x0]
@@ -539,6 +547,8 @@
             grt[part * 64 : (part + 1) * 64, :] = total[half].astype(BF16)
     far(grt, grown, ss.at[7], rs_gt.at[0], owner).start()
 
+    pl.loop(2, 5)(update)
+
     arrived(dwrecv, rs_dw.at[0])
     total = dwrecv[0].astype(F32)
     for m in range(1, 8):
@@ -550,7 +560,7 @@
         m, dev = plane(t)
         far(e1.at[pl.ds(pl.multiple_of(m * 8, 8), 8), :], e1recv.at[t], ss.at[12], rs_e1.at[0], dev).start()
 
-    pl.loop(4, 8)(update)
+    pl.loop(5, 8)(update)
 
     arrived(glown, rs_go.at[0])
     arrived(grown, rs_gt.at[0])
@@ -623,12 +633,12 @@
         far(f1, f1recv.at[me], ss.at[10], rs_f1.at[0], (m // 2, c, lax.rem(m, 2))).start()
 
     arrived(e3, rs_e2.at[0])
-    chunk = dwo_ref.at[pl.ds(pl.multiple_of(c * 128, 128), 128), :]
-    dwo_ref[pl.ds(pl.multiple_of(c * 128, 128), 128), :] = e3[...]
-    far(e3, chunk, ss.at[14], rs_e3.at[0], sibling).start()
-
+    rows = pl.ds(pl.multiple_of(c * 128, 128), 128)
+    e3out[rows, :] = e3[...].astype(BF16)
+    chunk = e3out.at[rows, :]
+    far(chunk, chunk, ss.at[14], rs_e3.at[0], sibling).start()
     for t in range(1, 4):
-        far(e3, chunk, ss.at[14], rs_e3.at[4 - t], (r, lax.rem(z + t, 4) * 2 + core, q)).start()
+        far(chunk, chunk, ss.at[14], rs_e3.at[4 - t], along_z(t)).start()
 
     arrived(f1recv, rs_f1.at[0])
     total = f1recv[0]
@@ -643,11 +653,12 @@
 
     for t in range(1, 4):
         m = lax.rem(z + t, 4) * 2 + core
-        chunk = dwo_ref.at[pl.ds(pl.multiple_of(m * 128, 128), 128), :]
+        chunk = e3out.at[pl.ds(pl.multiple_of(m * 128, 128), 128), :]
         arrived(chunk, rs_e3.at[t])
         far(chunk, chunk, ss.at[14], rs_e3.at[0], sibling).start()
 
-    arrived(dwo_ref.at[0:512, :], rs_e3.at[0])
+    arrived(e3out.at[0:512, :], rs_e3.at[0])
+    dwo_ref[...] = e3out[...].astype(F32)
 
     arrived(f2recv, rs_f2.at[0])
     fa_ref[...] = jnp.concatenate([f2recv[m] for m in range(4)], axis=0)
@@ -682,7 +693,7 @@
     sent(f2recv.at[0:7], 11)
     sent(e1recv.at[0:15], 12)
     sent(e1recv.at[0:15], 13)
-    sent(dwo_ref.at[0:896, :], 14)
+    sent(e3out.at[0:896, :], 14)
 
 
 def hand_over(*refs):
@@ -750,6 +761,7 @@
         pltpu.VMEM((16, 8, NZ), F32),
         pltpu.VMEM((8, NZ), F32),
         pltpu.VMEM((128, NZ), F32),
+        pltpu.VMEM((1024, NZ), BF16),
         pltpu.VMEM((NQ, 128, NS), BF16),
         pltpu.VMEM((2, 1024, 128), F32),
         dma((7,)),

time: 59.9 us -> 57.7 us (0.963)
  Pallas kernels: 59.2 us -> 56.9 us
    pallas_call x1, Pallas kernels: 58 us -> 55.7 us  [local(): pl.pallas_call(kernel, out_shape=(pltpu.VMEM((32, 64, NZ), BF16), pltpu.V...]
where the time goes in v7:
time: 57.7 us; the launch traced here: 57.6 us
  Pallas kernels  56.9 us (99%)
  between operations  0.64 us (1%)
    pallas_call x1, Pallas kernels, local(): pl.pallas_call(kernel, out_shape=(pltpu.VMEM((32, 64, NZ), BF16), pltpu.V...  55.7 us
    pallas_call x1, Pallas kernels, local(): pl.pallas_call(hand_over, out_shape=tuple((jax.ShapeDtypeStruct(o.shape,...  1.21 us

profile of v7, /device:TPU:1, one launch (start us, length us, event | category | flops | bytes accessed | tf_op | source)
XLA Modules:
  0.0 57.6 jit_solution(4314027973182081097)
XLA Ops:
  0.6 55.7 %shard_map.101 = (bf16[32,64,128]{2,1,0:T(8,128)(2,1)S(1)}, bf16[128,8,256]{2,1,0:T(8,128)(2,1)S(1)}, f32[32,256]{1,0:T(8,128)S(1)}, f32[32,256]{1,0:T(8,128)S(1)}, f32[1024,128]{1,0:T(8,128)S(1)}) custom-call(bf16[128,8,256]{2,1,0:T(8,128)(2,1)} %x_hbm.1, s32[8,256]{1,0:T(8,128)} %bitcast.7, bf16[32,256]{1,0:T(8,128)(2,1)} %bitcast.5, ...), custom_call_target="tpu_custom_call" | custom-call | tf_op jit(solution)/shard_map/pallas_call | solution.py:786
  56.3 1.2 %shard_map.102 = (bf16[32,64,128]{2,1,0:T(8,128)(2,1)}, bf16[128,8,256]{2,1,0:T(8,128)(2,1)}, f32[32,256]{1,0:T(8,128)}, f32[32,256]{1,0:T(8,128)}, f32[1024,128]{1,0:T(8,128)}) custom-call(bf16[32,64,128]{2,1,0:T(8,128)(2,1)S(1)} %get-tuple-element.15.refs_0_, bf16[128,8,256]{2,1,0:T(8,128)(2,1)S(1)} %get-tuple-element.16.refs_1_, ...), custom_call_target="tpu_custom_call" | custom-call | tf_op jit(solution)/shard_map/pallas_call | solution.py:801

commit v8 on v7

--- a/solution.py
+++ b/solution.py
@@ -412,10 +412,9 @@
             lturn[h * NS : (h + 1) * NS, m * 256 : (m + 1) * 256] = lrecv[m, h].T
 
     def right_part(t):
-        here = pl.ds(pl.multiple_of(t * 256, 256), 256)
-        a = dot(lturn[...], d2[:, here], 1, 0).astype(BF16)
-        for u in range(2):
-            at = pl.ds(pl.multiple_of((t * 2 + u) * 16, 16), 16)
+        a = dot(lturn[...], d2[:, t * 512 : (t + 1) * 512], 1, 0).astype(BF16)
+        for u in range(4):
+            at = pl.ds((t * 4 + u) * 16, 16)
             for h in range(2):
                 gt = a[h * NS : (h + 1) * NS, u * 128 : (u + 1) * 128].T
                 for m in range(8):
@@ -423,7 +422,7 @@
                     grsend[y, x, at, :] = gt[m * 16 : (m + 1) * 16]
 
     for n in range(4):
-        pl.loop(2 * n, 2 * n + 2)(right_part)
+        right_part(n)
         rows = slice(n * 64, (n + 1) * 64)
         for t in range(1, 4):
             y, x = lax.rem(y0 + t, 4), lax.rem(x0 + t, 4)
@@ -447,22 +446,22 @@
             put_right(t, u, range(16))
 
     def outer_product(t):
-        here = pl.ds(pl.multiple_of(t * 256, 256), 256)
+        here = pl.ds(pl.multiple_of(t * 512, 512), 512)
         a = dot(lscr[:HALF], rscr[0, here, :], 1, 1)
         b = dot(lscr[HALF:], rscr[1, here, :], 1, 1)
-        for u in range(2):
+        for u in range(4):
             lanes = slice(u * 128, (u + 1) * 128)
-            even = pl.ds(pl.multiple_of((t * 2 + u) * NP, NP), NP)
-            odd = pl.ds(pl.multiple_of(HALF + (t * 2 + u) * NP, NP), NP)
+            even = pl.ds(pl.multiple_of((t * 4 + u) * NP, NP), NP)
+            odd = pl.ds(pl.multiple_of(HALF + (t * 4 + u) * NP, NP), NP)
             for k in range(16):
                 lo = a[k * NP : (k + 1) * NP, lanes]
                 hi = b[k * NP : (k + 1) * NP, lanes]
                 beo[even, k * 128 : (k + 1) * 128] = jnp.where(low, lo, hi).astype(BF16)
                 beo[odd, k * 128 : (k + 1) * 128] = jnp.where(low, hi, lo).astype(BF16)
 
-    pl.loop(0, 4)(outer_product)
-
-    pl.loop(4, 8)(outer_product)
+    pl.loop(0, 2)(outer_product)
+
+    pl.loop(2, 4)(outer_product)
 
     for h in range(2):
         part = dot(beo[h * HALF : (h + 1) * HALF], s12[h], 1, 0)

time: 57.7 us -> 57.4 us (level)
  no operation moved by 1% of the time
where the time goes in v8:
time: 57.4 us; the launch traced here: 57.2 us
  Pallas kernels  56.6 us (99%)
  between operations  0.64 us (1%)
    pallas_call x1, Pallas kernels, local(): pl.pallas_call(kernel, out_shape=(pltpu.VMEM((32, 64, NZ), BF16), pltpu.V...  55.4 us
    pallas_call x1, Pallas kernels, local(): pl.pallas_call(hand_over, out_shape=tuple((jax.ShapeDtypeStruct(o.shape,...  1.21 us

profile of v8, /device:TPU:1, one launch (start us, length us, event | category | flops | bytes accessed | tf_op | source)
XLA Modules:
  0.0 57.2 jit_solution(9922886798476808910)
XLA Ops:
  0.6 55.4 %shard_map.101 = (bf16[32,64,128]{2,1,0:T(8,128)(2,1)S(1)}, bf16[128,8,256]{2,1,0:T(8,128)(2,1)S(1)}, f32[32,256]{1,0:T(8,128)S(1)}, f32[32,256]{1,0:T(8,128)S(1)}, f32[1024,128]{1,0:T(8,128)S(1)}) custom-call(bf16[128,8,256]{2,1,0:T(8,128)(2,1)} %x_hbm.1, s32[8,256]{1,0:T(8,128)} %bitcast.7, bf16[32,256]{1,0:T(8,128)(2,1)} %bitcast.5, ...), custom_call_target="tpu_custom_call" | custom-call | tf_op jit(solution)/shard_map/pallas_call | solution.py:785
  56.0 1.2 %shard_map.102 = (bf16[32,64,128]{2,1,0:T(8,128)(2,1)}, bf16[128,8,256]{2,1,0:T(8,128)(2,1)}, f32[32,256]{1,0:T(8,128)}, f32[32,256]{1,0:T(8,128)}, f32[1024,128]{1,0:T(8,128)}) custom-call(bf16[32,64,128]{2,1,0:T(8,128)(2,1)S(1)} %get-tuple-element.15.refs_0_, bf16[128,8,256]{2,1,0:T(8,128)(2,1)S(1)} %get-tuple-element.16.refs_1_, ...), custom_call_target="tpu_custom_call" | custom-call | tf_op jit(solution)/shard_map/pallas_call | solution.py:800

commit v9 on v8

--- a/solution.py
+++ b/solution.py
@@ -114,7 +114,6 @@
 ):
     r, c, q = lax.axis_index("row"), lax.axis_index("col"), lax.axis_index("seq")
     inner = q == c // 4
-    diagonal = r == c
     me = r * 2 + q
     core, z = lax.rem(c, 2), c // 2
     sibling = (r, c + 1 - 2 * core, q)
@@ -176,17 +175,6 @@
 
     barrier = pltpu.get_barrier_semaphore()
 
-    def mask_to(t):
-        return (lax.rem(r + t, 8), r, q)
-
-    def mask_from(t):
-        return (c, lax.rem(c + t, 8), q)
-
-    @pl.loop(1, 8)
-    def _(t):
-        pl.semaphore_signal(barrier, inc=1, device_id=mask_to(t), device_id_type=MESH)
-        pl.semaphore_signal(barrier, inc=1, device_id=mask_from(t), device_id_type=MESH)
-
     @pl.loop(1, 16)
     def _(t):
         pl.semaphore_signal(barrier, inc=1, device_id=plane(t)[1], device_id_type=MESH)
@@ -221,11 +209,6 @@
 
     for dev in (holder, owner):
         pl.semaphore_signal(barrier, inc=1, device_id=dev, device_id_type=MESH)
-
-    @pl.when(jnp.logical_not(diagonal))
-    def _():
-        for dev in (mask_to(0), mask_from(0)):
-            pl.semaphore_signal(barrier, inc=1, device_id=dev, device_id_type=MESH)
 
     load_occ.wait()
     occ = occ_ref[...].astype(F32)
@@ -256,7 +239,7 @@
         tmp[pl.ds(k, NP, stride=NQ), :] = p[NP:]
     rsend[...] = tmp[...].astype(BF16)
 
-    pl.semaphore_wait(barrier, jnp.where(diagonal, 41, 43))
+    pl.semaphore_wait(barrier, 27)
 
     mine_of_line = lax.rem(jnp.where(inner, z, z + 3 - 2 * lax.rem(z, 2)), 2)
     seq_of_line = jnp.where(inner, q, 1 - q)
@@ -279,11 +262,9 @@
 
     far(rsend, rrecv.at[holder_slot[0], holder_slot[1]], ss.at[3], rs_r.at[0], holder).start()
 
-    put(diagonal, msend, mcol.at[c], ss.at[1], rs_mc.at[0], mask_to(0))
-
-    @pl.loop(1, 8)
-    def _(t):
-        far(msend, mcol.at[c], ss.at[1], rs_mc.at[0], mask_to(t)).start()
+    @pl.when(q == 0)
+    def _():
+        far(msend, mcol.at[c], ss.at[1], rs_mc.at[0], holder).start()
 
     @pl.when(inner)
     def _():
@@ -336,6 +317,17 @@
         arrived(given, given_mark)
         left_along()
 
+    mask_of, mask_seq = owner[1], owner[2]
+
+    @pl.when(mask_seq == 0)
+    def _():
+        came = mcol.at[mask_of]
+        arrived(came, rs_mc.at[0])
+
+        @pl.loop(1, 16)
+        def _(t):
+            far(came, came, ss.at[15], rs_mc.at[1], plane(t)[1]).start()
+
     came = block(0, 0, 0, 256)
     arrived(came, rs_r.at[0])
     upper, lower = block(0, 0, 0, 128), block(0, 0, 128, 256)
@@ -347,26 +339,6 @@
         far(lower, lower, ss.at[3], rs_r.at[7], along_x(t)).start()
 
     pl.loop(4, 8)(outer_adjoint)
-
-    arrived(mrow, rs_mr.at[0])
-    arrived(mcol, rs_mc.at[0])
-
-    count = jnp.zeros((64, 32), F32)
-    count_lanes = jnp.zeros((32, 128), F32)
-    for h in range(2):
-        rows = jnp.concatenate([mrow[m].astype(F32)[h * NQ : (h + 1) * NQ] for m in range(4)], axis=0).astype(BF16)
-        groups = [mcol[m].astype(F32)[h * NQ : (h + 1) * NQ] for m in range(8)]
-        cols = jnp.concatenate(groups, axis=0).astype(BF16)
-        twice = jnp.concatenate([g for g in groups for _ in range(2)], axis=0).astype(BF16)
-        count = count + dot(cols, rows, 1, 1)
-        count_lanes = count_lanes + dot(rows, twice, 1, 1)
-    over_lanes[...] = 1.0 / (count_lanes + 0.001)
-    inv[...] = jnp.where(low[:16], over_lanes[:16], over_lanes[16:])
-
-    @pl.loop(0, 32)
-    def _(i):
-        rows = pl.ds(pl.multiple_of(i * NP, NP), NP)
-        d2[rows, :] = (dpre[rows, :] * jnp.concatenate([over_lanes[pl.ds(i, 1), :]] * 16, axis=1)).astype(BF16)
 
     for t in range(1, 4):
         zt = lax.rem(z + t, 4)
@@ -404,6 +376,34 @@
     for t in range(1, 4):
         put_right(0, t, range(8))
         put_right(t, 0, range(8, 16))
+
+    arrived(mrow, rs_mr.at[0])
+
+    @pl.when(mask_seq == 0)
+    def _():
+        arrived(mcol.at[0:7], rs_mc.at[1])
+
+    @pl.when(mask_seq == 1)
+    def _():
+        arrived(mcol, rs_mc.at[1])
+
+
+    count = jnp.zeros((64, 32), F32)
+    count_lanes = jnp.zeros((32, 128), F32)
+    for h in range(2):
+        rows = jnp.concatenate([mrow[m].astype(F32)[h * NQ : (h + 1) * NQ] for m in range(4)], axis=0).astype(BF16)
+        groups = [mcol[m].astype(F32)[h * NQ : (h + 1) * NQ] for m in range(8)]
+        cols = jnp.concatenate(groups, axis=0).astype(BF16)
+        twice = jnp.concatenate([g for g in groups for _ in range(2)], axis=0).astype(BF16)
+        count = count + dot(cols, rows, 1, 1)
+        count_lanes = count_lanes + dot(rows, twice, 1, 1)
+    over_lanes[...] = 1.0 / (count_lanes + 0.001)
+    inv[...] = jnp.where(low[:16], over_lanes[:16], over_lanes[16:])
+
+    @pl.loop(0, 32)
+    def _(i):
+        rows = pl.ds(pl.multiple_of(i * NP, NP), NP)
+        d2[rows, :] = (dpre[rows, :] * jnp.concatenate([over_lanes[pl.ds(i, 1), :]] * 16, axis=1)).astype(BF16)
 
     arrived(lrecv.at[0:2], rs_ls.at[0])
     for h in range(2):
@@ -674,13 +674,13 @@
         sent(rrecv.at[0], 2)
         sent(rrecv.at[0], 4)
 
-    @pl.when(diagonal)
-    def _():
-        sent(mcol.at[0:7], 1)
-
-    @pl.when(jnp.logical_not(diagonal))
-    def _():
-        sent(mcol, 1)
+    @pl.when(q == 0)
+    def _():
+        sent(msend, 1)
+
+    @pl.when(mask_seq == 0)
+    def _():
+        sent(e1recv.at[0:15], 15)
 
     sent(rrecv, 3)
     sent(gra.at[0:3], 5)
@@ -764,9 +764,9 @@
         pltpu.VMEM((NQ, 128, NS), BF16),
         pltpu.VMEM((2, 1024, 128), F32),
         dma((7,)),
-        dma((15,)),
-        dma((1,)),
-        dma((1,)),
+        dma((16,)),
+        dma((1,)),
+        dma((2,)),
         dma((2, 2)),
         dma((1,)),
         dma((8,)),

time: 57.4 us -> 57.7 us (level)
  no operation moved by 1% of the time
where the time goes in v9:
time: 57.7 us; the launch traced here: 57.5 us
  Pallas kernels  56.9 us (99%)
  between operations  0.64 us (1%)
    pallas_call x1, Pallas kernels, local(): pl.pallas_call(kernel, out_shape=(pltpu.VMEM((32, 64, NZ), BF16), pltpu.V...  55.7 us
    pallas_call x1, Pallas kernels, local(): pl.pallas_call(hand_over, out_shape=tuple((jax.ShapeDtypeStruct(o.shape,...  1.21 us

profile of v9, /device:TPU:1, one launch (start us, length us, event | category | flops | bytes accessed | tf_op | source)
XLA Modules:
  0.0 57.5 jit_solution(6022129040940045990)
XLA Ops:
  0.6 55.7 %shard_map.101 = (bf16[32,64,128]{2,1,0:T(8,128)(2,1)S(1)}, bf16[128,8,256]{2,1,0:T(8,128)(2,1)S(1)}, f32[32,256]{1,0:T(8,128)S(1)}, f32[32,256]{1,0:T(8,128)S(1)}, f32[1024,128]{1,0:T(8,128)S(1)}) custom-call(bf16[128,8,256]{2,1,0:T(8,128)(2,1)} %x_hbm.1, s32[8,256]{1,0:T(8,128)} %bitcast.7, bf16[32,256]{1,0:T(8,128)(2,1)} %bitcast.5, ...), custom_call_target="tpu_custom_call" | custom-call | tf_op jit(solution)/shard_map/pallas_call | solution.py:785
  56.3 1.2 %shard_map.102 = (bf16[32,64,128]{2,1,0:T(8,128)(2,1)}, bf16[128,8,256]{2,1,0:T(8,128)(2,1)}, f32[32,256]{1,0:T(8,128)}, f32[32,256]{1,0:T(8,128)}, f32[1024,128]{1,0:T(8,128)}) custom-call(bf16[32,64,128]{2,1,0:T(8,128)(2,1)S(1)} %get-tuple-element.15.refs_0_, bf16[128,8,256]{2,1,0:T(8,128)(2,1)S(1)} %get-tuple-element.16.refs_1_, ...), custom_call_target="tpu_custom_call" | custom-call | tf_op jit(solution)/shard_map/pallas_call | solution.py:800
